TPU v7x, 32 devices: a whole 2x2x4 slice. The times are simulated.
32 devices in a mesh: rows: 16 (over z, y, core), ang: 2 (over x).
Axes of the slice: x: 2, y: 2, z: 4, core: 2. Of those that a mesh axis runs over, the one named last changes fastest.
Arguments:
- measured: bfloat16 [2, 2048, 2, 2048], P('ang', 'rows'), may hold values from -6 to 6
- slices: bfloat16 [2, 2048, 2, 2048], P(None, 'rows', None, 'ang'), may hold values from -5 to 5
- kernel_taps: bfloat16 [2, 65], replicated, may hold values from -1.25 to 1.25
- angle_freq: float32 [128, 2], replicated, may hold values from -40 to 40
- chosen: int32 [2], P('ang'), may hold values from 0 to 127
Outputs:
- grad_near: float32 [2048, 2, 2048], P('rows', None, 'ang')
- grad_far: float32 [2048, 2, 2048], P('rows', None, 'ang')
Inputs may be any that keep to these rules, and one draw needn't show every extreme that they name: `chosen`: indices into the angle table; an index may repeat.
All inputs are finite; a program needn't handle non-finite values.
Results may differ from a plain program's by a relative error of at most 0.014.
Values may be sent and summed in bfloat16 or wider, within the bound.
No kernel may reach another device: no remote copies, remote signals or barrier semaphores. Data moves between devices by JAX's collectives and lax.ppermute only.
A program may use at most 64 MiB of HBM per device.

v0:
```python
import math

import jax
import jax.numpy as jnp
from jax import lax
from jax.sharding import PartitionSpec as P


def with_halo(block, sides, width):
    for axis, dim in sides:
        count = lax.axis_size(axis)
        forward = [(i, i + 1) for i in range(count - 1)]
        backward = [(target, source) for source, target in forward]
        low = lax.ppermute(
            lax.slice_in_dim(block, block.shape[dim] - width, None, axis=dim), axis, forward
        )
        high = lax.ppermute(lax.slice_in_dim(block, 0, width, axis=dim), axis, backward)
        block = jnp.concatenate([low, block, high], axis=dim)
    return block


def toeplitz(row_taps, out_width):
    tap_count = row_taps.shape[0]
    window = out_width + tap_count - 1
    padded = jnp.concatenate([row_taps, jnp.zeros((out_width,), row_taps.dtype)])
    tiled = jnp.tile(padded, out_width)[: out_width * window]
    return tiled.reshape(out_width, window).T


def kernel_pair(kernel_taps, out_width):
    return jnp.concatenate(
        [toeplitz(kernel_taps[0], out_width), toeplitz(kernel_taps[1], out_width)], axis=1
    )


def adjoint_taps(kernel_taps):
    return jnp.stack([kernel_taps[0][::-1], -kernel_taps[1][::-1]])


def correlate_columns(field, kernel):
    window, doubled = kernel.shape
    tile_len = doubled // 2
    half_taps = (window - tile_len) // 2
    leading, comps, length = field.shape
    blocks = length // tile_len
    padded = jnp.pad(field, ((0, 0), (0, 0), (half_taps, tile_len - half_taps)))
    main_part = padded[:, :, :length].reshape(leading, comps, blocks, tile_len)
    tail_part = padded[:, :, tile_len : tile_len + length].reshape(
        leading, comps, blocks, tile_len
    )[..., : 2 * half_taps]
    windows = jnp.concatenate([main_part, tail_part], axis=3)
    product = jnp.einsum("rpnw,wk->rpnk", windows, kernel, preferred_element_type=jnp.float32)
    real_part = product[:, 0, :, :tile_len] - product[:, 1, :, tile_len:]
    imag_part = product[:, 0, :, tile_len:] + product[:, 1, :, :tile_len]
    return (
        jnp.stack([real_part, imag_part], axis=1)
        .reshape(leading, comps, length)
        .astype(jnp.bfloat16)
    )


def band_rows(padded, band):
    out_rows = band.shape[1] // 2
    product = jnp.einsum("jpc,jk->kpc", padded, band, preferred_element_type=jnp.float32)
    real_part = product[:out_rows, 0] - product[out_rows:, 1]
    imag_part = product[out_rows:, 0] + product[:out_rows, 1]
    return jnp.stack([real_part, imag_part], axis=1).astype(jnp.bfloat16)


def complex_times(left, right):
    left = left.astype(jnp.float32)
    right = right.astype(jnp.float32)
    real_part = left[:, 0] * right[:, 0] - left[:, 1] * right[:, 1]
    imag_part = left[:, 0] * right[:, 1] + left[:, 1] * right[:, 0]
    return jnp.stack([real_part, imag_part], axis=1)


def conjugate_times(left, right):
    left = left.astype(jnp.float32)
    right = right.astype(jnp.float32)
    real_part = left[:, 0] * right[:, 0] + left[:, 1] * right[:, 1]
    imag_part = left[:, 0] * right[:, 1] - left[:, 1] * right[:, 0]
    return jnp.stack([real_part, imag_part], axis=1)


def incident(freq, row_pos, col_pos, length):
    scale = 2.0 * math.pi / length
    phase = scale * (freq[0] * row_pos[:, None] + freq[1] * col_pos[None, :])
    return jnp.stack([jnp.cos(phase), jnp.sin(phase)], axis=1)


def local(measured, slices, kernel_taps, angle_freq, chosen):
    rows_dev = measured.shape[1]
    length = measured.shape[3]
    half_taps = (kernel_taps.shape[1] - 1) // 2
    backward_taps = adjoint_taps(kernel_taps)
    forward_kernel = kernel_pair(kernel_taps, 128)
    adjoint_kernel = kernel_pair(backward_taps, 128)
    forward_band = kernel_pair(kernel_taps, rows_dev)
    adjoint_band = kernel_pair(backward_taps, rows_dev)
    gathered = lax.all_gather(slices, "ang", axis=3, tiled=True)
    near_slab = gathered[0]
    far_slab = gathered[1]
    start = lax.axis_index("rows") * rows_dev
    row_pos = (start + jnp.arange(rows_dev, dtype=jnp.int32)).astype(jnp.float32)
    col_pos = jnp.arange(length).astype(jnp.float32)
    onehot = (chosen[:, None] == jnp.arange(angle_freq.shape[0], dtype=jnp.int32)[None, :]).astype(
        jnp.float32
    )
    freqs = jnp.dot(onehot, angle_freq, precision=lax.Precision.HIGHEST)

    def along_rows(field, band):
        padded = with_halo(field, (("rows", 0),), half_taps)
        result = band_rows(padded, band)
        return result

    member = 0
    entering = incident(freqs[member], row_pos, col_pos, length)
    entry0 = complex_times(near_slab, entering).astype(jnp.bfloat16)
    inner = along_rows(correlate_columns(entry0, forward_kernel), forward_band)
    entry1 = complex_times(far_slab, inner).astype(jnp.bfloat16)
    exit_field = along_rows(correlate_columns(entry1, forward_kernel), forward_band)
    residue = (exit_field.astype(jnp.float32) - measured[member].astype(jnp.float32)).astype(
        jnp.bfloat16
    )
    back_far = correlate_columns(along_rows(residue, adjoint_band), adjoint_kernel)
    grad_far = conjugate_times(inner, back_far)
    carried_list = [conjugate_times(far_slab, back_far).astype(jnp.bfloat16)]
    member = 0
    entering = incident(freqs[member], row_pos, col_pos, length)
    back_near = correlate_columns(along_rows(carried_list[member], adjoint_band), adjoint_kernel)
    grad_near = conjugate_times(entering, back_near)
    near_total, far_total = (
        lax.psum_scatter(
            grad_near.astype(jnp.bfloat16), "ang", scatter_dimension=2, tiled=True
        ).astype(jnp.float32),
        lax.psum_scatter(
            grad_far.astype(jnp.bfloat16), "ang", scatter_dimension=2, tiled=True
        ).astype(jnp.float32),
    )
    return (near_total, far_total)


def solution(mesh):
    return jax.shard_map(
        local,
        mesh=mesh,
        in_specs=(P("ang", "rows", None, None), P(None, "rows", None, "ang"), P(), P(), P("ang")),
        out_specs=(P("rows", None, "ang"), P("rows", None, "ang")),
        check_vma=False,
    )
```

profile of v0, /device:TPU:17, one launch (start us, length us, event | category | flops | bytes accessed | tf_op | source)
XLA Modules:
  0.0 195.4 jit_solution(627522954004043626)
XLA Ops:
  7.2 2.5 %copy.25 = bf16[2,128,2,1024]{3,1,2,0:T(8,128)(2,1)} copy(bf16[2,128,2,1024]{3,2,1,0:T(2,128)(2,1)} %param.6) | data formatting | bytes 2097152 | tf_op args[1]
  13.6 30.8 %all-gather.2.cloned.1.call-done = bf16[2,128,2,2048]{3,1,2,0:T(8,128)(2,1)} async-done(((bf16[2,128,2,1024]{3,1,2,0:T(8,128)(2,1)}), bf16[2,128,2,2048]{3,1,2,0:T(8,128)(2,1)}) %all-gather.2.cloned.1.call-update) | async-done | bytes 2097168 | tf_op jit(solution)/shard_map/all_gather | solution.py:101
  44.4 1.9 fusion.74
  46.3 4.3 %subtract_convert_fusion.4 = (bf16[128,1,2048]{2,0,1:T(8,128)(2,1)S(1)}, bf16[128,1,2048]{2,0,1:T(8,128)(2,1)S(1)}) fusion(f32[128,2,2048]{2,0,1:T(8,128)S(1)} %get-tuple-element.35, f32[2048]{0:T(1024)S(1)} %convert_multiply_fusion, f32[128]{0:T(128)S(1)} %convert_multiply_fusion.1), kind=kLoop, calls=%fused_computation.112 | loop fusion | flops 2621440 | bytes 3154432 | tf_op jit(solution)/shard_map/convert.35
  51.3 1.2 fusion.102
  52.5 2.3 %copy.29 = bf16[128,2,2048]{0,2,1:T(8,128)(2,1)} copy(bf16[128,2,2048]{2,0,1:T(8,128)(2,1)} %get-tuple-element.43) | data formatting | bytes 2097152 | tf_op jit(solution)/shard_map/slice | solution.py:48
  54.8 1.9 slice.332
  56.6 1.3 copy.28
  57.9 2.2 %fusion.2 = f32[128,2,16,256]{3,0,2,1:T(8,128)S(1)} fusion(bf16[128,2,16,64]{0,3,2,1:T(8,128)(2,1)} %slice.332, bf16[128,2,16,128]{0,3,2,1:T(8,128)(2,1)} %bitcast.86, bf16[192,128]{1,0:T(8,128)(2,1)S(1)} %bitcast.103, bf16[192,128]{1,0:T(8,128)(2,1)S(1)} %bitcast.99), kind=kOutput, calls=%fused_computation.5 | convolution fusion | flops 405995520 | bytes 5865472 | tf_op jit(solution)/shard_map/rpnw,wk->rpnk/dot_general | solution.py:52
  60.4 1.0 copy.30
  61.4 1.2 copy.32
  62.7 1.0 copy.31
  63.7 1.2 copy.33
  65.0 3.7 %collective-permute-start = (bf16[32,2,2048]{2,0,1:T(8,128)(2,1)S(1)}, bf16[32,2,2048]{2,0,1:T(8,128)(2,1)S(1)}, u32[]{:S(2)}, u32[]{:S(2)}) collective-permute-start(bf16[32,2,2048]{2,0,1:T(8,128)(2,1)S(1)} %get-tuple-element.50), channel_id=1, source_target_pairs={{0,2},{2,4},{4,6},{6,8},{8,10},{10,12},{12,14},{14,16},{16,18},{18... | collective-permute-start | bytes 786440 | tf_op jit(solution)/shard_map/ppermute | solution.py:14
  68.7 1.9 collective-permute-start.1
  70.6 1.4 collective-permute-done
  72.0 4.4 %collective-permute-done.1 = bf16[32,2,2048]{2,0,1:T(8,128)(2,1)S(1)} collective-permute-done((bf16[32,2,2048]{2,0,1:T(8,128)(2,1)S(1)}, bf16[32,2,2048]{2,0,1:T(8,128)(2,1)S(1)}, u32[]{:S(2)}, u32[]{:S(2)}) %collective-permute-start.1) | collective-permute-done | bytes 262176 | tf_op jit(solution)/shard_map/ppermute | solution.py:17
  76.4 0.7 fusion.6
  78.0 0.9 copy-done.2
  79.6 1.2 fusion.101
  80.9 2.3 %copy.54 = bf16[128,2,2048]{0,2,1:T(8,128)(2,1)} copy(bf16[128,2,2048]{2,0,1:T(8,128)(2,1)} %get-tuple-element.41) | data formatting | bytes 2097152 | tf_op jit(solution)/shard_map/reshape | solution.py:48
  83.1 1.9 slice.346
  85.0 1.3 copy.53
  86.3 2.2 %fusion.14 = f32[128,2,16,256]{3,0,2,1:T(8,128)S(1)} fusion(bf16[128,2,16,64]{0,3,2,1:T(8,128)(2,1)} %slice.346, bf16[128,2,16,128]{0,3,2,1:T(8,128)(2,1)} %bitcast.87, bf16[192,128]{1,0:T(8,128)(2,1)S(1)} %bitcast.105, bf16[192,128]{1,0:T(8,128)(2,1)S(1)} %bitcast.101), kind=kOutput, calls=%fused_computation.17 | convolution fusion | flops 405995520 | bytes 5865472 | tf_op jit(solution)/shard_map/rpnw,wk->rpnk/dot_general | solution.py:52
  88.8 1.0 copy.36
  89.8 1.2 copy.38
  91.0 1.0 copy.37
  92.1 1.2 copy.39
  93.4 1.9 collective-permute-start.2
  95.3 2.6 %collective-permute-start.3 = (bf16[32,2,2048]{2,0,1:T(8,128)(2,1)S(1)}, bf16[32,2,2048]{2,0,1:T(8,128)(2,1)S(1)}, u32[]{:S(2)}, u32[]{:S(2)}) collective-permute-start(bf16[32,2,2048]{2,0,1:T(8,128)(2,1)S(1)} %get-tuple-element.49), channel_id=1, source_target_pairs={{2,0},{4,2},{6,4},{8,6},{10,8},{12,10},{14,12},{16,14},{18,16},{20... | collective-permute-start | bytes 786440 | tf_op jit(solution)/shard_map/ppermute | solution.py:17
  98.6 5.3 %collective-permute-done.3 = bf16[32,2,2048]{2,0,1:T(8,128)(2,1)S(1)} collective-permute-done((bf16[32,2,2048]{2,0,1:T(8,128)(2,1)S(1)}, bf16[32,2,2048]{2,0,1:T(8,128)(2,1)S(1)}, u32[]{:S(2)}, u32[]{:S(2)}) %collective-permute-start.3) | collective-permute-done | bytes 262176 | tf_op jit(solution)/shard_map/ppermute | solution.py:17
  103.9 0.7 fusion.18
  104.9 0.9 copy-done.5
  106.4 0.8 fusion.103
  107.2 1.9 collective-permute-start.4
  109.2 2.4 %collective-permute-start.5 = (bf16[32,2,2048]{2,0,1:T(8,128)(2,1)}, bf16[32,2,2048]{2,0,1:T(8,128)(2,1)}, u32[]{:S(2)}, u32[]{:S(2)}) collective-permute-start(bf16[32,2,2048]{2,0,1:T(8,128)(2,1)} %get-tuple-element.47), channel_id=1, source_target_pairs={{2,0},{4,2},{6,4},{8,6},{10,8},{12,10},{14,12},{16,14},{18,16},{20... | collective-permute-start | bytes 786440 | tf_op jit(solution)/shard_map/ppermute | solution.py:17
  111.8 0.9 tile.19
  112.7 0.8 slice.322
  113.5 0.7 reshape.207
  114.3 0.9 copy.24
  115.9 1.8 tile.17
  117.7 0.8 slice.321
  119.2 0.9 copy.23
  120.2 1.7 fusion.26
  122.9 1.2 fusion.100
  124.1 2.3 %copy.56 = bf16[128,2,2048]{0,2,1:T(8,128)(2,1)} copy(bf16[128,2,2048]{2,0,1:T(8,128)(2,1)} %get-tuple-element.39) | data formatting | bytes 2097152 | tf_op jit(solution)/shard_map/reshape | solution.py:48
  126.4 1.9 slice.363
  128.3 1.3 copy.55
  129.6 2.2 %fusion.32 = f32[128,2,16,256]{3,0,2,1:T(8,128)S(1)} fusion(bf16[128,2,16,64]{0,3,2,1:T(8,128)(2,1)} %slice.363, bf16[128,2,16,128]{0,3,2,1:T(8,128)(2,1)} %bitcast.88, bf16[192,128]{1,0:T(8,128)(2,1)S(1)} %bitcast.108, bf16[192,128]{1,0:T(8,128)(2,1)S(1)} %bitcast.112), kind=kOutput, calls=%fused_computation.35 | convolution fusion | flops 405995520 | bytes 5865472 | tf_op jit(solution)/shard_map/rpnw,wk->rpnk/dot_general | solution.py:52
  132.3 1.4 copy-done.3
  133.8 0.8 add_convert_fusion
  134.6 3.9 %collective-permute-start.6 = (bf16[32,2,2048]{2,0,1:T(8,128)(2,1)S(1)}, bf16[32,2,2048]{2,0,1:T(8,128)(2,1)S(1)}, u32[]{:S(2)}, u32[]{:S(2)}) collective-permute-start(bf16[32,2,2048]{2,0,1:T(8,128)(2,1)S(1)} %get-tuple-element.44), channel_id=1, source_target_pairs={{0,2},{2,4},{4,6},{6,8},{8,10},{10,12},{12,14},{14,16},{16,18},{18... | collective-permute-start | bytes 786440 | tf_op jit(solution)/shard_map/ppermute | solution.py:14
  138.5 1.9 collective-permute-start.7
  140.4 1.1 pad_maximum_fusion.1
  141.8 5.5 %collective-permute-done.7 = bf16[32,2,2048]{2,0,1:T(8,128)(2,1)S(1)} collective-permute-done((bf16[32,2,2048]{2,0,1:T(8,128)(2,1)S(1)}, bf16[32,2,2048]{2,0,1:T(8,128)(2,1)S(1)}, u32[]{:S(2)}, u32[]{:S(2)}) %collective-permute-start.7) | collective-permute-done | bytes 262176 | tf_op jit(solution)/shard_map/ppermute | solution.py:17
  147.3 0.7 fusion.36
  150.0 0.8 slice.376
  151.8 0.8 fusion.44
  153.3 4.3 %add_convert_fusion.1 = (bf16[128,1,2048]{2,0,1:T(8,128)(2,1)S(1)}, bf16[128,1,2048]{2,0,1:T(8,128)(2,1)S(1)}) fusion(f32[128,2,2048]{2,0,1:T(8,128)S(1)} %maximum_convert_fusion.2, f32[2048]{0:T(1024)S(1)} %convert_multiply_fusion, f32[128]{0:T(128)S(1)} %convert_multiply_fusion.1), kind=kLoop, calls=%fused_computation.106 | loop fusion | flops 2621440 | bytes 3154432 | tf_op jit(solution)/shard_map/convert.5
  157.6 1.1 pad_maximum_fusion
  158.7 4.3 %reduce-scatter.5.cloned.1.call-done = bf16[128,2,1024]{2,0,1:T(8,128)(2,1)} async-done(((bf16[128,2,2048]{2,0,1:T(8,128)(2,1)}), bf16[128,2,1024]{2,0,1:T(8,128)(2,1)}) %reduce-scatter.5.cloned.1.call-update) | async-done | bytes 524304 | tf_op jit(solution)/shard_map/reduce_scatter | solution.py:137
  163.0 2.5 %copy.50 = f32[128,2,1024]{2,1,0:T(2,128)} copy(bf16[128,2,1024]{2,0,1:T(8,128)(2,1)} %reduce-scatter.5.cloned.1.call-done) | data formatting | bytes 1572864
  165.6 20.8 %reduce-scatter.3.cloned.1.call-done = bf16[128,2,1024]{2,0,1:T(8,128)(2,1)} async-done(((bf16[128,2,2048]{2,0,1:T(8,128)(2,1)}), bf16[128,2,1024]{2,0,1:T(8,128)(2,1)}) %reduce-scatter.3.cloned.1.call-update) | async-done | bytes 524304 | tf_op jit(solution)/shard_map/reduce_scatter | solution.py:134
  186.3 2.5 %copy.49 = f32[128,2,1024]{2,1,0:T(2,128)} copy(bf16[128,2,1024]{2,0,1:T(8,128)(2,1)} %reduce-scatter.3.cloned.1.call-done) | data formatting | bytes 1572864
  (72 shorter events, 14.7 us)
Async XLA Ops:
  7.2 4.4 %copy-start = (f32[128,2]{0,1:T(2,128)S(1)}, f32[128,2]{0,1:T(2,128)}, u32[]{:S(2)}) copy-start(f32[128,2]{0,1:T(2,128)} %param.8) | copy-start | bytes 3076
  7.2 3.3 %copy-start.6 = (bf16[2,65]{1,0:T(2,128)(2,1)S(1)}, bf16[2,65]{1,0:T(2,128)(2,1)}, u32[]{:S(2)}) copy-start(bf16[2,65]{1,0:T(2,128)(2,1)} %param.7) | copy-start | bytes 784
  7.2 37.2 %all-gather.2.cloned.1.call-start = ((), (), s32[]{:S(2)}) async-start(), calls=%async_computation.2 | async-start | bytes 3145728 | tf_op jit(solution)/shard_map/all_gather | solution.py:101
  9.7 153.3 %reduce-scatter.5.cloned.1.call-start = ((), (), s32[]{:S(2)}) async-start(), calls=%async_computation.4 | async-start | bytes 1572864 | tf_op jit(solution)/shard_map/reduce_scatter | solution.py:137
  65.0 7.0 %collective-permute-start = (bf16[32,2,2048]{2,0,1:T(8,128)(2,1)S(1)}, bf16[32,2,2048]{2,0,1:T(8,128)(2,1)S(1)}, u32[]{:S(2)}, u32[]{:S(2)}) collective-permute-start(bf16[32,2,2048]{2,0,1:T(8,128)(2,1)S(1)} %get-tuple-element.50), channel_id=1, source_target_pairs={{0,2},{2,4},{4,6},{6,8},{8,10},{10,12},{12,14},{14,16},{16,18},{18... | collective-permute-start | bytes 786440 | tf_op jit(solution)/shard_map/ppermute | solution.py:14
  68.7 7.7 %collective-permute-start.1 = (bf16[32,2,2048]{2,0,1:T(8,128)(2,1)S(1)}, bf16[32,2,2048]{2,0,1:T(8,128)(2,1)S(1)}, u32[]{:S(2)}, u32[]{:S(2)}) collective-permute-start(bf16[32,2,2048]{2,0,1:T(8,128)(2,1)S(1)} %get-tuple-element.51), channel_id=1, source_target_pairs={{2,0},{4,2},{6,4},{8,6},{10,8},{12,10},{14,12},{16,14},{18,16},{20... | collective-permute-start | bytes 786440 | tf_op jit(solution)/shard_map/ppermute | solution.py:17
  77.5 1.4 copy-start.2
  93.4 5.2 %collective-permute-start.2 = (bf16[32,2,2048]{2,0,1:T(8,128)(2,1)S(1)}, bf16[32,2,2048]{2,0,1:T(8,128)(2,1)S(1)}, u32[]{:S(2)}, u32[]{:S(2)}) collective-permute-start(bf16[32,2,2048]{2,0,1:T(8,128)(2,1)S(1)} %get-tuple-element.48), channel_id=1, source_target_pairs={{0,2},{2,4},{4,6},{6,8},{8,10},{10,12},{12,14},{14,16},{16,18},{18... | collective-permute-start | bytes 786440 | tf_op jit(solution)/shard_map/ppermute | solution.py:14
  95.3 8.6 %collective-permute-start.3 = (bf16[32,2,2048]{2,0,1:T(8,128)(2,1)S(1)}, bf16[32,2,2048]{2,0,1:T(8,128)(2,1)S(1)}, u32[]{:S(2)}, u32[]{:S(2)}) collective-permute-start(bf16[32,2,2048]{2,0,1:T(8,128)(2,1)S(1)} %get-tuple-element.49), channel_id=1, source_target_pairs={{2,0},{4,2},{6,4},{8,6},{10,8},{12,10},{14,12},{16,14},{18,16},{20... | collective-permute-start | bytes 786440 | tf_op jit(solution)/shard_map/ppermute | solution.py:17
  104.6 1.2 copy-start.5
  107.2 12.9 %collective-permute-start.4 = (bf16[32,2,2048]{2,0,1:T(8,128)(2,1)}, bf16[32,2,2048]{2,0,1:T(8,128)(2,1)S(1)}, u32[]{:S(2)}, u32[]{:S(2)}) collective-permute-start(bf16[32,2,2048]{2,0,1:T(8,128)(2,1)} %get-tuple-element.46), channel_id=1, source_target_pairs={{0,2},{2,4},{4,6},{6,8},{8,10},{10,12},{12,14},{14,16},{16,18},{18... | collective-permute-start | bytes 786440 | tf_op jit(solution)/shard_map/ppermute | solution.py:14
  109.2 11.0 %collective-permute-start.5 = (bf16[32,2,2048]{2,0,1:T(8,128)(2,1)}, bf16[32,2,2048]{2,0,1:T(8,128)(2,1)}, u32[]{:S(2)}, u32[]{:S(2)}) collective-permute-start(bf16[32,2,2048]{2,0,1:T(8,128)(2,1)} %get-tuple-element.47), channel_id=1, source_target_pairs={{2,0},{4,2},{6,4},{8,6},{10,8},{12,10},{14,12},{16,14},{18,16},{20... | collective-permute-start | bytes 786440 | tf_op jit(solution)/shard_map/ppermute | solution.py:17
  132.2 1.6 copy-start.3
  134.6 7.2 %collective-permute-start.6 = (bf16[32,2,2048]{2,0,1:T(8,128)(2,1)S(1)}, bf16[32,2,2048]{2,0,1:T(8,128)(2,1)S(1)}, u32[]{:S(2)}, u32[]{:S(2)}) collective-permute-start(bf16[32,2,2048]{2,0,1:T(8,128)(2,1)S(1)} %get-tuple-element.44), channel_id=1, source_target_pairs={{0,2},{2,4},{4,6},{6,8},{8,10},{10,12},{12,14},{14,16},{16,18},{18... | collective-permute-start | bytes 786440 | tf_op jit(solution)/shard_map/ppermute | solution.py:14
  138.5 8.8 %collective-permute-start.7 = (bf16[32,2,2048]{2,0,1:T(8,128)(2,1)S(1)}, bf16[32,2,2048]{2,0,1:T(8,128)(2,1)S(1)}, u32[]{:S(2)}, u32[]{:S(2)}) collective-permute-start(bf16[32,2,2048]{2,0,1:T(8,128)(2,1)S(1)} %get-tuple-element.45), channel_id=1, source_target_pairs={{2,0},{4,2},{6,4},{8,6},{10,8},{12,10},{14,12},{16,14},{18,16},{20... | collective-permute-start | bytes 786440 | tf_op jit(solution)/shard_map/ppermute | solution.py:17
  141.5 44.8 %reduce-scatter.3.cloned.1.call-start = ((), (), s32[]{:S(2)}) async-start(), calls=%async_computation.3 | async-start | bytes 1572864 | tf_op jit(solution)/shard_map/reduce_scatter | solution.py:134
  150.8 1.0 copy-start.4
  158.7 30.2 %copy-start.1 = (f32[128,2]{0,1:T(2,128)S(1)}, f32[128,2]{0,1:T(2,128)}, u32[]{:S(2)}) copy-start(f32[128,2]{0,1:T(2,128)} %param.8) | copy-start | bytes 3076
Sparse Core Ops, SparseCore 0:
  10.1 34.1 all-gather.1
  141.7 21.3 reduce-scatter.4
  165.9 20.3 reduce-scatter.2
where the time goes:
time: 198 us; the launch traced here: 195 us
  waiting for transfers between devices  73.2 us (37%)
  local copies, waits for them, and re-layouts  54.3 us (27%)
  other arithmetic  21.2 us (11%)
  starting transfers between devices  20.5 us (10%)
  between operations  14.9 us (8%)
  matrix products  11.3 us (6%)
    all_gather x1, waiting for transfers between devices, local(): gathered = lax.all_gather(slices, 'ang', axis=3, tiled=True)  30.8 us
    reduce_scatter x1, waiting for transfers between devices, local(): lax.psum_scatter(grad_near.astype(jnp.bfloat16), 'ang', scatter_dimension...  20.8 us
    ppermute x4, waiting for transfers between devices, with_halo(): lax.ppermute(lax.slice_in_dim(block, 0, width, axis=dim), axis, backward)  15.2 us
    another operation x10, other arithmetic  11.4 us
    ppermute x4, starting transfers between devices, with_halo(): lax.ppermute(lax.slice_in_dim(block, block.shape[dim] - width, None, axis...  11.4 us
    unnamed x17, local copies, waits for them, and re-layouts  11.3 us
    ppermute x4, starting transfers between devices, with_halo(): lax.ppermute(lax.slice_in_dim(block, 0, width, axis=dim), axis, backward)  8.84 us
    slice x5, local copies, waits for them, and re-layouts, correlate_columns(): padded[:, :, tile_len:tile_len + length]  8.71 us
  transfers between devices with their start and end apart: 11, of which 8 were waited for; matrix products, arithmetic and copies ran while one was open for 13% of the time, Pallas kernels for 0%

commit v1 on v0

--- a/solution.py
+++ b/solution.py
@@ -1,9 +1,412 @@
+import functools
 import math
 
 import jax
 import jax.numpy as jnp
 from jax import lax
+from jax.experimental import pallas as pl
+from jax.experimental.pallas import tpu as pltpu
 from jax.sharding import PartitionSpec as P
+
+LANES = 128
+BF16 = jnp.bfloat16
+F32 = jnp.float32
+
+
+def dot(left, right):
+    return jnp.dot(left, right, preferred_element_type=F32)
+
+
+def iota(shape, dim):
+    return lax.broadcasted_iota(jnp.int32, shape, dim)
+
+
+def lane_chunks(width, step=2 * LANES):
+    return [(at, min(step, width - at)) for at in range(0, width, step)]
+
+
+def edges_kernel(half, slices, angle_freq, chosen, outer, inner, across, corner):
+    rows, cols = slices.shape[1], slices.shape[3]
+    parity = lax.axis_index("rows") % 2
+    side = lax.axis_index("ang")
+    near_rows, far_rows = 2 * half, half
+    for out, late in ((outer, parity), (inner, 1 - parity)):
+        near = slices[0, pl.ds(late * (rows - near_rows), near_rows)]
+        far = slices[1, pl.ds(late * (rows - far_rows), far_rows)]
+        out[: 2 * near_rows] = near.reshape(2 * near_rows, cols)
+        out[2 * near_rows :] = far.reshape(2 * far_rows, cols)
+    corner[...] = jnp.where(side == 0, outer[:, cols - LANES :], outer[:, :LANES])
+    for slab in range(2):
+        left = slices[slab, :, :, :LANES].reshape(2 * rows, LANES)
+        right = slices[slab, :, :, cols - LANES :].reshape(2 * rows, LANES)
+        across[slab * 2 * rows : (slab + 1) * 2 * rows] = jnp.where(side == 0, right, left)
+    row = iota((16, LANES), 0)
+    block = jnp.zeros((16, LANES), F32)
+    for part in range(2):
+        rest = jnp.full((16, LANES), angle_freq[chosen[0], part], F32)
+        for piece in range(3):
+            rounded = rest.astype(BF16).astype(F32)
+            block = jnp.where(row == 3 * part + piece, rounded, block)
+            rest = rest - rounded
+    across[4 * rows :] = block.astype(BF16)
+
+
+def measured_kernel(measured, own, other):
+    rows, cols = measured.shape[1], measured.shape[3] // 2
+    side = lax.axis_index("ang")
+    first = measured[0, :, :, :cols].reshape(2 * rows, cols)
+    second = measured[0, :, :, cols:].reshape(2 * rows, cols)
+    before = measured[0, :, :, cols - LANES : cols].reshape(2 * rows, LANES)
+    after = measured[0, :, :, cols : cols + LANES].reshape(2 * rows, LANES)
+    own[:, :cols] = jnp.where(side == 0, first, second)
+    own[:, cols:] = jnp.where(side == 0, after, before)
+    other[:, :cols] = jnp.where(side == 0, second, first)
+    other[:, cols:] = jnp.where(side == 0, before, after)
+
+
+def skewed(base, count, stride):
+    width = base.shape[1]
+    return pltpu.roll(jnp.broadcast_to(base, (count, width)), 0, 1, stride=stride, stride_axis=0)
+
+
+def matrices_kernel(
+    rows, cols, length, taps, angle_freq, chosen, across,
+    row_near, row_fwd, row_adj, row_near_adj, col_taps, split_far, split_meas, waves,
+):
+    count = taps.shape[1]
+    half = (count - 1) // 2
+    wide = rows + 4 * half
+    mid = rows + 2 * half
+    side = lax.axis_index("ang")
+    table = jnp.concatenate(
+        [jnp.concatenate([taps[...], jnp.zeros((2, LANES - count), BF16)], axis=1),
+         jnp.zeros((14, LANES), BF16)], axis=0,
+    )
+
+    def spread(width, place):
+        tap = iota((LANES, width), 0)
+        lane = iota((LANES, width), 1)
+        hit = jnp.logical_and(lane == place(tap), tap < count)
+        return dot(table, jnp.where(hit, 1.0, 0.0).astype(BF16))
+
+    sent = across[4 * rows :].astype(F32)
+    freqs = []
+    for part in range(2):
+        own = jnp.full((1, 1), angle_freq[chosen[0], part], F32)
+        got = sent[3 * part : 3 * part + 1] + sent[3 * part + 1 : 3 * part + 2]
+        got = got + sent[3 * part + 2 : 3 * part + 3]
+        freqs.append((own, got[:, :1]))
+    scale = 2.0 * math.pi / length
+
+    lane = iota((1, cols + LANES), 1)
+    col = jnp.where(side == 0, lane, jnp.where(lane < cols, lane + cols, lane - LANES)).astype(F32)
+    for member in range(2):
+        phase = scale * (freqs[1][member] * col)
+        waves[2 * member : 2 * member + 1] = jnp.cos(phase)
+        waves[2 * member + 1 : 2 * member + 2] = jnp.sin(phase)
+
+    even = spread(2 * wide, lambda tap: 2 * tap)
+    odd = spread(2 * wide, lambda tap: 2 * tap + 1)
+    real = skewed(even[0:1] - odd[1:2], mid, 2)
+    imag = skewed(even[1:2] + odd[0:1], mid, 2)
+    start = lax.axis_index("rows") * rows - 2 * half
+    row = (start + iota((1, 2 * wide), 1) // 2).astype(F32)
+    for member in range(2):
+        phase = scale * (freqs[0][member] * row)
+        cos, sin = jnp.cos(phase), jnp.sin(phase)
+        full = jnp.concatenate([real * cos - imag * sin, imag * cos + real * sin], axis=0)
+        at = member * 2 * mid
+        row_near[at : at + 2 * mid] = full.astype(BF16)
+        row_near_adj[:, at : at + 2 * mid] = full.T.astype(BF16)
+
+    low = spread(2 * mid, lambda tap: tap)
+    high = spread(2 * mid, lambda tap: mid + tap)
+    full = jnp.concatenate(
+        [skewed(low[0:1] - high[1:2], rows, 1), skewed(low[1:2] + high[0:1], rows, 1)], axis=0
+    )
+    row_fwd[...] = full.astype(BF16)
+    row_adj[...] = full.T.astype(BF16)
+
+    window = 2 * LANES
+    source = iota((window, LANES), 0)
+    target = iota((window, LANES), 1)
+    same_side = (source < LANES) == (target < LANES - half)
+    left_only = source < window - half
+    right_only = source >= LANES - half
+    everything = source >= 0
+    at = 0
+    for adjoint in (False, True):
+        for offset, masks in ((0, (everything, same_side)), (2 * half, (everything, left_only, right_only))):
+            if adjoint:
+                base = spread(window, lambda tap: (window - offset - (count - 1) + tap) % window)
+            else:
+                base = spread(window, lambda tap: (window - offset - tap) % window)
+            re = skewed(base[0:1], window, 1)[:, :LANES]
+            im = skewed(base[1:2], window, 1)[:, :LANES]
+            im = -im if adjoint else im
+            for mask in masks:
+                mre = jnp.where(mask, re, 0.0).astype(BF16)
+                mim = jnp.where(mask, im, 0.0).astype(BF16)
+                col_taps[at, :window, :LANES] = mre
+                col_taps[at, :window, LANES:] = mim
+                col_taps[at, window:, :LANES] = -mim
+                col_taps[at, window:, LANES:] = mre
+                at += 1
+
+    for out in (split_far, split_meas):
+        size = out.shape[0]
+        to, frm = iota((size, size), 0), iota((size, size), 1)
+        out[...] = jnp.where(frm == 2 * (to % (size // 2)) + to // (size // 2), 1.0, 0.0).astype(BF16)
+
+
+def main_kernel(
+    half,
+    slices, outer, inner, across, corner, across_inner, meas_own, meas_other,
+    row_near, row_fwd, row_adj, row_near_adj, col_taps, split_far, split_meas, waves,
+    near_own, far_own, outer_sums, inner_sums,
+    near_slab, far_raw, far_slab, entry, field, after, carry, shifted, narrow, meas, into, far_sum,
+):
+    rows, cols = slices.shape[1], slices.shape[3]
+    tiles = cols // LANES + 1
+    width = tiles * LANES
+    wide, mid = rows + 4 * half, rows + 2 * half
+    parity = lax.axis_index("rows") % 2
+    side = lax.axis_index("ang")
+    chunks = lane_chunks(width)
+    cut = tiles - 1 - side
+    cut_next = lax.rem(cut + 1, tiles)
+
+    def tile(j):
+        return pl.ds(pl.multiple_of(j * LANES, LANES), LANES)
+
+    def pair(j):
+        return pl.ds(pl.multiple_of(j * LANES, LANES), 2 * LANES)
+
+    def ahead(j, base):
+        return base + jnp.where(j == cut, 1, 0)
+
+    def back(j, base):
+        return base + jnp.where(j == cut, 1, jnp.where(j == cut_next, 2, 0))
+
+    for slab, ref, margin in ((0, near_slab, 4 * half), (1, far_raw, 2 * half)):
+        ref[margin : margin + 2 * rows, :cols] = slices[slab].reshape(2 * rows, cols)
+        ref[margin : margin + 2 * rows, cols:width] = across[slab * 2 * rows : (slab + 1) * 2 * rows]
+        begin = 0 if slab == 0 else 4 * half
+        for late, body, tail in ((parity, outer, corner), (1 - parity, inner, None)):
+            at = pl.ds(pl.multiple_of(late * (2 * rows + margin), 16), margin)
+            ref[at, :cols] = body[begin : begin + margin]
+            if tail is not None:
+                ref[at, cols:width] = tail[begin : begin + margin]
+            else:
+                frm = slab * 2 * rows + (1 - late) * (2 * rows - margin)
+                ref[at, cols:width] = across_inner[pl.ds(pl.multiple_of(frm, 16), margin)]
+    far_raw[:, width:] = far_raw[:, :LANES]
+
+    def planar(j, carry_):
+        both = dot(split_far[...], far_raw[:, pair(j)])
+        far_slab[:, tile(j)] = both[:, half : half + LANES]
+        return carry_
+
+    lax.fori_loop(0, tiles, planar, 0)
+
+    for at, size in chunks:
+        result = dot(row_near[...], near_slab[:, at : at + size])
+        for member in range(2):
+            top = member * 2 * mid
+            re, im = result[top : top + mid], result[top + mid : top + 2 * mid]
+            vr = waves[2 * member : 2 * member + 1, at : at + size]
+            vi = waves[2 * member + 1 : 2 * member + 2, at : at + size]
+            entry[member, :mid, at : at + size] = (re * vr - im * vi).astype(BF16)
+            entry[member, mid:, at : at + size] = (re * vi + im * vr).astype(BF16)
+    for member in range(2):
+        entry[member, :, width:] = entry[member, :, :LANES]
+
+    def angle(member, measured):
+        def first(j, carry_):
+            x = jnp.concatenate([entry[member, :mid, pair(j)], entry[member, mid:, pair(j)]], axis=1)
+            y = dot(x, col_taps[ahead(j, 0)]).astype(BF16)
+            re, im = y[:, :LANES], y[:, LANES:]
+            field[:mid, tile(j)] = re
+            field[mid:, tile(j)] = im
+            re, im = re.astype(F32), im.astype(F32)
+            sr, si = far_slab[:mid, tile(j)], far_slab[mid:, tile(j)]
+            after[:mid, tile(j)] = (sr * re - si * im).astype(BF16)
+            after[mid:, tile(j)] = (sr * im + si * re).astype(BF16)
+            return carry_
+
+        lax.fori_loop(0, tiles, first, 0)
+        for at, size in chunks:
+            narrow[:, LANES + at : LANES + at + size] = dot(row_fwd[...], after[:, at : at + size]).astype(BF16)
+            meas[:, at : at + size] = dot(split_meas[...], measured[:, at : at + size])
+        narrow[:, :LANES] = narrow[:, width : width + LANES]
+
+        def second(j, carry_):
+            x = jnp.concatenate([narrow[:rows, pair(j)], narrow[rows:, pair(j)]], axis=1)
+            y = dot(x, col_taps[back(j, 2)]).astype(BF16).astype(F32)
+            shifted[:rows, tile(j)] = (y[:, :LANES] - meas[:rows, tile(j)]).astype(BF16)
+            shifted[rows:, tile(j)] = (y[:, LANES:] - meas[rows:, tile(j)]).astype(BF16)
+            return carry_
+
+        lax.fori_loop(0, tiles, second, 0)
+        shifted[:, width:] = shifted[:, :LANES]
+
+        def third(j, carry_):
+            x = jnp.concatenate([shifted[:rows, pair(j)], shifted[rows:, pair(j)]], axis=1)
+            y = dot(x, col_taps[ahead(j, 5)]).astype(BF16)
+            narrow[:rows, tile(j)] = y[:, :LANES]
+            narrow[rows:, tile(j)] = y[:, LANES:]
+            return carry_
+
+        lax.fori_loop(0, tiles, third, 0)
+        for at, size in chunks:
+            y = dot(row_adj[...], narrow[:, at : at + size])
+            br, bi = y[:mid], y[mid:]
+            ir, ii = field[:mid, at : at + size].astype(F32), field[mid:, at : at + size].astype(F32)
+            sr, si = far_slab[:mid, at : at + size], far_slab[mid:, at : at + size]
+            here = slice(LANES + at, LANES + at + size)
+            carry[:mid, here] = (sr * br + si * bi).astype(BF16)
+            carry[mid:, here] = (sr * bi - si * br).astype(BF16)
+            fr, fi = ir * br + ii * bi, ir * bi - ii * br
+            if member == 0:
+                far_sum[:mid, here] = fr
+                far_sum[mid:, here] = fi
+            else:
+                far_sum[:mid, here] += fr
+                far_sum[mid:, here] += fi
+        carry[:, :LANES] = carry[:, width : width + LANES]
+
+        def fourth(j, carry_):
+            x = jnp.concatenate([carry[:mid, pair(j)], carry[mid:, pair(j)]], axis=1)
+            y = dot(x, col_taps[back(j, 7)])
+            re, im = y[:, :LANES], y[:, LANES:]
+            vr = waves[2 * member : 2 * member + 1, tile(j)]
+            vi = waves[2 * member + 1 : 2 * member + 2, tile(j)]
+            top = member * 2 * mid
+            into[top : top + mid, tile(j)] = (re * vr + im * vi).astype(BF16)
+            into[top + mid : top + 2 * mid, tile(j)] = (im * vr - re * vi).astype(BF16)
+            return carry_
+
+        lax.fori_loop(0, tiles - 1, fourth, 0)
+
+    angle(0, meas_own)
+    angle(1, meas_other)
+
+    near_margin = 4 * half
+    for at, size in lane_chunks(cols):
+        here = slice(at, at + size)
+        y = dot(row_near_adj[...], into[:, here])
+        near_own[:, here] = y[near_margin : near_margin + 2 * rows]
+        low = y[:near_margin].astype(BF16)
+        high = y[near_margin + 2 * rows :].astype(BF16)
+        outer_sums[:near_margin, here] = jnp.where(parity == 0, low, high)
+        inner_sums[:near_margin, here] = jnp.where(parity == 0, high, low)
+    far_sum[:, :LANES] = far_sum[:, width : width + LANES]
+
+    def far_out(j, carry_):
+        y = far_sum[:, pair(j)][:, LANES - half : 2 * LANES - half]
+        for comp in range(2):
+            part = y[comp * mid : (comp + 1) * mid]
+            far_own[comp, :, tile(j)] = part[half : half + rows]
+            low, high = part[:half].astype(BF16), part[half + rows :].astype(BF16)
+            top = near_margin + comp * half
+            outer_sums[top : top + half, tile(j)] = jnp.where(parity == 0, low, high)
+            inner_sums[top : top + half, tile(j)] = jnp.where(parity == 0, high, low)
+        return carry_
+
+    lax.fori_loop(0, tiles - 1, far_out, 0)
+
+
+def finish_kernel(half, near_own, far_own, outer, inner, near, far, total):
+    rows, cols = near.shape[0], near.shape[2]
+    parity = lax.axis_index("rows") % 2
+    size = 4 * half
+    total[...] = near_own[...]
+    for late, got in ((parity, outer), (1 - parity, inner)):
+        at = pl.ds(pl.multiple_of(late * (2 * rows - size), 16), size)
+        total[at] += got[:size].astype(F32)
+    near[...] = total[...].reshape(rows, 2, cols)
+    for comp in range(2):
+        total[:rows] = far_own[comp]
+        for late, got in ((parity, outer), (1 - parity, inner)):
+            at = pl.ds(pl.multiple_of(late * (rows - half), 16), half)
+            total[at] += got[size + comp * half : size + (comp + 1) * half].astype(F32)
+        far[:, comp, :] = total[:rows]
+
+
+def call(kernel, outs, operands, scalars=(), scratch=(), cost=0):
+    specs = [
+        pl.BlockSpec(memory_space=pltpu.SMEM if i in scalars else pltpu.VMEM) for i in range(len(operands))
+    ]
+    return pl.pallas_call(
+        kernel,
+        out_shape=[jax.ShapeDtypeStruct(shape, dtype) for shape, dtype in outs],
+        in_specs=specs,
+        out_specs=[pl.BlockSpec(memory_space=pltpu.VMEM)] * len(outs),
+        scratch_shapes=[pltpu.VMEM(shape, dtype) for shape, dtype in scratch],
+        compiler_params=pltpu.CompilerParams(vmem_limit_bytes=40 * 2**20),
+        cost_estimate=pl.CostEstimate(flops=cost, bytes_accessed=0, transcendentals=0),
+    )(*operands)
+
+
+def columns_local(measured, slices, kernel_taps, angle_freq, chosen):
+    rows, cols = slices.shape[1], slices.shape[3]
+    length = measured.shape[3]
+    half = (kernel_taps.shape[1] - 1) // 2
+    wide, mid, width = rows + 4 * half, rows + 2 * half, cols + LANES
+    count = lax.axis_size("rows")
+    sides = lax.axis_size("ang")
+    outer_pairs = [(i, j) for i in range(count) if 0 <= (j := i - 1 + 2 * (i % 2)) < count]
+    inner_pairs = [(i, i + 1 - 2 * (i % 2)) for i in range(count)]
+    side_pairs = [(i, 1 - i) for i in range(sides)]
+    corner_pairs = [
+        (i * sides + s, j * sides + 1 - s) for i, j in outer_pairs for s in range(sides)
+    ]
+    edge = 6 * half
+    outer, inner, across, corner = call(
+        functools.partial(edges_kernel, half),
+        [((edge, cols), BF16), ((edge, cols), BF16), ((4 * rows + 16, LANES), BF16), ((edge, LANES), BF16)],
+        (slices, angle_freq, chosen), scalars=(1, 2),
+    )
+    outer_got = lax.ppermute(outer, "rows", outer_pairs)
+    across_got = lax.ppermute(across, "ang", side_pairs)
+    corner_got = lax.ppermute(corner, ("rows", "ang"), corner_pairs)
+    inner_got = lax.ppermute(inner, "rows", inner_pairs)
+    meas_own, meas_out = call(
+        measured_kernel, [((2 * rows, width), BF16)] * 2, (measured,),
+    )
+    meas_got = lax.ppermute(meas_out, "ang", side_pairs)
+    across_inner = lax.ppermute(across_got, "rows", inner_pairs)
+    mats = call(
+        functools.partial(matrices_kernel, rows, cols, length),
+        [
+            ((4 * mid, 2 * wide), BF16), ((2 * rows, 2 * mid), BF16), ((2 * mid, 2 * rows), BF16),
+            ((2 * wide, 4 * mid), BF16), ((10, 4 * LANES, 2 * LANES), BF16),
+            ((2 * mid, 2 * mid), BF16), ((2 * rows, 2 * rows), BF16), ((8, width), F32),
+        ],
+        (kernel_taps, angle_freq, chosen, across_got), scalars=(1, 2),
+    )
+    near_own, far_own, outer_sums, inner_sums = call(
+        functools.partial(main_kernel, half),
+        [((2 * rows, cols), F32), ((2, rows, cols), F32), ((edge, cols), BF16), ((edge, cols), BF16)],
+        (slices, outer_got, inner_got, across_got, corner_got, across_inner, meas_own, meas_got, *mats),
+        scratch=[
+            ((2 * wide, width), BF16), ((2 * mid, width + LANES), BF16), ((2 * mid, width), F32),
+            ((2, 2 * mid, width + LANES), BF16), ((2 * mid, width), BF16), ((2 * mid, width), BF16),
+            ((2 * mid, width + LANES), BF16), ((2 * rows, width + LANES), BF16),
+            ((2 * rows, width + LANES), BF16), ((2 * rows, width), F32), ((4 * mid, cols), BF16),
+            ((2 * mid, width + LANES), F32),
+        ],
+        cost=8 * 10**9,
+    )
+    outer_back = lax.ppermute(outer_sums, "rows", outer_pairs)
+    inner_back = lax.ppermute(inner_sums, "rows", inner_pairs)
+    near, far = call(
+        functools.partial(finish_kernel, half),
+        [((rows, 2, cols), F32)] * 2,
+        (near_own, far_own, outer_back, inner_back),
+        scratch=[((2 * rows, cols), F32)],
+    )
+    return near, far
 
 
 def with_halo(block, sides, width):
@@ -141,9 +544,24 @@
     return (near_total, far_total)
 
 
+def pick(measured, slices, kernel_taps, angle_freq, chosen):
+    rows, cols = slices.shape[1], slices.shape[3]
+    taps = kernel_taps.shape[1]
+    fits = (
+        lax.axis_size("ang") == 2
+        and lax.axis_size("rows") % 2 == 0
+        and 2 * (taps - 1) == LANES
+        and rows >= taps - 1
+        and rows % LANES == 0
+        and cols % (2 * LANES) == 0
+    )
+    run = columns_local if fits else local
+    return run(measured, slices, kernel_taps, angle_freq, chosen)
+
+
 def solution(mesh):
     return jax.shard_map(
-        local,
+        pick,
         mesh=mesh,
         in_specs=(P("ang", "rows", None, None), P(None, "rows", None, "ang"), P(), P(), P("ang")),
         out_specs=(P("rows", None, "ang"), P("rows", None, "ang")),

time: 198 us -> 69.7 us (0.35); the launches traced: 195 us -> 69.4 us
  waiting for transfers between devices: 73.2 us -> 16.7 us
  local copies, waits for them, and re-layouts: 54.3 us -> 5.1 us
  Pallas kernels: 0 us -> 31.5 us
  other arithmetic: 21.2 us -> 0 us
  between operations: 14.9 us -> 1.41 us
  matrix products: 11.3 us -> 0 us
  starting transfers between devices: 20.5 us -> 14.6 us
    pallas_call x0 -> x5, Pallas kernels: none -> 31.5 us  [call(): pl.pallas_call(kernel, out_shape=[jax.ShapeDtypeStruct(shape, dtype) for...]
    all_gather x1 -> x0, waiting for transfers between devices: 30.8 us -> none  [local(): gathered = lax.all_gather(slices, 'ang', axis=3, tiled=True)]
    reduce_scatter x2 -> x0, waiting for transfers between devices: 25.1 us -> none  [the longest x1 20.8 us: local(): lax.psum_scatter(grad_near.astype(jnp.bfloat16), 'ang', scatter_dimension...]
    slice x16 -> x0, local copies, waits for them, and re-layouts: 17.1 us -> none  [the longest x5 8.71 us: correlate_columns(): padded[:, :, tile_len:tile_len + length]]
    another operation x16 -> x0, other arithmetic: 16.4 us -> none
    another operation x19 -> x0, local copies, waits for them, and re-layouts: 13.5 us -> none  [the longest x7 5.39 us: correlate_columns(): jnp.stack([real_part, imag_part], axis=1).reshape(leading, comps, length)]
    reshape x14 -> x0, local copies, waits for them, and re-layouts: 12.2 us -> none  [the longest x3 5.18 us: correlate_columns(): padded[:, :, tile_len:tile_len + length]]
    dot_general x9 -> x0, matrix products: 11.3 us -> none  [the longest x4 7.27 us: correlate_columns(): jnp.einsum('rpnw,wk->rpnk', windows, kernel, preferred_element_type=jnp.f...]
  transfers between devices with their start and end apart: 11 -> 8, of which waited for: 8 -> 2; matrix products, arithmetic and copies ran while one was open for 13% -> 1% of each run, Pallas kernels for 0% -> 7%
where the time goes in v1:
time: 69.7 us; the launch traced here: 69.4 us
  Pallas kernels  31.5 us (45%)
  waiting for transfers between devices  16.7 us (24%)
  starting transfers between devices  14.6 us (21%)
  local copies, waits for them, and re-layouts  5.1 us (7%)
  between operations  1.41 us (2%)
    pallas_call x5, Pallas kernels, call(): pl.pallas_call(kernel, out_shape=[jax.ShapeDtypeStruct(shape, dtype) for...  31.5 us
    ppermute x1, waiting for transfers between devices, columns_local(): outer_back = lax.ppermute(outer_sums, 'rows', outer_pairs)  9.81 us
    ppermute x1, waiting for transfers between devices, columns_local(): across_got = lax.ppermute(across, 'ang', side_pairs)  6.87 us
    unnamed x9, local copies, waits for them, and re-layouts  5.1 us
    ppermute x1, starting transfers between devices, columns_local(): outer_got = lax.ppermute(outer, 'rows', outer_pairs)  3.99 us
    ppermute x1, starting transfers between devices, columns_local(): corner_got = lax.ppermute(corner, ('rows', 'ang'), corner_pairs)  3.95 us
    ppermute x1, starting transfers between devices, columns_local(): outer_back = lax.ppermute(outer_sums, 'rows', outer_pairs)  2.52 us
    ppermute x1, starting transfers between devices, columns_local(): across_inner = lax.ppermute(across_got, 'rows', inner_pairs)  1.55 us
  transfers between devices with their start and end apart: 8, of which 2 were waited for; matrix products, arithmetic and copies ran while one was open for 1% of the time, Pallas kernels for 7%

profile of v1, /device:TPU:17, one launch (start us, length us, event | category | flops | bytes accessed | tf_op | source)
XLA Modules:
  0.0 69.4 jit_solution(14107073405780853367)
XLA Ops:
  0.6 0.0 copy-start
  0.6 1.2 %copy-done = bf16[1,128,2,2048]{3,2,1,0:T(2,128)(2,1)S(1)} copy-done((bf16[1,128,2,2048]{3,2,1,0:T(2,128)(2,1)S(1)}, bf16[1,128,2,2048]{3,2,1,0:T(2,128)(2,1)}, u32[]{:S(2)}) %copy-start) | copy-done | bytes 1048600
  1.9 0.3 shard_map.69
  2.1 1.3 %collective-permute-start.5 = (bf16[256,1152]{1,0:T(8,128)(2,1)S(1)}, bf16[256,1152]{1,0:T(8,128)(2,1)S(1)}, u32[]{:S(2)}, u32[]{:S(2)}) collective-permute-start(bf16[256,1152]{1,0:T(8,128)(2,1)S(1)} %get-tuple-element.25), channel_id=1, source_target_pairs={{0,1},{1,0},{2,3},{3,2},{4,5},{5,4},{6,7},{7,6},{8,9},{9,8},{10,11... | collective-permute-start | bytes 1769480 | tf_op jit(solution)/shard_map/ppermute | solution.py:377
  4.1 0.8 %copy.7.angle_freq = f32[128,2]{1,0:T(8,128)S(1)} copy(f32[128,2]{0,1:T(2,128)} %param.8) | data formatting | bytes 2048 | tf_op args[3]
  4.8 0.0 copy-start.1
  4.9 1.2 %copy-done.1 = bf16[2,128,2,1024]{3,2,1,0:T(2,128)(2,1)S(1)} copy-done((bf16[2,128,2,1024]{3,2,1,0:T(2,128)(2,1)S(1)}, bf16[2,128,2,1024]{3,2,1,0:T(2,128)(2,1)}, u32[]{:S(2)}) %copy-start.1) | copy-done | bytes 1048600
  6.1 1.9 %shard_map.68 = (bf16[192,1024]{1,0:T(8,128)(2,1)S(1)}, bf16[192,1024]{1,0:T(8,128)(2,1)S(1)}, bf16[528,128]{1,0:T(8,128)(2,1)S(1)}, bf16[192,128]{1,0:T(8,128)(2,1)S(1)}) custom-call(bf16[2,128,2,1024]{3,2,1,0:T(2,128)(2,1)S(1)} %copy-done.1, f32[128,2]{1,0:T(8,128)S(1)} %copy.7.angle_freq, s32[1]{0:T(128)S(6)} %copy.9.chosen), custom_call_target="tpu_custom_call" | custom-call | tf_op jit(solution)/shard_map/pallas_call | solution.py:340
  8.0 4.0 %collective-permute-start = (bf16[192,1024]{1,0:T(8,128)(2,1)S(1)}, bf16[192,1024]{1,0:T(8,128)(2,1)S(1)}, u32[]{:S(2)}, u32[]{:S(2)}) collective-permute-start(bf16[192,1024]{1,0:T(8,128)(2,1)S(1)} %get-tuple-element.20), channel_id=1, source_target_pairs={{2,4},{4,2},{6,8},{8,6},{10,12},{12,10},{14,16},{16,14},{18,20},{2... | collective-permute-start | bytes 1179656 | tf_op jit(solution)/shard_map/ppermute | solution.py:370
  12.0 0.1 collective-permute-start.1
  12.1 0.3 collective-permute-start.2
  12.4 6.9 %collective-permute-done.2.across = bf16[528,128]{1,0:T(8,128)(2,1)S(1)} collective-permute-done((bf16[528,128]{1,0:T(8,128)(2,1)S(1)}, bf16[528,128]{1,0:T(8,128)(2,1)S(1)}, u32[]{:S(2)}, u32[]{:S(2)}) %collective-permute-start.2) | collective-permute-done | bytes 135200 | tf_op jit(solution)/shard_map/ppermute | solution.py:371
  19.3 1.5 %collective-permute-start.4 = (bf16[528,128]{1,0:T(8,128)(2,1)S(1)}, bf16[528,128]{1,0:T(8,128)(2,1)S(1)}, u32[]{:S(2)}, u32[]{:S(2)}) collective-permute-start(bf16[528,128]{1,0:T(8,128)(2,1)S(1)} %collective-permute-done.2.across), channel_id=1, source_target_pairs={{0,2},{2,0},{4,6},{6,4},{8,10},{10,8},{12,14},{14,12},{16,18},{18,... | collective-permute-start | bytes 405512 | tf_op jit(solution)/shard_map/ppermute | solution.py:378
  20.8 4.0 %collective-permute-start.3 = (bf16[192,128]{1,0:T(8,128)(2,1)S(1)}, bf16[192,128]{1,0:T(8,128)(2,1)S(1)}, u32[]{:S(2)}, u32[]{:S(2)}) collective-permute-start(bf16[192,128]{1,0:T(8,128)(2,1)S(1)} %get-tuple-element.23), channel_id=1, source_target_pairs={{2,5},{3,4},{4,3},{5,2},{6,9},{7,8},{8,7},{9,6},{10,13},{11,12},{1... | collective-permute-start | bytes 147464 | tf_op jit(solution)/shard_map/ppermute | solution.py:372
  24.8 0.0 copy-start.3
  24.8 0.6 copy-done.3
  25.5 3.2 %shard_map.70 = (bf16[768,512]{1,0:T(8,128)(2,1)S(1)}, bf16[256,384]{1,0:T(8,128)(2,1)S(1)}, bf16[384,256]{1,0:T(8,128)(2,1)S(1)}, bf16[512,768]{1,0:T(8,128)(2,...) custom-call(bf16[2,65]{1,0:T(2,128)(2,1)S(1)} %copy-done.3, ...), custom_call_target="tpu_custom_call" | custom-call | tf_op jit(solution)/shard_map/pallas_call | solution.py:340
  28.7 0.0 collective-permute-done.3.corner
  28.7 0.0 collective-permute-done.4.across_inner
  28.7 0.0 collective-permute-done.outer
  28.7 0.0 collective-permute-done.1.inner
  28.7 0.0 collective-permute-done.5.meas_other
  28.7 0.0 copy-start.2
  28.7 1.2 %copy-done.2 = bf16[2,128,2,1024]{3,2,1,0:T(2,128)(2,1)S(1)} copy-done((bf16[2,128,2,1024]{3,2,1,0:T(2,128)(2,1)S(1)}, bf16[2,128,2,1024]{3,2,1,0:T(2,128)(2,1)}, u32[]{:S(2)}) %copy-start.2) | copy-done | bytes 1048600
  29.9 24.4 %shard_map.71 = (f32[256,1024]{1,0:T(8,128)S(1)}, f32[2,128,1024]{2,1,0:T(8,128)S(1)}, bf16[192,1024]{1,0:T(8,128)(2,1)S(1)}, bf16[192,1024]{1,0:T(8,128)(2,1)S(1)}) custom-call(bf16[2,128,2,1024]{3,2,1,0:T(2,128)(2,1)S(1)} %copy-done.2, bf16[192,1024]{1,0:T(8,128)(2,1)S(1)} %collective-permute-done.outer, ...), custom_call_target="tpu_custom_call" | custom-call | flops 8000000000 | tf_op jit(solution)/shard_map/pallas_call | solution.py:340
  54.3 2.5 %collective-permute-start.6 = (bf16[192,1024]{1,0:T(8,128)(2,1)S(1)}, bf16[192,1024]{1,0:T(8,128)(2,1)S(1)}, u32[]{:S(2)}, u32[]{:S(2)}) collective-permute-start(bf16[192,1024]{1,0:T(8,128)(2,1)S(1)} %get-tuple-element.36), channel_id=1, source_target_pairs={{2,4},{4,2},{6,8},{8,6},{10,12},{12,10},{14,16},{16,14},{18,20},{2... | collective-permute-start | bytes 1179656 | tf_op jit(solution)/shard_map/ppermute | solution.py:401
  56.8 1.0 %collective-permute-start.7 = (bf16[192,1024]{1,0:T(8,128)(2,1)S(1)}, bf16[192,1024]{1,0:T(8,128)(2,1)S(1)}, u32[]{:S(2)}, u32[]{:S(2)}) collective-permute-start(bf16[192,1024]{1,0:T(8,128)(2,1)S(1)} %get-tuple-element.37), channel_id=1, source_target_pairs={{0,2},{2,0},{4,6},{6,4},{8,10},{10,8},{12,14},{14,12},{16,18},{18,... | collective-permute-start | bytes 1179656 | tf_op jit(solution)/shard_map/ppermute | solution.py:402
  57.8 9.8 %collective-permute-done.6.outer = bf16[192,1024]{1,0:T(8,128)(2,1)S(1)} collective-permute-done((bf16[192,1024]{1,0:T(8,128)(2,1)S(1)}, bf16[192,1024]{1,0:T(8,128)(2,1)S(1)}, u32[]{:S(2)}, u32[]{:S(2)}) %collective-permute-start.6) | collective-permute-done | bytes 393248 | tf_op jit(solution)/shard_map/ppermute | solution.py:401
  67.6 0.0 collective-permute-done.7.inner
  67.6 1.7 %shard_map.72 = (f32[128,2,1024]{2,1,0:T(2,128)}, f32[128,2,1024]{2,1,0:T(2,128)}) custom-call(f32[256,1024]{1,0:T(8,128)S(1)} %get-tuple-element.34.near_own, f32[2,128,1024]{2,1,0:T(8,128)S(1)} %get-tuple-element.35.far_own, bf16[192,1024]{1,0:T(8,128)(2,1)S(1)} %collective-permute-done.6.outer, bf16[192,1024]{1,0:T(8,128)(2,1)S(1)} %collective-permute-done.7.inner), custom_call_target="tpu_custom_call" | custom-call | tf_op jit(solution)/shard_map/pallas_call | solution.py:340
Async XLA Ops:
  0.6 1.2 %copy-start = (bf16[1,128,2,2048]{3,2,1,0:T(2,128)(2,1)S(1)}, bf16[1,128,2,2048]{3,2,1,0:T(2,128)(2,1)}, u32[]{:S(2)}) copy-start(bf16[1,128,2,2048]{3,2,1,0:T(2,128)(2,1)} %measured.1) | copy-start | bytes 3145732
  2.1 26.6 %collective-permute-start.5 = (bf16[256,1152]{1,0:T(8,128)(2,1)S(1)}, bf16[256,1152]{1,0:T(8,128)(2,1)S(1)}, u32[]{:S(2)}, u32[]{:S(2)}) collective-permute-start(bf16[256,1152]{1,0:T(8,128)(2,1)S(1)} %get-tuple-element.25), channel_id=1, source_target_pairs={{0,1},{1,0},{2,3},{3,2},{4,5},{5,4},{6,7},{7,6},{8,9},{9,8},{10,11... | collective-permute-start | bytes 1769480 | tf_op jit(solution)/shard_map/ppermute | solution.py:377
  4.8 1.2 %copy-start.1 = (bf16[2,128,2,1024]{3,2,1,0:T(2,128)(2,1)S(1)}, bf16[2,128,2,1024]{3,2,1,0:T(2,128)(2,1)}, u32[]{:S(2)}) copy-start(bf16[2,128,2,1024]{3,2,1,0:T(2,128)(2,1)} %slices.3) | copy-start | bytes 3145732
  8.0 20.6 %collective-permute-start = (bf16[192,1024]{1,0:T(8,128)(2,1)S(1)}, bf16[192,1024]{1,0:T(8,128)(2,1)S(1)}, u32[]{:S(2)}, u32[]{:S(2)}) collective-permute-start(bf16[192,1024]{1,0:T(8,128)(2,1)S(1)} %get-tuple-element.20), channel_id=1, source_target_pairs={{2,4},{4,2},{6,8},{8,6},{10,12},{12,10},{14,16},{16,14},{18,20},{2... | collective-permute-start | bytes 1179656 | tf_op jit(solution)/shard_map/ppermute | solution.py:370
  12.0 16.7 %collective-permute-start.1 = (bf16[192,1024]{1,0:T(8,128)(2,1)S(1)}, bf16[192,1024]{1,0:T(8,128)(2,1)S(1)}, u32[]{:S(2)}, u32[]{:S(2)}) collective-permute-start(bf16[192,1024]{1,0:T(8,128)(2,1)S(1)} %get-tuple-element.21), channel_id=1, source_target_pairs={{0,2},{2,0},{4,6},{6,4},{8,10},{10,8},{12,14},{14,12},{16,18},{18,... | collective-permute-start | bytes 1179656 | tf_op jit(solution)/shard_map/ppermute | solution.py:373
  12.1 7.2 %collective-permute-start.2 = (bf16[528,128]{1,0:T(8,128)(2,1)S(1)}, bf16[528,128]{1,0:T(8,128)(2,1)S(1)}, u32[]{:S(2)}, u32[]{:S(2)}) collective-permute-start(bf16[528,128]{1,0:T(8,128)(2,1)S(1)} %get-tuple-element.22), channel_id=1, source_target_pairs={{0,1},{1,0},{2,3},{3,2},{4,5},{5,4},{6,7},{7,6},{8,9},{9,8},{10,11... | collective-permute-start | bytes 405512 | tf_op jit(solution)/shard_map/ppermute | solution.py:371
  19.3 9.4 %collective-permute-start.4 = (bf16[528,128]{1,0:T(8,128)(2,1)S(1)}, bf16[528,128]{1,0:T(8,128)(2,1)S(1)}, u32[]{:S(2)}, u32[]{:S(2)}) collective-permute-start(bf16[528,128]{1,0:T(8,128)(2,1)S(1)} %collective-permute-done.2.across), channel_id=1, source_target_pairs={{0,2},{2,0},{4,6},{6,4},{8,10},{10,8},{12,14},{14,12},{16,18},{18,... | collective-permute-start | bytes 405512 | tf_op jit(solution)/shard_map/ppermute | solution.py:378
  20.8 7.8 %collective-permute-start.3 = (bf16[192,128]{1,0:T(8,128)(2,1)S(1)}, bf16[192,128]{1,0:T(8,128)(2,1)S(1)}, u32[]{:S(2)}, u32[]{:S(2)}) collective-permute-start(bf16[192,128]{1,0:T(8,128)(2,1)S(1)} %get-tuple-element.23), channel_id=1, source_target_pairs={{2,5},{3,4},{4,3},{5,2},{6,9},{7,8},{8,7},{9,6},{10,13},{11,12},{1... | collective-permute-start | bytes 147464 | tf_op jit(solution)/shard_map/ppermute | solution.py:372
  24.8 0.7 copy-start.3
  28.7 1.2 %copy-start.2 = (bf16[2,128,2,1024]{3,2,1,0:T(2,128)(2,1)S(1)}, bf16[2,128,2,1024]{3,2,1,0:T(2,128)(2,1)}, u32[]{:S(2)}) copy-start(bf16[2,128,2,1024]{3,2,1,0:T(2,128)(2,1)} %slices.3) | copy-start | bytes 3145732
  54.3 13.3 %collective-permute-start.6 = (bf16[192,1024]{1,0:T(8,128)(2,1)S(1)}, bf16[192,1024]{1,0:T(8,128)(2,1)S(1)}, u32[]{:S(2)}, u32[]{:S(2)}) collective-permute-start(bf16[192,1024]{1,0:T(8,128)(2,1)S(1)} %get-tuple-element.36), channel_id=1, source_target_pairs={{2,4},{4,2},{6,8},{8,6},{10,12},{12,10},{14,16},{16,14},{18,20},{2... | collective-permute-start | bytes 1179656 | tf_op jit(solution)/shard_map/ppermute | solution.py:401
  56.8 10.8 %collective-permute-start.7 = (bf16[192,1024]{1,0:T(8,128)(2,1)S(1)}, bf16[192,1024]{1,0:T(8,128)(2,1)S(1)}, u32[]{:S(2)}, u32[]{:S(2)}) collective-permute-start(bf16[192,1024]{1,0:T(8,128)(2,1)S(1)} %get-tuple-element.37), channel_id=1, source_target_pairs={{0,2},{2,0},{4,6},{6,4},{8,10},{10,8},{12,14},{14,12},{16,18},{18,... | collective-permute-start | bytes 1179656 | tf_op jit(solution)/shard_map/ppermute | solution.py:402

commit v2 on v1

--- a/solution.py
+++ b/solution.py
@@ -10,6 +10,7 @@
 
 LANES = 128
 BF16 = jnp.bfloat16
+OWN_FLOPS = 4 * 10**9
 F32 = jnp.float32
 
 
@@ -25,25 +26,45 @@
     return [(at, min(step, width - at)) for at in range(0, width, step)]
 
 
-def edges_kernel(half, slices, angle_freq, chosen, outer, inner, across, corner):
+def outer_kernel(half, slices, outer, sems):
+    rows = slices.shape[1]
+    parity = lax.axis_index("rows") % 2
+    copies = []
+    for slab, at, size in ((0, 0, 2 * half), (1, 2 * half, half)):
+        first = pl.ds(parity * (rows - size), size)
+        copies.append(pltpu.make_async_copy(slices.at[slab, first], outer.at[pl.ds(at, size)], sems.at[slab]))
+    for copy in copies:
+        copy.start()
+    for copy in copies:
+        copy.wait()
+
+
+def strip_kernel(half, across, strip):
+    rows = (across.shape[0] - 16) // 4
+    parity = lax.axis_index("rows") % 2
+    begin = 0
+    for slab, size in ((0, 4 * half), (1, 2 * half)):
+        frm = slab * 2 * rows + parity * (2 * rows - size)
+        strip[begin : begin + size] = across[pl.ds(pl.multiple_of(frm, 16), size)]
+        begin += size
+
+
+def edges_kernel(half, slices, angle_freq, chosen, sent, inner, across):
     rows, cols = slices.shape[1], slices.shape[3]
     parity = lax.axis_index("rows") % 2
     side = lax.axis_index("ang")
-    near_rows, far_rows = 2 * half, half
-    for out, late in ((outer, parity), (inner, 1 - parity)):
-        near = slices[0, pl.ds(late * (rows - near_rows), near_rows)]
-        far = slices[1, pl.ds(late * (rows - far_rows), far_rows)]
-        out[: 2 * near_rows] = near.reshape(2 * near_rows, cols)
-        out[2 * near_rows :] = far.reshape(2 * far_rows, cols)
-    corner[...] = jnp.where(side == 0, outer[:, cols - LANES :], outer[:, :LANES])
+    near = slices[0, pl.ds((1 - parity) * (rows - 2 * half), 2 * half)]
+    far = slices[1, pl.ds((1 - parity) * (rows - half), half)]
+    inner[: 4 * half] = near.reshape(4 * half, cols)
+    inner[4 * half :] = far.reshape(2 * half, cols)
     for slab in range(2):
         left = slices[slab, :, :, :LANES].reshape(2 * rows, LANES)
         right = slices[slab, :, :, cols - LANES :].reshape(2 * rows, LANES)
         across[slab * 2 * rows : (slab + 1) * 2 * rows] = jnp.where(side == 0, right, left)
     row = iota((16, LANES), 0)
     block = jnp.zeros((16, LANES), F32)
-    for part in range(2):
-        rest = jnp.full((16, LANES), angle_freq[chosen[0], part], F32)
+    for part, freq in enumerate(frequencies(angle_freq, chosen)):
+        rest = jnp.broadcast_to(freq, (16, LANES))
         for piece in range(3):
             rounded = rest.astype(BF16).astype(F32)
             block = jnp.where(row == 3 * part + piece, rounded, block)
@@ -51,7 +72,13 @@
     across[4 * rows :] = block.astype(BF16)
 
 
-def measured_kernel(measured, own, other):
+def frequencies(angle_freq, chosen):
+    entry = jnp.where(iota(angle_freq.shape, 1) == chosen[0], angle_freq[...], 0.0)
+    pair = jnp.sum(entry, axis=1, keepdims=True)
+    return pair[0:1], pair[1:2]
+
+
+def measured_kernel(measured, inner, own, other):
     rows, cols = measured.shape[1], measured.shape[3] // 2
     side = lax.axis_index("ang")
     first = measured[0, :, :, :cols].reshape(2 * rows, cols)
@@ -91,8 +118,7 @@
 
     sent = across[4 * rows :].astype(F32)
     freqs = []
-    for part in range(2):
-        own = jnp.full((1, 1), angle_freq[chosen[0], part], F32)
+    for part, own in enumerate(frequencies(angle_freq, chosen)):
         got = sent[3 * part : 3 * part + 1] + sent[3 * part + 1 : 3 * part + 2]
         got = got + sent[3 * part + 2 : 3 * part + 3]
         freqs.append((own, got[:, :1]))
@@ -159,192 +185,251 @@
         out[...] = jnp.where(frm == 2 * (to % (size // 2)) + to // (size // 2), 1.0, 0.0).astype(BF16)
 
 
-def main_kernel(
+class Tiles:
+    def __init__(self, cols):
+        self.count = cols // LANES + 1
+        self.width = self.count * LANES
+        self.cut = self.count - 1 - lax.axis_index("ang")
+        self.after = lax.rem(self.cut + 1, self.count)
+
+    def ahead(self, j, base):
+        return base + jnp.where(j == self.cut, 1, 0) if j >= self.count - 2 else base
+
+    def back(self, j, base):
+        if 0 < j < self.count - 2:
+            return base
+        return base + jnp.where(j == self.cut, 1, jnp.where(j == self.after, 2, 0))
+
+
+def tile(j):
+    return slice(j * LANES, (j + 1) * LANES)
+
+
+def pair(j):
+    return slice(j * LANES, (j + 2) * LANES)
+
+
+def both_parts(ref, j):
+    size = ref.shape[0] // 2
+    return jnp.concatenate([ref[:size, pair(j)], ref[size:, pair(j)]], axis=1)
+
+
+def forward_angle(tiles, entry, far_slab, row_fwd, col_taps, field, after, narrow, leaving):
+    mid = field.shape[0] // 2
+    rows = leaving.shape[0] // 2
+    for j in range(tiles.count):
+        y = dot(both_parts(entry, j), col_taps[tiles.ahead(j, 0)]).astype(BF16)
+        re, im = y[:, :LANES], y[:, LANES:]
+        field[:mid, tile(j)] = re
+        field[mid:, tile(j)] = im
+        re, im = re.astype(F32), im.astype(F32)
+        sr, si = far_slab[:mid, tile(j)], far_slab[mid:, tile(j)]
+        after[:mid, tile(j)] = (sr * re - si * im).astype(BF16)
+        after[mid:, tile(j)] = (sr * im + si * re).astype(BF16)
+    for at, size in lane_chunks(tiles.width):
+        narrow[:, LANES + at : LANES + at + size] = dot(row_fwd[...], after[:, at : at + size]).astype(BF16)
+    narrow[:, :LANES] = narrow[:, tiles.width :]
+    for j in range(tiles.count):
+        y = dot(both_parts(narrow, j), col_taps[tiles.back(j, 2)]).astype(BF16)
+        leaving[:rows, tile(j)] = y[:, :LANES]
+        leaving[rows:, tile(j)] = y[:, LANES:]
+
+
+def backward_angle(
+    tiles, member, leaving, measured, field, far_slab, split_meas, row_adj, col_taps, waves, residue, narrow, carry,
+    far_sum, into,
+):
+    mid = field.shape[0] // 2
+    rows = leaving.shape[0] // 2
+    for at, size in lane_chunks(tiles.width):
+        here = slice(at, at + size)
+        meas = dot(split_meas[...], measured[:, here])
+        residue[:, here] = (leaving[:, here].astype(F32) - meas).astype(BF16)
+    residue[:, tiles.width :] = residue[:, :LANES]
+    for j in range(tiles.count):
+        y = dot(both_parts(residue, j), col_taps[tiles.ahead(j, 5)]).astype(BF16)
+        narrow[:rows, tile(j)] = y[:, :LANES]
+        narrow[rows:, tile(j)] = y[:, LANES:]
+    for at, size in lane_chunks(tiles.width):
+        y = dot(row_adj[...], narrow[:, at : at + size])
+        br, bi = y[:mid], y[mid:]
+        ir, ii = field[:mid, at : at + size].astype(F32), field[mid:, at : at + size].astype(F32)
+        sr, si = far_slab[:mid, at : at + size], far_slab[mid:, at : at + size]
+        here = slice(LANES + at, LANES + at + size)
+        carry[:mid, here] = (sr * br + si * bi).astype(BF16)
+        carry[mid:, here] = (sr * bi - si * br).astype(BF16)
+        far_sum(at, here, ir * br + ii * bi, ir * bi - ii * br)
+    carry[:, :LANES] = carry[:, tiles.width :]
+    for j in range(tiles.count - 1):
+        y = dot(both_parts(carry, j), col_taps[tiles.back(j, 7)])
+        re, im = y[:, :LANES], y[:, LANES:]
+        vr, vi = waves[2 * member : 2 * member + 1, tile(j)], waves[2 * member + 1 : 2 * member + 2, tile(j)]
+        into[:mid, tile(j)] = (re * vr + im * vi).astype(BF16)
+        into[mid:, tile(j)] = (im * vr - re * vi).astype(BF16)
+
+
+def own_kernel(
     half,
-    slices, outer, inner, across, corner, across_inner, meas_own, meas_other,
-    row_near, row_fwd, row_adj, row_near_adj, col_taps, split_far, split_meas, waves,
-    near_own, far_own, outer_sums, inner_sums,
-    near_slab, far_raw, far_slab, entry, field, after, carry, shifted, narrow, meas, into, far_sum,
+    slices, outer, inner, across, corner, across_inner, meas_own,
+    row_near, row_fwd, row_adj, col_taps, split_far, split_meas, waves,
+    far_slab, field_other, leaving_other, far_sum, into_own,
+    near_slab, far_raw, entry, field, after, narrow, leaving, residue, carry,
 ):
     rows, cols = slices.shape[1], slices.shape[3]
-    tiles = cols // LANES + 1
-    width = tiles * LANES
-    wide, mid = rows + 4 * half, rows + 2 * half
+    tiles = Tiles(cols)
+    width = tiles.width
+    mid = rows + 2 * half
     parity = lax.axis_index("rows") % 2
-    side = lax.axis_index("ang")
-    chunks = lane_chunks(width)
-    cut = tiles - 1 - side
-    cut_next = lax.rem(cut + 1, tiles)
-
-    def tile(j):
-        return pl.ds(pl.multiple_of(j * LANES, LANES), LANES)
-
-    def pair(j):
-        return pl.ds(pl.multiple_of(j * LANES, LANES), 2 * LANES)
-
-    def ahead(j, base):
-        return base + jnp.where(j == cut, 1, 0)
-
-    def back(j, base):
-        return base + jnp.where(j == cut, 1, jnp.where(j == cut_next, 2, 0))
 
     for slab, ref, margin in ((0, near_slab, 4 * half), (1, far_raw, 2 * half)):
         ref[margin : margin + 2 * rows, :cols] = slices[slab].reshape(2 * rows, cols)
         ref[margin : margin + 2 * rows, cols:width] = across[slab * 2 * rows : (slab + 1) * 2 * rows]
         begin = 0 if slab == 0 else 4 * half
-        for late, body, tail in ((parity, outer, corner), (1 - parity, inner, None)):
-            at = pl.ds(pl.multiple_of(late * (2 * rows + margin), 16), margin)
-            ref[at, :cols] = body[begin : begin + margin]
-            if tail is not None:
-                ref[at, cols:width] = tail[begin : begin + margin]
-            else:
-                frm = slab * 2 * rows + (1 - late) * (2 * rows - margin)
-                ref[at, cols:width] = across_inner[pl.ds(pl.multiple_of(frm, 16), margin)]
+        outer_at = pl.ds(pl.multiple_of(parity * (2 * rows + margin), 16), margin)
+        inner_at = pl.ds(pl.multiple_of((1 - parity) * (2 * rows + margin), 16), margin)
+        ref[outer_at, :cols] = outer[begin // 2 : (begin + margin) // 2].reshape(margin, cols)
+        ref[outer_at, cols:width] = corner[begin : begin + margin]
+        ref[inner_at, :cols] = inner[begin : begin + margin]
+        frm = slab * 2 * rows + parity * (2 * rows - margin)
+        ref[inner_at, cols:width] = across_inner[pl.ds(pl.multiple_of(frm, 16), margin)]
     far_raw[:, width:] = far_raw[:, :LANES]
 
-    def planar(j, carry_):
-        both = dot(split_far[...], far_raw[:, pair(j)])
-        far_slab[:, tile(j)] = both[:, half : half + LANES]
-        return carry_
-
-    lax.fori_loop(0, tiles, planar, 0)
-
-    for at, size in chunks:
-        result = dot(row_near[...], near_slab[:, at : at + size])
+    for j in range(tiles.count):
+        far_slab[:, tile(j)] = dot(split_far[...], far_raw[:, pair(j)])[:, half : half + LANES]
+
+    for at, size in lane_chunks(width):
+        here = slice(at, at + size)
+        result = dot(row_near[...], near_slab[:, here])
         for member in range(2):
             top = member * 2 * mid
             re, im = result[top : top + mid], result[top + mid : top + 2 * mid]
-            vr = waves[2 * member : 2 * member + 1, at : at + size]
-            vi = waves[2 * member + 1 : 2 * member + 2, at : at + size]
-            entry[member, :mid, at : at + size] = (re * vr - im * vi).astype(BF16)
-            entry[member, mid:, at : at + size] = (re * vi + im * vr).astype(BF16)
+            vr, vi = waves[2 * member : 2 * member + 1, here], waves[2 * member + 1 : 2 * member + 2, here]
+            entry[member, :mid, here] = (re * vr - im * vi).astype(BF16)
+            entry[member, mid:, here] = (re * vi + im * vr).astype(BF16)
     for member in range(2):
         entry[member, :, width:] = entry[member, :, :LANES]
 
-    def angle(member, measured):
-        def first(j, carry_):
-            x = jnp.concatenate([entry[member, :mid, pair(j)], entry[member, mid:, pair(j)]], axis=1)
-            y = dot(x, col_taps[ahead(j, 0)]).astype(BF16)
-            re, im = y[:, :LANES], y[:, LANES:]
-            field[:mid, tile(j)] = re
-            field[mid:, tile(j)] = im
-            re, im = re.astype(F32), im.astype(F32)
-            sr, si = far_slab[:mid, tile(j)], far_slab[mid:, tile(j)]
-            after[:mid, tile(j)] = (sr * re - si * im).astype(BF16)
-            after[mid:, tile(j)] = (sr * im + si * re).astype(BF16)
-            return carry_
-
-        lax.fori_loop(0, tiles, first, 0)
-        for at, size in chunks:
-            narrow[:, LANES + at : LANES + at + size] = dot(row_fwd[...], after[:, at : at + size]).astype(BF16)
-            meas[:, at : at + size] = dot(split_meas[...], measured[:, at : at + size])
-        narrow[:, :LANES] = narrow[:, width : width + LANES]
-
-        def second(j, carry_):
-            x = jnp.concatenate([narrow[:rows, pair(j)], narrow[rows:, pair(j)]], axis=1)
-            y = dot(x, col_taps[back(j, 2)]).astype(BF16).astype(F32)
-            shifted[:rows, tile(j)] = (y[:, :LANES] - meas[:rows, tile(j)]).astype(BF16)
-            shifted[rows:, tile(j)] = (y[:, LANES:] - meas[rows:, tile(j)]).astype(BF16)
-            return carry_
-
-        lax.fori_loop(0, tiles, second, 0)
-        shifted[:, width:] = shifted[:, :LANES]
-
-        def third(j, carry_):
-            x = jnp.concatenate([shifted[:rows, pair(j)], shifted[rows:, pair(j)]], axis=1)
-            y = dot(x, col_taps[ahead(j, 5)]).astype(BF16)
-            narrow[:rows, tile(j)] = y[:, :LANES]
-            narrow[rows:, tile(j)] = y[:, LANES:]
-            return carry_
-
-        lax.fori_loop(0, tiles, third, 0)
-        for at, size in chunks:
-            y = dot(row_adj[...], narrow[:, at : at + size])
-            br, bi = y[:mid], y[mid:]
-            ir, ii = field[:mid, at : at + size].astype(F32), field[mid:, at : at + size].astype(F32)
-            sr, si = far_slab[:mid, at : at + size], far_slab[mid:, at : at + size]
-            here = slice(LANES + at, LANES + at + size)
-            carry[:mid, here] = (sr * br + si * bi).astype(BF16)
-            carry[mid:, here] = (sr * bi - si * br).astype(BF16)
-            fr, fi = ir * br + ii * bi, ir * bi - ii * br
-            if member == 0:
-                far_sum[:mid, here] = fr
-                far_sum[mid:, here] = fi
-            else:
-                far_sum[:mid, here] += fr
-                far_sum[mid:, here] += fi
-        carry[:, :LANES] = carry[:, width : width + LANES]
-
-        def fourth(j, carry_):
-            x = jnp.concatenate([carry[:mid, pair(j)], carry[mid:, pair(j)]], axis=1)
-            y = dot(x, col_taps[back(j, 7)])
-            re, im = y[:, :LANES], y[:, LANES:]
-            vr = waves[2 * member : 2 * member + 1, tile(j)]
-            vi = waves[2 * member + 1 : 2 * member + 2, tile(j)]
-            top = member * 2 * mid
-            into[top : top + mid, tile(j)] = (re * vr + im * vi).astype(BF16)
-            into[top + mid : top + 2 * mid, tile(j)] = (im * vr - re * vi).astype(BF16)
-            return carry_
-
-        lax.fori_loop(0, tiles - 1, fourth, 0)
-
-    angle(0, meas_own)
-    angle(1, meas_other)
-
-    near_margin = 4 * half
+    def store(at, here, re, im):
+        far_sum[:mid, here] = re
+        far_sum[mid:, here] = im
+
+    forward_angle(tiles, entry.at[0], far_slab, row_fwd, col_taps, field, after, narrow, leaving)
+    backward_angle(
+        tiles, 0, leaving, meas_own, field, far_slab, split_meas, row_adj, col_taps, waves, residue, narrow, carry,
+        store, into_own,
+    )
+    forward_angle(
+        tiles, entry.at[1], far_slab, row_fwd, col_taps, field_other, after, narrow, leaving_other
+    )
+
+
+def other_kernel(
+    half,
+    far_slab, field, leaving, far_own, into_own, measured,
+    row_adj, row_near_adj, col_taps, split_meas, waves,
+    into, far_sum, outer_sums, inner_sums,
+    residue, narrow, carry,
+):
+    cols = into_own.shape[1]
+    tiles = Tiles(cols)
+    mid = field.shape[0] // 2
+    rows = mid - 2 * half
+    parity = lax.axis_index("rows") % 2
+
+    def add(at, here, re, im):
+        far_sum[:mid, here] = far_own[:mid, here] + re
+        far_sum[mid:, here] = far_own[mid:, here] + im
+
+    into[: 2 * mid] = into_own[...]
+    backward_angle(
+        tiles, 1, leaving, measured, field, far_slab, split_meas, row_adj, col_taps, waves, residue, narrow, carry,
+        add, into.at[2 * mid :],
+    )
+    far_sum[:, :LANES] = far_sum[:, tiles.width :]
+
+    margin = 4 * half
     for at, size in lane_chunks(cols):
         here = slice(at, at + size)
-        y = dot(row_near_adj[...], into[:, here])
-        near_own[:, here] = y[near_margin : near_margin + 2 * rows]
-        low = y[:near_margin].astype(BF16)
-        high = y[near_margin + 2 * rows :].astype(BF16)
-        outer_sums[:near_margin, here] = jnp.where(parity == 0, low, high)
-        inner_sums[:near_margin, here] = jnp.where(parity == 0, high, low)
-    far_sum[:, :LANES] = far_sum[:, width : width + LANES]
-
-    def far_out(j, carry_):
-        y = far_sum[:, pair(j)][:, LANES - half : 2 * LANES - half]
+        low = dot(row_near_adj[:margin], into[:, here]).astype(BF16)
+        high = dot(row_near_adj[margin + 2 * rows :], into[:, here]).astype(BF16)
+        outer_sums[:margin, here] = jnp.where(parity == 0, low, high)
+        inner_sums[:margin, here] = jnp.where(parity == 0, high, low)
+    for j in range(tiles.count - 1):
         for comp in range(2):
-            part = y[comp * mid : (comp + 1) * mid]
-            far_own[comp, :, tile(j)] = part[half : half + rows]
-            low, high = part[:half].astype(BF16), part[half + rows :].astype(BF16)
-            top = near_margin + comp * half
-            outer_sums[top : top + half, tile(j)] = jnp.where(parity == 0, low, high)
-            inner_sums[top : top + half, tile(j)] = jnp.where(parity == 0, high, low)
-        return carry_
-
-    lax.fori_loop(0, tiles - 1, far_out, 0)
-
-
-def finish_kernel(half, near_own, far_own, outer, inner, near, far, total):
+            top = comp * mid
+            low = far_sum[top : top + half, pair(j)][:, LANES - half : 2 * LANES - half].astype(BF16)
+            high = far_sum[top + half + rows : top + mid, pair(j)][:, LANES - half : 2 * LANES - half].astype(BF16)
+            there = slice(margin + comp * half, margin + (comp + 1) * half)
+            outer_sums[there, tile(j)] = jnp.where(parity == 0, low, high)
+            inner_sums[there, tile(j)] = jnp.where(parity == 0, high, low)
+
+
+def sums_kernel(
+    half, into, far_sum, row_near_adj, inner, near, far, near_edge, far_edge, near_total, far_total, sems
+):
+    cols = into.shape[1]
+    mid = far_sum.shape[0] // 2
+    rows = mid - 2 * half
+    parity = lax.axis_index("rows") % 2
+    margin = 4 * half
+    for j in range(cols // LANES):
+        for comp in range(2):
+            top = comp * mid + half
+            far_total[:, comp, tile(j)] = far_sum[top : top + rows, pair(j)][:, LANES - half : 2 * LANES - half]
+    at = pl.ds((1 - parity) * (rows - half), half)
+    for comp in range(2):
+        far_total[at, comp, :] += inner[margin + comp * half : margin + (comp + 1) * half].astype(F32)
+    far_edge[...] = far_total[pl.ds(parity * (rows - half), half)]
+    rest = pl.ds((1 - parity) * half, rows - half)
+    far_copy = pltpu.make_async_copy(far_total.at[rest], far.at[rest], sems.at[0])
+    far_copy.start()
+    for at, size in lane_chunks(cols):
+        here = slice(at, at + size)
+        y = dot(row_near_adj[margin : margin + 2 * rows], into[:, here])
+        near_total[:, :, here] = y.reshape(rows, 2, size)
+    at = pl.ds((1 - parity) * (rows - 2 * half), 2 * half)
+    near_total[at] += inner[:margin].astype(F32).reshape(2 * half, 2, cols)
+    near_edge[...] = near_total[pl.ds(parity * (rows - 2 * half), 2 * half)]
+    rest = pl.ds((1 - parity) * 2 * half, rows - 2 * half)
+    near_copy = pltpu.make_async_copy(near_total.at[rest], near.at[rest], sems.at[1])
+    near_copy.start()
+    far_copy.wait()
+    near_copy.wait()
+
+
+def finish_kernel(half, near_in, far_in, near_edge, far_edge, outer, near, far, near_total, far_total, sems):
     rows, cols = near.shape[0], near.shape[2]
     parity = lax.axis_index("rows") % 2
-    size = 4 * half
-    total[...] = near_own[...]
-    for late, got in ((parity, outer), (1 - parity, inner)):
-        at = pl.ds(pl.multiple_of(late * (2 * rows - size), 16), size)
-        total[at] += got[:size].astype(F32)
-    near[...] = total[...].reshape(rows, 2, cols)
+    margin = 4 * half
+    near_total[...] = near_edge[...] + outer[:margin].astype(F32).reshape(2 * half, 2, cols)
+    at = pl.ds(parity * (rows - 2 * half), 2 * half)
+    near_copy = pltpu.make_async_copy(near_total, near.at[at], sems.at[0])
+    near_copy.start()
     for comp in range(2):
-        total[:rows] = far_own[comp]
-        for late, got in ((parity, outer), (1 - parity, inner)):
-            at = pl.ds(pl.multiple_of(late * (rows - half), 16), half)
-            total[at] += got[size + comp * half : size + (comp + 1) * half].astype(F32)
-        far[:, comp, :] = total[:rows]
-
-
-def call(kernel, outs, operands, scalars=(), scratch=(), cost=0):
-    specs = [
-        pl.BlockSpec(memory_space=pltpu.SMEM if i in scalars else pltpu.VMEM) for i in range(len(operands))
-    ]
+        got = outer[margin + comp * half : margin + (comp + 1) * half].astype(F32)
+        far_total[:, comp, :] = far_edge[:, comp, :] + got
+    at = pl.ds(parity * (rows - half), half)
+    far_copy = pltpu.make_async_copy(far_total, far.at[at], sems.at[1])
+    far_copy.start()
+    near_copy.wait()
+    far_copy.wait()
+
+
+def call(kernel, outs, operands, scalars=(), outside=(), outs_outside=(), scratch=(), aliases=None, flops=0):
+    def place(i):
+        return pltpu.SMEM if i in scalars else pl.ANY if i in outside else pltpu.VMEM
+
     return pl.pallas_call(
         kernel,
         out_shape=[jax.ShapeDtypeStruct(shape, dtype) for shape, dtype in outs],
-        in_specs=specs,
-        out_specs=[pl.BlockSpec(memory_space=pltpu.VMEM)] * len(outs),
-        scratch_shapes=[pltpu.VMEM(shape, dtype) for shape, dtype in scratch],
+        in_specs=[pl.BlockSpec(memory_space=place(i)) for i in range(len(operands))],
+        out_specs=[
+            pl.BlockSpec(memory_space=pl.ANY if i in outs_outside else pltpu.VMEM) for i in range(len(outs))
+        ],
+        scratch_shapes=[one if not isinstance(one, tuple) else pltpu.VMEM(*one) for one in scratch],
+        input_output_aliases=aliases or {},
         compiler_params=pltpu.CompilerParams(vmem_limit_bytes=40 * 2**20),
-        cost_estimate=pl.CostEstimate(flops=cost, bytes_accessed=0, transcendentals=0),
+        cost_estimate=pl.CostEstimate(flops=flops, bytes_accessed=0, transcendentals=0),
     )(*operands)
 
 
@@ -354,57 +439,84 @@
     half = (kernel_taps.shape[1] - 1) // 2
     wide, mid, width = rows + 4 * half, rows + 2 * half, cols + LANES
     count = lax.axis_size("rows")
-    sides = lax.axis_size("ang")
     outer_pairs = [(i, j) for i in range(count) if 0 <= (j := i - 1 + 2 * (i % 2)) < count]
     inner_pairs = [(i, i + 1 - 2 * (i % 2)) for i in range(count)]
-    side_pairs = [(i, 1 - i) for i in range(sides)]
-    corner_pairs = [
-        (i * sides + s, j * sides + 1 - s) for i, j in outer_pairs for s in range(sides)
-    ]
+    side_pairs = [(i, 1 - i) for i in range(lax.axis_size("ang"))]
     edge = 6 * half
-    outer, inner, across, corner = call(
+    (outer,) = call(
+        functools.partial(outer_kernel, half), [((3 * half, 2, cols), BF16)], (slices,), outside=(0,),
+        outs_outside=(0,), scratch=[pltpu.SemaphoreType.DMA((2,))],
+    )
+    outer_got = lax.ppermute(outer, "rows", outer_pairs)
+    angle_freq = angle_freq.T
+    inner, across = call(
         functools.partial(edges_kernel, half),
-        [((edge, cols), BF16), ((edge, cols), BF16), ((4 * rows + 16, LANES), BF16), ((edge, LANES), BF16)],
-        (slices, angle_freq, chosen), scalars=(1, 2),
-    )
-    outer_got = lax.ppermute(outer, "rows", outer_pairs)
+        [((edge, cols), BF16), ((4 * rows + 16, LANES), BF16)],
+        (slices, angle_freq, chosen, outer), scalars=(2,), outside=(3,),
+    )
     across_got = lax.ppermute(across, "ang", side_pairs)
-    corner_got = lax.ppermute(corner, ("rows", "ang"), corner_pairs)
     inner_got = lax.ppermute(inner, "rows", inner_pairs)
     meas_own, meas_out = call(
-        measured_kernel, [((2 * rows, width), BF16)] * 2, (measured,),
+        measured_kernel, [((2 * rows, width), BF16)] * 2, (measured, inner), outside=(1,),
     )
     meas_got = lax.ppermute(meas_out, "ang", side_pairs)
     across_inner = lax.ppermute(across_got, "rows", inner_pairs)
-    mats = call(
+    (strip,) = call(functools.partial(strip_kernel, half), [((edge, LANES), BF16)], (across_got,))
+    corner_got = lax.ppermute(strip, "rows", outer_pairs)
+    row_near, row_fwd, row_adj, row_near_adj, col_taps, split_far, split_meas, waves = call(
         functools.partial(matrices_kernel, rows, cols, length),
         [
             ((4 * mid, 2 * wide), BF16), ((2 * rows, 2 * mid), BF16), ((2 * mid, 2 * rows), BF16),
             ((2 * wide, 4 * mid), BF16), ((10, 4 * LANES, 2 * LANES), BF16),
             ((2 * mid, 2 * mid), BF16), ((2 * rows, 2 * rows), BF16), ((8, width), F32),
         ],
-        (kernel_taps, angle_freq, chosen, across_got), scalars=(1, 2),
-    )
-    near_own, far_own, outer_sums, inner_sums = call(
-        functools.partial(main_kernel, half),
-        [((2 * rows, cols), F32), ((2, rows, cols), F32), ((edge, cols), BF16), ((edge, cols), BF16)],
-        (slices, outer_got, inner_got, across_got, corner_got, across_inner, meas_own, meas_got, *mats),
+        (kernel_taps, angle_freq, chosen, across_got), scalars=(2,),
+    )
+    far_slab, field_other, leaving_other, far_sum, into_own = call(
+        functools.partial(own_kernel, half),
+        [
+            ((2 * mid, width), F32), ((2 * mid, width), BF16), ((2 * rows, width), BF16),
+            ((2 * mid, width + LANES), F32), ((2 * mid, cols), BF16),
+        ],
+        (
+            slices, outer_got, inner_got, across_got, corner_got, across_inner, meas_own,
+            row_near, row_fwd, row_adj, col_taps, split_far, split_meas, waves,
+        ),
         scratch=[
-            ((2 * wide, width), BF16), ((2 * mid, width + LANES), BF16), ((2 * mid, width), F32),
-            ((2, 2 * mid, width + LANES), BF16), ((2 * mid, width), BF16), ((2 * mid, width), BF16),
-            ((2 * mid, width + LANES), BF16), ((2 * rows, width + LANES), BF16),
-            ((2 * rows, width + LANES), BF16), ((2 * rows, width), F32), ((4 * mid, cols), BF16),
-            ((2 * mid, width + LANES), F32),
+            ((2 * wide, width), BF16), ((2 * mid, width + LANES), BF16), ((2, 2 * mid, width + LANES), BF16),
+            ((2 * mid, width), BF16), ((2 * mid, width), BF16), ((2 * rows, width + LANES), BF16),
+            ((2 * rows, width), BF16), ((2 * rows, width + LANES), BF16), ((2 * mid, width + LANES), BF16),
         ],
-        cost=8 * 10**9,
+        flops=OWN_FLOPS,
+    )
+    into, far_sum, outer_sums, inner_sums = call(
+        functools.partial(other_kernel, half),
+        [
+            ((4 * mid, cols), BF16), ((2 * mid, width + LANES), F32), ((edge, cols), BF16), ((edge, cols), BF16),
+        ],
+        (
+            far_slab, field_other, leaving_other, far_sum, into_own, meas_got,
+            row_adj, row_near_adj, col_taps, split_meas, waves,
+        ),
+        scratch=[
+            ((2 * rows, width + LANES), BF16), ((2 * rows, width + LANES), BF16), ((2 * mid, width + LANES), BF16),
+        ],
     )
     outer_back = lax.ppermute(outer_sums, "rows", outer_pairs)
     inner_back = lax.ppermute(inner_sums, "rows", inner_pairs)
+    near, far, near_edge, far_edge = call(
+        functools.partial(sums_kernel, half),
+        [
+            ((rows, 2, cols), F32), ((rows, 2, cols), F32), ((2 * half, 2, cols), F32), ((half, 2, cols), F32),
+        ],
+        (into, far_sum, row_near_adj, inner_back), outs_outside=(0, 1),
+        scratch=[((rows, 2, cols), F32), ((rows, 2, cols), F32), pltpu.SemaphoreType.DMA((2,))],
+    )
     near, far = call(
         functools.partial(finish_kernel, half),
         [((rows, 2, cols), F32)] * 2,
-        (near_own, far_own, outer_back, inner_back),
-        scratch=[((2 * rows, cols), F32)],
+        (near, far, near_edge, far_edge, outer_back), outside=(0, 1), outs_outside=(0, 1), aliases={0: 0, 1: 1},
+        scratch=[((2 * half, 2, cols), F32), ((half, 2, cols), F32), pltpu.SemaphoreType.DMA((2,))],
     )
     return near, far
 

time: 69.7 us -> 47.5 us (0.68)
  Pallas kernels: 31.5 us -> 18.8 us
  waiting for transfers between devices: 16.7 us -> 10.4 us
  local copies, waits for them, and re-layouts: 5.1 us -> 1.92 us
    pallas_call x5 -> x9, Pallas kernels: 31.5 us -> 18.8 us  [call(): pl.pallas_call(kernel, out_shape=[jax.ShapeDtypeStruct(shape, dtype) for...]
    ppermute x1, waiting for transfers between devices: 9.81 us -> 5.83 us  [columns_local(): outer_back = lax.ppermute(outer_sums, 'rows', outer_pairs)]
    ppermute x1, waiting for transfers between devices: 6.87 us -> 2.91 us  [columns_local(): across_got = lax.ppermute(across, 'ang', side_pairs)]
    unnamed x9 -> x14, local copies, waits for them, and re-layouts: 5.1 us -> 1.92 us
    ppermute x1, waiting for transfers between devices: 0.01 us -> 1.6 us  [columns_local(): corner_got = lax.ppermute(strip, 'rows', outer_pairs)]
    ppermute x1, starting transfers between devices: 2.52 us -> 3.61 us  [columns_local(): outer_back = lax.ppermute(outer_sums, 'rows', outer_pairs)]
    ppermute x1, starting transfers between devices: 0.32 us -> 1.28 us  [columns_local(): across_got = lax.ppermute(across, 'ang', side_pairs)]
    ppermute x1, starting transfers between devices: 1.28 us -> 0.32 us  [columns_local(): meas_got = lax.ppermute(meas_out, 'ang', side_pairs)]
  transfers between devices with their start and end apart: 8 -> 8, of which waited for: 2 -> 3; matrix products, arithmetic and copies ran while one was open for 1% -> 0% of each run, Pallas kernels for 7% -> 28%
where the time goes in v2:
time: 47.5 us; the launch traced here: 47.2 us
  Pallas kernels  18.8 us (40%)
  starting transfers between devices  14.5 us (31%)
  waiting for transfers between devices  10.4 us (22%)
  local copies, waits for them, and re-layouts  1.92 us (4%)
  between operations  1.6 us (3%)
    pallas_call x9, Pallas kernels, call(): pl.pallas_call(kernel, out_shape=[jax.ShapeDtypeStruct(shape, dtype) for...  18.8 us
    ppermute x1, waiting for transfers between devices, columns_local(): outer_back = lax.ppermute(outer_sums, 'rows', outer_pairs)  5.83 us
    ppermute x1, starting transfers between devices, columns_local(): outer_got = lax.ppermute(outer, 'rows', outer_pairs)  3.84 us
    ppermute x1, starting transfers between devices, columns_local(): outer_back = lax.ppermute(outer_sums, 'rows', outer_pairs)  3.61 us
    ppermute x1, starting transfers between devices, columns_local(): corner_got = lax.ppermute(strip, 'rows', outer_pairs)  3.04 us
    ppermute x1, waiting for transfers between devices, columns_local(): across_got = lax.ppermute(across, 'ang', side_pairs)  2.91 us
    ppermute x1, starting transfers between devices, columns_local(): across_inner = lax.ppermute(across_got, 'rows', inner_pairs)  2.14 us
    unnamed x14, local copies, waits for them, and re-layouts  1.92 us
  transfers between devices with their start and end apart: 8, of which 3 were waited for; matrix products, arithmetic and copies ran while one was open for 0% of the time, Pallas kernels for 28%

profile of v2, /device:TPU:17, one launch (start us, length us, event | category | flops | bytes accessed | tf_op | source)
XLA Modules:
  0.0 47.2 jit_solution(15796093723157783412)
XLA Ops:
  0.6 0.0 copy-start
  0.6 1.2 %copy-done = bf16[2,128,2,1024]{3,2,1,0:T(2,128)(2,1)S(1)} copy-done((bf16[2,128,2,1024]{3,2,1,0:T(2,128)(2,1)S(1)}, bf16[2,128,2,1024]{3,2,1,0:T(2,128)(2,1)}, u32[]{:S(2)}) %copy-start) | copy-done | bytes 1048600
  1.9 0.0 copy-start.3
  1.9 0.0 copy-start.5
  1.9 0.0 copy-start.6
  1.9 0.2 shard_map.68.sent
  2.1 0.0 copy-start.1
  2.1 3.8 %collective-permute-start = (bf16[96,2,1024]{2,1,0:T(2,128)(2,1)S(1)}, bf16[96,2,1024]{2,1,0:T(2,128)(2,1)S(1)}, u32[]{:S(2)}, u32[]{:S(2)}) collective-permute-start(bf16[96,2,1024]{2,1,0:T(2,128)(2,1)S(1)} %shard_map.68.sent), channel_id=1, source_target_pairs={{2,4},{4,2},{6,8},{8,6},{10,12},{12,10},{14,16},{16,14},{18,20},{2... | collective-permute-start | bytes 1179656 | tf_op jit(solution)/shard_map/ppermute | solution.py:450
  6.6 0.0 copy-start.4
  6.6 0.7 %copy-done.4 = f32[128,2]{0,1:T(2,128)S(1)} copy-done((f32[128,2]{0,1:T(2,128)S(1)}, f32[128,2]{0,1:T(2,128)}, u32[]{:S(2)}) %copy-start.4) | copy-done | bytes 1048
  7.3 0.3 shard_map.69
  7.6 0.0 collective-permute-start.1
  7.7 1.3 %collective-permute-start.2 = (bf16[528,128]{1,0:T(8,128)(2,1)S(1)}, bf16[528,128]{1,0:T(8,128)(2,1)S(1)}, u32[]{:S(2)}, u32[]{:S(2)}) collective-permute-start(bf16[528,128]{1,0:T(8,128)(2,1)S(1)} %get-tuple-element.28), channel_id=1, source_target_pairs={{0,1},{1,0},{2,3},{3,2},{4,5},{5,4},{6,7},{7,6},{8,9},{9,8},{10,11... | collective-permute-start | bytes 405512 | tf_op jit(solution)/shard_map/ppermute | solution.py:457
  8.9 0.0 copy-done.3
  8.9 0.3 shard_map.71
  9.2 0.3 collective-permute-start.5
  9.5 2.9 %collective-permute-done.2.across = bf16[528,128]{1,0:T(8,128)(2,1)S(1)} collective-permute-done((bf16[528,128]{1,0:T(8,128)(2,1)S(1)}, bf16[528,128]{1,0:T(8,128)(2,1)S(1)}, u32[]{:S(2)}, u32[]{:S(2)}) %collective-permute-start.2) | collective-permute-done | bytes 135200 | tf_op jit(solution)/shard_map/ppermute | solution.py:457
  12.5 2.1 %collective-permute-start.4 = (bf16[528,128]{1,0:T(8,128)(2,1)S(1)}, bf16[528,128]{1,0:T(8,128)(2,1)S(1)}, u32[]{:S(2)}, u32[]{:S(2)}) collective-permute-start(bf16[528,128]{1,0:T(8,128)(2,1)S(1)} %collective-permute-done.2.across), channel_id=1, source_target_pairs={{0,2},{2,0},{4,6},{6,4},{8,10},{10,8},{12,14},{14,12},{16,18},{18,... | collective-permute-start | bytes 405512 | tf_op jit(solution)/shard_map/ppermute | solution.py:463
  14.6 3.0 %collective-permute-start.3 = (bf16[192,128]{1,0:T(8,128)(2,1)S(1)}, bf16[192,128]{1,0:T(8,128)(2,1)S(1)}, u32[]{:S(2)}, u32[]{:S(2)}) collective-permute-start(bf16[192,128]{1,0:T(8,128)(2,1)S(1)} %shard_map.70), channel_id=1, source_target_pairs={{2,4},{4,2},{6,8},{8,6},{10,12},{12,10},{14,16},{16,14},{18,20},{2... | collective-permute-start | bytes 147464 | tf_op jit(solution)/shard_map/ppermute | solution.py:465
  17.6 0.0 copy-done.5
  17.7 0.0 copy-done.6
  17.7 1.5 %shard_map.72 = (bf16[768,512]{1,0:T(8,128)(2,1)S(1)}, bf16[256,384]{1,0:T(8,128)(2,1)S(1)}, bf16[384,256]{1,0:T(8,128)(2,1)S(1)}, bf16[512,768]{1,0:T(8,128)(2,...) custom-call(bf16[2,65]{1,0:T(2,128)(2,1)S(1)} %copy-done.6, ...), custom_call_target="tpu_custom_call" | custom-call | tf_op jit(solution)/shard_map/pallas_call | solution.py:422
  19.2 0.0 copy-start.2
  19.2 1.6 %collective-permute-done.3.corner = bf16[192,128]{1,0:T(8,128)(2,1)S(1)} collective-permute-done((bf16[192,128]{1,0:T(8,128)(2,1)S(1)}, bf16[192,128]{1,0:T(8,128)(2,1)S(1)}, u32[]{:S(2)}, u32[]{:S(2)}) %collective-permute-start.3) | collective-permute-done | bytes 49184 | tf_op jit(solution)/shard_map/ppermute | solution.py:465
  20.8 0.0 collective-permute-done.4.across_inner
  20.8 0.0 collective-permute-done.outer
  20.8 0.0 collective-permute-done.1.inner
  20.8 0.0 copy-done.1
  20.8 7.2 %shard_map.73 = (f32[384,1152]{1,0:T(8,128)S(1)}, bf16[384,1152]{1,0:T(8,128)(2,1)S(1)}, bf16[256,1152]{1,0:T(8,128)(2,1)S(1)}, f32[384,1280]{1,0:T(8,128)S(1)}, bf16[384,1024]{1,0:T(8,128)(2,1)S(1)}) custom-call(bf16[2,128,2,1024]{3,2,1,0:T(2,128)(2,1)S(1)} %copy-done.1, bf16[96,2,1024]{2,1,0:T(2,128)(2,1)S(1)} %collective-permute-done.outer, ...), custom_call_target="tpu_custom_call" | custom-call | flops 4000000000 | tf_op jit(solution)/shard_map/pallas_call | solution.py:422
  28.0 0.0 copy-done.2
  28.1 0.0 collective-permute-done.5.measured
  28.1 4.5 %shard_map.74 = (bf16[768,1024]{1,0:T(8,128)(2,1)S(1)}, f32[384,1280]{1,0:T(8,128)S(1)}, bf16[192,1024]{1,0:T(8,128)(2,1)S(1)}, bf16[192,1024]{1,0:T(8,128)(2,1)S(1)}) custom-call(f32[384,1152]{1,0:T(8,128)S(1)} %get-tuple-element.37.far_slab, bf16[384,1152]{1,0:T(8,128)(2,1)S(1)} %get-tuple-element.38.field, ...), custom_call_target="tpu_custom_call" | custom-call | tf_op jit(solution)/shard_map/pallas_call | solution.py:422
  32.6 0.2 collective-permute-start.6
  32.8 3.6 %collective-permute-start.7 = (bf16[192,1024]{1,0:T(8,128)(2,1)S(1)}, bf16[192,1024]{1,0:T(8,128)(2,1)S(1)}, u32[]{:S(2)}, u32[]{:S(2)}) collective-permute-start(bf16[192,1024]{1,0:T(8,128)(2,1)S(1)} %get-tuple-element.51), channel_id=1, source_target_pairs={{2,4},{4,2},{6,8},{8,6},{10,12},{12,10},{14,16},{16,14},{18,20},{2... | collective-permute-start | bytes 1179656 | tf_op jit(solution)/shard_map/ppermute | solution.py:505
  36.4 0.0 collective-permute-done.6.inner
  36.4 3.8 %shard_map.75 = (f32[128,2,1024]{2,1,0:T(2,128)}, f32[128,2,1024]{2,1,0:T(2,128)}, f32[64,2,1024]{2,1,0:T(2,128)S(1)}, f32[32,2,1024]{2,1,0:T(2,128)S(1)}) custom-call(bf16[768,1024]{1,0:T(8,128)(2,1)S(1)} %get-tuple-element.44.into, f32[384,1280]{1,0:T(8,128)S(1)} %get-tuple-element.45.far_sum, bf16[512,768]{1,0:T(8,128)(2,1)S(1)} %get-tuple-element.43.row_near_adj, ...), custom_call_target="tpu_custom_call" | custom-call | tf_op jit(solution)/shard_map/pallas_call | solution.py:422
  40.3 5.8 %collective-permute-done.7.outer = bf16[192,1024]{1,0:T(8,128)(2,1)S(1)} collective-permute-done((bf16[192,1024]{1,0:T(8,128)(2,1)S(1)}, bf16[192,1024]{1,0:T(8,128)(2,1)S(1)}, u32[]{:S(2)}, u32[]{:S(2)}) %collective-permute-start.7) | collective-permute-done | bytes 393248 | tf_op jit(solution)/shard_map/ppermute | solution.py:505
  46.1 1.0 %shard_map.76 = (f32[128,2,1024]{2,1,0:T(2,128)}, f32[128,2,1024]{2,1,0:T(2,128)}) custom-call(f32[128,2,1024]{2,1,0:T(2,128)} %get-tuple-element.47.near_in, f32[128,2,1024]{2,1,0:T(2,128)} %get-tuple-element.48.far_in, f32[64,2,1024]{2,1,0:T(2,128)S(1)} %get-tuple-element.49.near_edge, ...), custom_call_target="tpu_custom_call", output_to_operand_aliasing={{0}: (0, {}), {1}: (1, {})} | custom-call | tf_op jit(solution)/shard_map/pallas_call | solution.py:422
  (1 shorter events, 0.0 us)
Async XLA Ops:
  0.6 1.2 %copy-start = (bf16[2,128,2,1024]{3,2,1,0:T(2,128)(2,1)S(1)}, bf16[2,128,2,1024]{3,2,1,0:T(2,128)(2,1)}, u32[]{:S(2)}) copy-start(bf16[2,128,2,1024]{3,2,1,0:T(2,128)(2,1)} %slices.5) | copy-start | bytes 3145732
  1.9 7.1 %copy-start.3 = (bf16[1,128,2,2048]{3,2,1,0:T(2,128)(2,1)S(1)}, bf16[1,128,2,2048]{3,2,1,0:T(2,128)(2,1)}, u32[]{:S(2)}) copy-start(bf16[1,128,2,2048]{3,2,1,0:T(2,128)(2,1)} %measured.1) | copy-start | bytes 3145732
  1.9 15.8 %copy-start.5 = (f32[128,2]{0,1:T(2,128)S(1)}, f32[128,2]{0,1:T(2,128)}, u32[]{:S(2)}) copy-start(f32[128,2]{0,1:T(2,128)} %param.8) | copy-start | bytes 3076
  1.9 15.8 %copy-start.6 = (bf16[2,65]{1,0:T(2,128)(2,1)S(1)}, bf16[2,65]{1,0:T(2,128)(2,1)}, u32[]{:S(2)}) copy-start(bf16[2,65]{1,0:T(2,128)(2,1)} %taps.1) | copy-start | bytes 784
  2.1 18.8 %copy-start.1 = (bf16[2,128,2,1024]{3,2,1,0:T(2,128)(2,1)S(1)}, bf16[2,128,2,1024]{3,2,1,0:T(2,128)(2,1)}, u32[]{:S(2)}) copy-start(bf16[2,128,2,1024]{3,2,1,0:T(2,128)(2,1)} %slices.5) | copy-start | bytes 3145732
  2.1 18.7 %collective-permute-start = (bf16[96,2,1024]{2,1,0:T(2,128)(2,1)S(1)}, bf16[96,2,1024]{2,1,0:T(2,128)(2,1)S(1)}, u32[]{:S(2)}, u32[]{:S(2)}) collective-permute-start(bf16[96,2,1024]{2,1,0:T(2,128)(2,1)S(1)} %shard_map.68.sent), channel_id=1, source_target_pairs={{2,4},{4,2},{6,8},{8,6},{10,12},{12,10},{14,16},{16,14},{18,20},{2... | collective-permute-start | bytes 1179656 | tf_op jit(solution)/shard_map/ppermute | solution.py:450
  6.6 0.7 %copy-start.4 = (f32[128,2]{0,1:T(2,128)S(1)}, f32[128,2]{0,1:T(2,128)}, u32[]{:S(2)}) copy-start(f32[128,2]{0,1:T(2,128)} %param.8) | copy-start | bytes 3076
  7.6 13.2 %collective-permute-start.1 = (bf16[192,1024]{1,0:T(8,128)(2,1)S(1)}, bf16[192,1024]{1,0:T(8,128)(2,1)S(1)}, u32[]{:S(2)}, u32[]{:S(2)}) collective-permute-start(bf16[192,1024]{1,0:T(8,128)(2,1)S(1)} %get-tuple-element.27.inner), channel_id=1, source_target_pairs={{0,2},{2,0},{4,6},{6,4},{8,10},{10,8},{12,14},{14,12},{16,18},{18,... | collective-permute-start | bytes 1179656 | tf_op jit(solution)/shard_map/ppermute | solution.py:458
  7.7 4.8 %collective-permute-start.2 = (bf16[528,128]{1,0:T(8,128)(2,1)S(1)}, bf16[528,128]{1,0:T(8,128)(2,1)S(1)}, u32[]{:S(2)}, u32[]{:S(2)}) collective-permute-start(bf16[528,128]{1,0:T(8,128)(2,1)S(1)} %get-tuple-element.28), channel_id=1, source_target_pairs={{0,1},{1,0},{2,3},{3,2},{4,5},{5,4},{6,7},{7,6},{8,9},{9,8},{10,11... | collective-permute-start | bytes 405512 | tf_op jit(solution)/shard_map/ppermute | solution.py:457
  9.2 18.8 %collective-permute-start.5 = (bf16[256,1152]{1,0:T(8,128)(2,1)S(1)}, bf16[256,1152]{1,0:T(8,128)(2,1)S(1)}, u32[]{:S(2)}, u32[]{:S(2)}) collective-permute-start(bf16[256,1152]{1,0:T(8,128)(2,1)S(1)} %get-tuple-element.42), channel_id=1, source_target_pairs={{0,1},{1,0},{2,3},{3,2},{4,5},{5,4},{6,7},{7,6},{8,9},{9,8},{10,11... | collective-permute-start | bytes 1769480 | tf_op jit(solution)/shard_map/ppermute | solution.py:462
  12.5 8.4 %collective-permute-start.4 = (bf16[528,128]{1,0:T(8,128)(2,1)S(1)}, bf16[528,128]{1,0:T(8,128)(2,1)S(1)}, u32[]{:S(2)}, u32[]{:S(2)}) collective-permute-start(bf16[528,128]{1,0:T(8,128)(2,1)S(1)} %collective-permute-done.2.across), channel_id=1, source_target_pairs={{0,2},{2,0},{4,6},{6,4},{8,10},{10,8},{12,14},{14,12},{16,18},{18,... | collective-permute-start | bytes 405512 | tf_op jit(solution)/shard_map/ppermute | solution.py:463
  14.6 6.2 %collective-permute-start.3 = (bf16[192,128]{1,0:T(8,128)(2,1)S(1)}, bf16[192,128]{1,0:T(8,128)(2,1)S(1)}, u32[]{:S(2)}, u32[]{:S(2)}) collective-permute-start(bf16[192,128]{1,0:T(8,128)(2,1)S(1)} %shard_map.70), channel_id=1, source_target_pairs={{2,4},{4,2},{6,8},{8,6},{10,12},{12,10},{14,16},{16,14},{18,20},{2... | collective-permute-start | bytes 147464 | tf_op jit(solution)/shard_map/ppermute | solution.py:465
  19.2 8.8 %copy-start.2 = (bf16[10,512,256]{2,1,0:T(8,128)(2,1)}, bf16[10,512,256]{2,1,0:T(8,128)(2,1)S(1)}, u32[]{:S(2)}) copy-start(bf16[10,512,256]{2,1,0:T(8,128)(2,1)S(1)} %get-tuple-element.33.col_taps) | copy-start | bytes 7864324
  32.6 3.9 %collective-permute-start.6 = (bf16[192,1024]{1,0:T(8,128)(2,1)S(1)}, bf16[192,1024]{1,0:T(8,128)(2,1)S(1)}, u32[]{:S(2)}, u32[]{:S(2)}) collective-permute-start(bf16[192,1024]{1,0:T(8,128)(2,1)S(1)} %get-tuple-element.46), channel_id=1, source_target_pairs={{0,2},{2,0},{4,6},{6,4},{8,10},{10,8},{12,14},{14,12},{16,18},{18,... | collective-permute-start | bytes 1179656 | tf_op jit(solution)/shard_map/ppermute | solution.py:506
  32.8 13.3 %collective-permute-start.7 = (bf16[192,1024]{1,0:T(8,128)(2,1)S(1)}, bf16[192,1024]{1,0:T(8,128)(2,1)S(1)}, u32[]{:S(2)}, u32[]{:S(2)}) collective-permute-start(bf16[192,1024]{1,0:T(8,128)(2,1)S(1)} %get-tuple-element.51), channel_id=1, source_target_pairs={{2,4},{4,2},{6,8},{8,6},{10,12},{12,10},{14,16},{16,14},{18,20},{2... | collective-permute-start | bytes 1179656 | tf_op jit(solution)/shard_map/ppermute | solution.py:505

commit v3 on v0

--- a/solution.py
+++ b/solution.py
@@ -1,9 +1,674 @@
+import functools
 import math
 
 import jax
 import jax.numpy as jnp
 from jax import lax
+from jax.experimental import pallas as pl
+from jax.experimental.pallas import tpu as pltpu
 from jax.sharding import PartitionSpec as P
+
+LANES = 128
+BF16 = jnp.bfloat16
+STRIP_FLOPS = 1 * 10**9
+INNER_FLOPS = 0
+MATS_FLOPS = 0
+OWN_FLOPS = 1 * 10**9
+F32 = jnp.float32
+
+
+def dot(left, right):
+    return jnp.dot(left, right, preferred_element_type=F32)
+
+
+def iota(shape, dim):
+    return lax.broadcasted_iota(jnp.int32, shape, dim)
+
+
+def lane_chunks(width, step=2 * LANES):
+    return [(at, min(step, width - at)) for at in range(0, width, step)]
+
+
+def edges_kernel(half, slices, angle_freq, chosen, outer, inner, across, strips, table, sems):
+    rows, cols = slices.shape[1], slices.shape[3]
+    parity = lax.axis_index("rows") % 2
+    side = lax.axis_index("ang")
+    lane = pl.multiple_of((1 - side) * (cols - LANES), LANES)
+    copies = [(angle_freq, table), (slices.at[:, :, :, pl.ds(lane, LANES)], strips)]
+    for late, out in ((parity, outer), (1 - parity, inner)):
+        for slab, at, size in ((0, 0, 2 * half), (1, 2 * half, half)):
+            copies.append((slices.at[slab, pl.ds(late * (rows - size), size)], out.at[pl.ds(at, size)]))
+    copies = [pltpu.make_async_copy(frm, to, sems.at[i]) for i, (frm, to) in enumerate(copies)]
+    for copy in copies:
+        copy.start()
+    for copy in copies[:2]:
+        copy.wait()
+    for slab in range(2):
+        across[slab * 2 * rows : (slab + 1) * 2 * rows] = strips[slab].reshape(2 * rows, LANES)
+    row = iota((16, LANES), 0)
+    block = jnp.zeros((16, LANES), F32)
+    entry = jnp.where(iota(table.shape, 1) == chosen[0], table[...], 0.0)
+    freqs = jnp.sum(entry, axis=1, keepdims=True)
+    for part in range(2):
+        rest = jnp.broadcast_to(freqs[part : part + 1], (16, LANES))
+        for piece in range(3):
+            rounded = rest.astype(BF16).astype(F32)
+            block = jnp.where(row == 3 * part + piece, rounded, block)
+            rest = rest - rounded
+    across[4 * rows :] = block.astype(BF16)
+    for copy in copies[2:]:
+        copy.wait()
+
+
+def sent_frequencies(across):
+    sent = across[across.shape[0] - 16 :].astype(F32)
+    return [(sent[i : i + 1] + sent[i + 1 : i + 2] + sent[i + 2 : i + 3])[:, :1] for i in (0, 3)]
+
+
+def strip_kernel(half, across, row_half, strip, inner_strip):
+    rows = (across.shape[0] - 16) // 4
+    parity = lax.axis_index("rows") % 2
+    for late, out in ((parity, strip), (1 - parity, inner_strip)):
+        begin = 0
+        for slab, size in ((0, 4 * half), (1, 2 * half)):
+            frm = slab * 2 * rows + late * (2 * rows - size)
+            out[begin : begin + size] = across[pl.ds(pl.multiple_of(frm, 16), size)]
+            begin += size
+
+
+def measured_kernel(measured, sent, outer, inner, sems):
+    size, cols = outer.shape[0], measured.shape[3] // 2
+    parity = lax.axis_index("rows") % 2
+    side = lax.axis_index("ang")
+    copies = []
+    for late, out in ((parity, outer), (1 - parity, inner)):
+        for frm, at, lanes in (((1 - side) * cols, 0, cols), (cols - (1 - side) * LANES, cols, LANES)):
+            here = pl.ds(pl.multiple_of(frm, LANES), lanes)
+            there = measured.at[0, pl.ds(late * size, size), :, here]
+            copies.append(pltpu.make_async_copy(there, out.at[:, :, at : at + lanes], sems.at[len(copies)]))
+    for copy in copies:
+        copy.start()
+    for copy in copies:
+        copy.wait()
+
+
+def own_window(measured, late, at, size):
+    half_rows, cols = measured.shape[1] // 2, measured.shape[3] // 2
+    rows = pl.ds(late * half_rows, half_rows)
+    first, second = (at, cols + at) if at < cols else (cols, cols - LANES)
+    left = measured[0, rows, :, first : first + size].reshape(2 * half_rows, size)
+    right = measured[0, rows, :, second : second + size].reshape(2 * half_rows, size)
+    return jnp.where(lax.axis_index("ang") == 0, left, right)
+
+
+def got_window(window, at, size):
+    return window[:, :, at : at + size].reshape(2 * window.shape[0], size)
+
+
+def skewed(base, count, stride):
+    width = base.shape[1]
+    return pltpu.roll(jnp.broadcast_to(base, (count, width)), 0, 1, stride=stride, stride_axis=0)
+
+
+def matrices_kernel(rows, taps, row_real, row_imag, row_half, row_half_adj, row_adj, col_taps, split_far, split_meas):
+    count = taps.shape[1]
+    half = (count - 1) // 2
+    wide = rows + 4 * half
+    mid = rows + 2 * half
+    table = jnp.concatenate(
+        [jnp.concatenate([taps[...], jnp.zeros((2, LANES - count), BF16)], axis=1),
+         jnp.zeros((14, LANES), BF16)], axis=0,
+    )
+
+    def spread(width, place):
+        tap = iota((LANES, width), 0)
+        lane = iota((LANES, width), 1)
+        hit = jnp.logical_and(lane == place(tap), tap < count)
+        return dot(table, jnp.where(hit, 1.0, 0.0).astype(BF16))
+
+    even = spread(2 * wide, lambda tap: 2 * tap)
+    odd = spread(2 * wide, lambda tap: 2 * tap + 1)
+    row_real[...] = skewed(even[0:1] - odd[1:2], mid, 2)
+    row_imag[...] = skewed(even[1:2] + odd[0:1], mid, 2)
+
+    low = spread(2 * mid, lambda tap: tap)
+    high = spread(2 * mid, lambda tap: mid + tap)
+    full = jnp.concatenate(
+        [skewed(low[0:1] - high[1:2], rows, 1), skewed(low[1:2] + high[0:1], rows, 1)], axis=0
+    )
+    row_adj[...] = full.T.astype(BF16)
+    low = spread(2 * rows, lambda tap: tap)
+    high = spread(2 * rows, lambda tap: rows + tap)
+    full = jnp.concatenate(
+        [skewed(low[0:1] - high[1:2], rows // 2, 1), skewed(low[1:2] + high[0:1], rows // 2, 1)], axis=0
+    )
+    row_half[...] = full.astype(BF16)
+    row_half_adj[...] = full.T.astype(BF16)
+
+    window = 2 * LANES
+    source = iota((window, LANES), 0)
+    target = iota((window, LANES), 1)
+    same_side = (source < LANES) == (target < LANES - half)
+    left_only = source < window - half
+    right_only = source >= LANES - half
+    everything = source >= 0
+    at = 0
+    for adjoint in (False, True):
+        for offset, masks in ((0, (everything, same_side)), (2 * half, (everything, left_only, right_only))):
+            if adjoint:
+                base = spread(window, lambda tap: (window - offset - (count - 1) + tap) % window)
+            else:
+                base = spread(window, lambda tap: (window - offset - tap) % window)
+            re = skewed(base[0:1], window, 1)[:, :LANES]
+            im = skewed(base[1:2], window, 1)[:, :LANES]
+            im = -im if adjoint else im
+            for mask in masks:
+                mre = jnp.where(mask, re, 0.0).astype(BF16)
+                mim = jnp.where(mask, im, 0.0).astype(BF16)
+                col_taps[at, :window, :LANES] = mre
+                col_taps[at, :window, LANES:] = mim
+                col_taps[at, window:, :LANES] = -mim
+                col_taps[at, window:, LANES:] = mre
+                at += 1
+
+    for out in (split_far, split_meas):
+        size = out.shape[0]
+        to, frm = iota((size, size), 0), iota((size, size), 1)
+        out[...] = jnp.where(frm == 2 * (to % (size // 2)) + to // (size // 2), 1.0, 0.0).astype(BF16)
+
+
+def phases_kernel(half, length, row_real, row_imag, across, across_got, row_near, row_near_adj, row_edge, waves):
+    mid, wide = row_real.shape[0], row_real.shape[1] // 2
+    rows, cols = mid - 2 * half, waves.shape[1] - LANES
+    side = lax.axis_index("ang")
+    freqs = list(zip(sent_frequencies(across), sent_frequencies(across_got)))
+    scale = 2.0 * math.pi / length
+    lane = iota((1, cols + LANES), 1)
+    col = jnp.where(side == 0, lane, jnp.where(lane < cols, lane + cols, lane - LANES)).astype(F32)
+    start = lax.axis_index("rows") * rows - 2 * half
+    row = (start + iota((1, 2 * wide), 1) // 2).astype(F32)
+    for member in range(2):
+        phase = scale * (freqs[1][member] * col)
+        waves[2 * member : 2 * member + 1] = jnp.cos(phase)
+        waves[2 * member + 1 : 2 * member + 2] = jnp.sin(phase)
+        phase = scale * (freqs[0][member] * row)
+        cos, sin = jnp.cos(phase), jnp.sin(phase)
+        re = row_real[...] * cos - row_imag[...] * sin
+        im = row_imag[...] * cos + row_real[...] * sin
+        full = jnp.concatenate([re, im], axis=0)
+        at = member * 2 * mid
+        row_near[at : at + 2 * mid] = full.astype(BF16)
+        row_near_adj[:, at : at + 2 * mid] = full.T.astype(BF16)
+        for part in range(2):
+            low, high = 4 * half, 2 * wide - 4 * half
+            near = full[part * mid : part * mid + 2 * half, :low]
+            far = full[part * mid + mid - 2 * half : (part + 1) * mid, high:]
+            edge = jnp.where(lax.axis_index("rows") % 2 == 0, near, far)
+            row_edge[(2 * member + part) * 2 * half : (2 * member + part + 1) * 2 * half] = edge.astype(BF16)
+
+
+class Tiles:
+    def __init__(self, cols):
+        self.count = cols // LANES + 1
+        self.width = self.count * LANES
+        self.cut = self.count - 1 - lax.axis_index("ang")
+        self.after = lax.rem(self.cut + 1, self.count)
+
+    def ahead(self, j, base):
+        return base + jnp.where(j == self.cut, 1, 0) if j >= self.count - 2 else base
+
+    def back(self, j, base):
+        if 0 < j < self.count - 2:
+            return base
+        return base + jnp.where(j == self.cut, 1, jnp.where(j == self.after, 2, 0))
+
+
+def tile(j):
+    return slice(j * LANES, (j + 1) * LANES)
+
+
+def pair(j):
+    return slice(j * LANES, (j + 2) * LANES)
+
+
+class Rows:
+    def __init__(self, first, count, parts):
+        self.first, self.count, self.parts = first, count, parts
+
+    def at(self, part, top=0):
+        first = top + part * self.parts + self.first
+        return pl.ds(first if isinstance(first, int) else pl.multiple_of(first, 16), self.count)
+
+    def read(self, ref, lanes, top=0):
+        return jnp.concatenate([ref[self.at(0, top), lanes], ref[self.at(1, top), lanes]], axis=0)
+
+    def pairs(self, ref, j, top=0):
+        return jnp.concatenate([ref[self.at(0, top), pair(j)], ref[self.at(1, top), pair(j)]], axis=1)
+
+    def write(self, ref, lanes, both, top=0):
+        ref[self.at(0, top), lanes] = both[: self.count]
+        ref[self.at(1, top), lanes] = both[self.count :]
+
+
+def column_step(tiles, index, col_taps, load, store, count, limit=512):
+    groups, room = [], 0
+    for j in range(count):
+        which = index(j)
+        plain = isinstance(which, int)
+        if plain and groups and isinstance(groups[-1][0], int) and room > 0:
+            groups[-1][1].append(j)
+        else:
+            groups.append((which, [j]))
+            room = limit
+        room -= load(j).shape[0] if plain else limit
+    for which, members in groups:
+        parts = [load(j) for j in members]
+        size = parts[0].shape[0]
+        y = dot(jnp.concatenate(parts, axis=0), col_taps[which])
+        for at, j in enumerate(members):
+            store(j, y[at * size : (at + 1) * size])
+
+
+def forward_rows(
+    tiles, part, leave, near_slab, far_slab, row_near, row_half, col_taps, waves, entry, field, after, narrow, leaving,
+):
+    mid, width = part.parts, tiles.width
+    size = part.count
+    for at, lanes in lane_chunks(width):
+        here = slice(at, at + lanes)
+        left = jnp.concatenate(
+            [row_near[part.at(comp, member * 2 * mid), :] for member in range(2) for comp in range(2)], axis=0
+        )
+        result = dot(left, near_slab[:, here])
+        for member in range(2):
+            re = result[2 * member * size : (2 * member + 1) * size]
+            im = result[(2 * member + 1) * size : (2 * member + 2) * size]
+            vr, vi = waves[2 * member : 2 * member + 1, here], waves[2 * member + 1 : 2 * member + 2, here]
+            entry[member, :size, here] = (re * vr - im * vi).astype(BF16)
+            entry[member, size:, here] = (re * vi + im * vr).astype(BF16)
+    entry[:, :, width:] = entry[:, :, :LANES]
+
+    def load(j):
+        return jnp.concatenate(
+            [
+                jnp.concatenate([entry[member, :size, pair(j)], entry[member, size:, pair(j)]], axis=1)
+                for member in range(2)
+            ],
+            axis=0,
+        )
+
+    def store(j, y):
+        y = y.astype(BF16)
+        far = part.read(far_slab, tile(j))
+        sr, si = far[:size], far[size:]
+        for member in range(2):
+            re, im = y[member * size : (member + 1) * size, :LANES], y[member * size : (member + 1) * size, LANES:]
+            part.write(field.at[member], tile(j), jnp.concatenate([re, im], axis=0))
+            re, im = re.astype(F32), im.astype(F32)
+            both = jnp.concatenate([sr * re - si * im, sr * im + si * re], axis=0)
+            part.write(after.at[member], tile(j), both.astype(BF16))
+
+    column_step(tiles, lambda j: tiles.ahead(j, 0), col_taps, load, store, tiles.count)
+
+    source = Rows(leave.first, 2 * leave.count, mid)
+    for at, lanes in lane_chunks(width):
+        here = slice(at, at + lanes)
+        for member in range(2):
+            y = dot(row_half[...], source.read(after.at[member], here)).astype(BF16)
+            narrow[member, :, LANES + at : LANES + at + lanes] = y
+    narrow[:, :, :LANES] = narrow[:, :, width:]
+    size2 = leave.count
+
+    def load2(j):
+        return jnp.concatenate(
+            [
+                jnp.concatenate([narrow[member, :size2, pair(j)], narrow[member, size2:, pair(j)]], axis=1)
+                for member in range(2)
+            ],
+            axis=0,
+        )
+
+    def store2(j, y):
+        y = y.astype(BF16)
+        for member in range(2):
+            here = slice(member * size2, (member + 1) * size2)
+            leaving[member, :size2, tile(j)] = y[here, :LANES]
+            leaving[member, size2:, tile(j)] = y[here, LANES:]
+
+    column_step(tiles, lambda j: tiles.back(j, 2), col_taps, load2, store2, tiles.count)
+
+
+def residue_rows(tiles, members, windows, leave, split_meas, col_taps, leaving, residue, back):
+    size = leave.count
+    for member, window in zip(members, windows):
+        for at, lanes in lane_chunks(tiles.width):
+            here = slice(at, at + lanes)
+            meas = dot(split_meas[...], window(at, lanes))
+            residue[member, :, here] = (leaving[member, :, here].astype(F32) - meas).astype(BF16)
+        residue[member, :, tiles.width :] = residue[member, :, :LANES]
+
+    def load(j):
+        return jnp.concatenate(
+            [
+                jnp.concatenate([residue[member, :size, pair(j)], residue[member, size:, pair(j)]], axis=1)
+                for member in members
+            ],
+            axis=0,
+        )
+
+    def store(j, y):
+        y = y.astype(BF16)
+        for k, member in enumerate(members):
+            here = slice(k * size, (k + 1) * size)
+            leave.write(back.at[member], tile(j), jnp.concatenate([y[here, :LANES], y[here, LANES:]], axis=0))
+
+    column_step(tiles, lambda j: tiles.ahead(j, 5), col_taps, load, store, tiles.count)
+
+
+def backward_rows(tiles, members, part, left, right, field, far_slab, col_taps, waves, carry, far_sum, into):
+    size, mid = part.count, part.parts
+    for at, lanes in lane_chunks(tiles.width):
+        here = slice(at, at + lanes)
+        there = slice(LANES + at, LANES + at + lanes)
+        far = part.read(far_slab, here)
+        sr, si = far[:size], far[size:]
+        total = None
+        for member in members:
+            y = dot(left, right(member, here))
+            br, bi = y[:size], y[size:]
+            inner = part.read(field.at[member], here).astype(F32)
+            ir, ii = inner[:size], inner[size:]
+            carry[member, :size, there] = (sr * br + si * bi).astype(BF16)
+            carry[member, size:, there] = (sr * bi - si * br).astype(BF16)
+            term = jnp.concatenate([ir * br + ii * bi, ir * bi - ii * br], axis=0)
+            total = term if total is None else total + term
+        part.write(far_sum, there, total)
+    for member in members:
+        carry[member, :, :LANES] = carry[member, :, tiles.width :]
+
+    def load(j):
+        return jnp.concatenate(
+            [
+                jnp.concatenate([carry[member, :size, pair(j)], carry[member, size:, pair(j)]], axis=1)
+                for member in members
+            ],
+            axis=0,
+        )
+
+    def store(j, y):
+        for k, member in enumerate(members):
+            re, im = y[k * size : (k + 1) * size, :LANES], y[k * size : (k + 1) * size, LANES:]
+            vr, vi = waves[2 * member : 2 * member + 1, tile(j)], waves[2 * member + 1 : 2 * member + 2, tile(j)]
+            both = jnp.concatenate([re * vr + im * vi, im * vr - re * vi], axis=0)
+            part.write(into, tile(j), both.astype(BF16), member * 2 * mid)
+
+    column_step(tiles, lambda j: tiles.back(j, 7), col_taps, load, store, tiles.count - 1)
+
+
+def split_rows(tiles, part, split_far, far_raw, far_slab, half):
+    left = jnp.concatenate([split_far[part.at(0), :], split_far[part.at(1), :]], axis=0)
+    for j in range(tiles.count):
+        part.write(far_slab, tile(j), dot(left, far_raw[:, pair(j)])[:, half : half + LANES])
+
+
+def far_margin(tiles, half, part, far_sum, sums):
+    for j in range(tiles.count - 1):
+        y = part.read(far_sum, pair(j))[:, LANES - half : 2 * LANES - half]
+        sums[:, tile(j)] = y.astype(BF16)
+
+
+def outer_kernel(
+    half,
+    slices, outer, inner, across, corner, across_inner, measured, measured_got,
+    row_near, row_half, row_half_adj, row_edge, col_taps, split_far, split_meas, waves,
+    near_slab, far_raw, far_slab, field, after, back, far_sum, into, sums,
+    entry, narrow, leaving, residue, carry,
+):
+    rows, cols = slices.shape[1], slices.shape[3]
+    tiles = Tiles(cols)
+    width = tiles.width
+    mid = rows + 2 * half
+    parity = lax.axis_index("rows") % 2
+
+    for slab, ref, margin in ((0, near_slab, 4 * half), (1, far_raw, 2 * half)):
+        ref[margin : margin + 2 * rows, :cols] = slices[slab].reshape(2 * rows, cols)
+        ref[margin : margin + 2 * rows, cols:width] = across[slab * 2 * rows : (slab + 1) * 2 * rows]
+        begin = 0 if slab == 0 else 4 * half
+        outer_at = pl.ds(pl.multiple_of(parity * (2 * rows + margin), 16), margin)
+        inner_at = pl.ds(pl.multiple_of((1 - parity) * (2 * rows + margin), 16), margin)
+        ref[outer_at, :cols] = outer[begin // 2 : (begin + margin) // 2].reshape(margin, cols)
+        ref[outer_at, cols:width] = corner[begin : begin + margin]
+        ref[inner_at, :cols] = inner[begin // 2 : (begin + margin) // 2].reshape(margin, cols)
+        ref[inner_at, cols:width] = across_inner[begin : begin + margin]
+    far_raw[:, width:] = far_raw[:, :LANES]
+
+    part = Rows(parity * (rows // 2), rows, mid)
+    source = Rows(parity * (rows // 2), rows // 2, mid)
+    leave = Rows(parity * (rows // 2), rows // 2, rows)
+    edge = Rows(parity * rows, 2 * half, mid)
+    pick = Rows(parity * 2 * half, 2 * half, rows)
+    split_rows(tiles, part, split_far, far_raw, far_slab, half)
+    forward_rows(
+        tiles, part, source, near_slab, far_slab, row_near, row_half, col_taps, waves, entry, field, after, narrow,
+        leaving,
+    )
+    windows = (functools.partial(own_window, measured, parity), functools.partial(got_window, measured_got))
+    residue_rows(tiles, (0, 1), windows, leave, split_meas, col_taps, leaving, residue, back)
+    backward_rows(
+        tiles, (0, 1), edge, pick.read(row_half_adj, slice(None)), lambda one, here: leave.read(back.at[one], here),
+        field, far_slab, col_taps, waves, carry, far_sum, into,
+    )
+    far_sum[:, :LANES] = far_sum[:, width:]
+    left = row_edge[...].T
+    for at, size in lane_chunks(cols):
+        here = slice(at, at + size)
+        right = jnp.concatenate([edge.read(into, here, member * 2 * mid) for member in range(2)], axis=0)
+        sums[: 4 * half, here] = dot(left, right).astype(BF16)
+    far_margin(tiles, half, Rows(parity * (rows + half), half, mid), far_sum, sums.at[4 * half :])
+
+
+def inner_kernel(
+    half,
+    near_slab, far_raw, measured, measured_got, far_slab_in, field_in, after_in, back_in, far_in, into_in,
+    row_near, row_half, row_adj, row_near_adj, col_taps, split_far, split_meas, waves,
+    far_slab, field, after, back, far_sum, into, sums, far_sums,
+    entry, narrow, leaving, residue, carry,
+):
+    cols = into.shape[1]
+    tiles = Tiles(cols)
+    mid = far_sum.shape[0] // 2
+    rows = mid - 2 * half
+    other = 1 - lax.axis_index("rows") % 2
+    part = Rows(other * rows, 2 * half, mid)
+    source = Rows(other * (rows // 2), rows // 2, mid)
+    leave = Rows(other * (rows // 2), rows // 2, rows)
+    split_rows(tiles, part, split_far, far_raw, far_slab, half)
+    forward_rows(
+        tiles, part, source, near_slab, far_slab, row_near, row_half, col_taps, waves, entry, field, after, narrow,
+        leaving,
+    )
+    windows = (functools.partial(own_window, measured, other), functools.partial(got_window, measured_got))
+    residue_rows(tiles, (0, 1), windows, leave, split_meas, col_taps, leaving, residue, back)
+    rest = Rows(other * 2 * half, rows, mid)
+    left = jnp.concatenate([row_adj[rest.at(0), :], row_adj[rest.at(1), :]], axis=0)
+    backward_rows(
+        tiles, (0, 1), rest, left, lambda one, here: back[one, :, here], field, far_slab, col_taps, waves, carry,
+        far_sum, into,
+    )
+    far_sum[:, :LANES] = far_sum[:, tiles.width :]
+    at = pl.ds(pl.multiple_of(other * 2 * (rows + 2 * half), 16), 4 * half)
+    for first, size in lane_chunks(cols):
+        here = slice(first, first + size)
+        sums[:, here] = dot(row_near_adj[at, :], into[:, here]).astype(BF16)
+    far_margin(tiles, half, Rows(other * (rows + half), half, mid), far_sum, far_sums)
+
+
+def sums_kernel(
+    half, into, far_sum, row_near_adj, inner, inner_far, near, far, near_edge, far_edge, near_total, far_total, sems
+):
+    cols = into.shape[1]
+    mid = far_sum.shape[0] // 2
+    rows = mid - 2 * half
+    parity = lax.axis_index("rows") % 2
+    margin = 4 * half
+    for j in range(cols // LANES):
+        for comp in range(2):
+            top = comp * mid + half
+            far_total[:, comp, tile(j)] = far_sum[top : top + rows, pair(j)][:, LANES - half : 2 * LANES - half]
+    at = pl.ds((1 - parity) * (rows - half), half)
+    for comp in range(2):
+        far_total[at, comp, :] += inner_far[comp * half : (comp + 1) * half].astype(F32)
+    far_edge[...] = far_total[pl.ds(parity * (rows - half), half)]
+    rest = pl.ds((1 - parity) * half, rows - half)
+    far_copy = pltpu.make_async_copy(far_total.at[rest], far.at[rest], sems.at[0])
+    far_copy.start()
+    for at, size in lane_chunks(cols):
+        here = slice(at, at + size)
+        y = dot(row_near_adj[margin : margin + 2 * rows], into[:, here])
+        near_total[:, :, here] = y.reshape(rows, 2, size)
+    at = pl.ds((1 - parity) * (rows - 2 * half), 2 * half)
+    near_total[at] += inner[...].astype(F32).reshape(2 * half, 2, cols)
+    near_edge[...] = near_total[pl.ds(parity * (rows - 2 * half), 2 * half)]
+    rest = pl.ds((1 - parity) * 2 * half, rows - 2 * half)
+    near_copy = pltpu.make_async_copy(near_total.at[rest], near.at[rest], sems.at[1])
+    near_copy.start()
+    far_copy.wait()
+    near_copy.wait()
+
+
+def finish_kernel(half, near_in, far_in, near_edge, far_edge, outer, near, far, near_total, far_total, sems):
+    rows, cols = near.shape[0], near.shape[2]
+    parity = lax.axis_index("rows") % 2
+    margin = 4 * half
+    near_total[...] = near_edge[...] + outer[:margin].astype(F32).reshape(2 * half, 2, cols)
+    at = pl.ds(parity * (rows - 2 * half), 2 * half)
+    near_copy = pltpu.make_async_copy(near_total, near.at[at], sems.at[0])
+    near_copy.start()
+    for comp in range(2):
+        got = outer[margin + comp * half : margin + (comp + 1) * half].astype(F32)
+        far_total[:, comp, :] = far_edge[:, comp, :] + got
+    at = pl.ds(parity * (rows - half), half)
+    far_copy = pltpu.make_async_copy(far_total, far.at[at], sems.at[1])
+    far_copy.start()
+    near_copy.wait()
+    far_copy.wait()
+
+
+def call(kernel, outs, operands, hbm=(), scalars=(), outside=(), outs_outside=(), scratch=(), aliases=None, flops=0):
+    def place(i):
+        if i in scalars:
+            return pltpu.SMEM
+        return pltpu.HBM if i in hbm else pl.ANY if i in outside else pltpu.VMEM
+
+    return pl.pallas_call(
+        kernel,
+        out_shape=[jax.ShapeDtypeStruct(shape, dtype) for shape, dtype in outs],
+        in_specs=[pl.BlockSpec(memory_space=place(i)) for i in range(len(operands))],
+        out_specs=[
+            pl.BlockSpec(memory_space=pl.ANY if i in outs_outside else pltpu.VMEM) for i in range(len(outs))
+        ],
+        scratch_shapes=[one if not isinstance(one, tuple) else pltpu.VMEM(*one) for one in scratch],
+        input_output_aliases=aliases or {},
+        compiler_params=pltpu.CompilerParams(vmem_limit_bytes=20 * 2**20),
+        cost_estimate=pl.CostEstimate(flops=flops, bytes_accessed=0, transcendentals=0),
+    )(*(pltpu.with_memory_space_constraint(x, pltpu.HBM) if i in hbm else x for i, x in enumerate(operands)))
+
+
+def columns_local(measured, slices, kernel_taps, angle_freq, chosen):
+    rows, cols = slices.shape[1], slices.shape[3]
+    length = measured.shape[3]
+    half = (kernel_taps.shape[1] - 1) // 2
+    wide, mid, width = rows + 4 * half, rows + 2 * half, cols + LANES
+    count = lax.axis_size("rows")
+    outer_pairs = [(i, j) for i in range(count) if 0 <= (j := i - 1 + 2 * (i % 2)) < count]
+    inner_pairs = [(i, i + 1 - 2 * (i % 2)) for i in range(count)]
+    side_pairs = [(i, 1 - i) for i in range(lax.axis_size("ang"))]
+    edge = 6 * half
+    outer, inner, across = call(
+        functools.partial(edges_kernel, half),
+        [((3 * half, 2, cols), BF16), ((3 * half, 2, cols), BF16), ((4 * rows + 16, LANES), BF16)],
+        (slices, angle_freq.T, chosen), hbm=(0, 1), scalars=(2,), outs_outside=(0, 1),
+        scratch=[((2, rows, 2, LANES), BF16), (angle_freq.shape[::-1], F32), pltpu.SemaphoreType.DMA((6,))],
+    )
+    outer_got = lax.ppermute(outer, "rows", outer_pairs)
+    across_got = lax.ppermute(across, "ang", side_pairs)
+    inner_got = lax.ppermute(inner, "rows", inner_pairs)
+    meas_outer, meas_inner = call(
+        measured_kernel, [((rows // 2, 2, width), BF16)] * 2, (measured, across), hbm=(0,), outside=(1,),
+        outs_outside=(0, 1), scratch=[pltpu.SemaphoreType.DMA((4,))],
+    )
+    outer_meas = lax.ppermute(meas_outer, "ang", side_pairs)
+    inner_meas = lax.ppermute(meas_inner, "ang", side_pairs)
+    row_real, row_imag, row_half, row_half_adj, row_adj, col_taps, split_far, split_meas = call(
+        functools.partial(matrices_kernel, rows),
+        [
+            ((mid, 2 * wide), F32), ((mid, 2 * wide), F32), ((rows, 2 * rows), BF16), ((2 * rows, rows), BF16),
+            ((2 * mid, 2 * rows), BF16), ((10, 4 * LANES, 2 * LANES), BF16), ((2 * mid, 2 * mid), BF16),
+            ((rows, rows), BF16),
+        ],
+        (kernel_taps,), flops=MATS_FLOPS,
+    )
+    strip, inner_strip = call(
+        functools.partial(strip_kernel, half), [((edge, LANES), BF16)] * 2, (across_got, row_half), outside=(1,),
+        flops=STRIP_FLOPS,
+    )
+    corner_got = lax.ppermute(strip, "rows", outer_pairs)
+    across_inner = lax.ppermute(inner_strip, "rows", inner_pairs)
+    row_near, row_near_adj, row_edge, waves = call(
+        functools.partial(phases_kernel, half, length),
+        [((4 * mid, 2 * wide), BF16), ((2 * wide, 4 * mid), BF16), ((8 * half, 4 * half), BF16), ((8, width), F32)],
+        (row_real, row_imag, across, across_got),
+    )
+    state = [
+        ((2 * mid, width), F32), ((2, 2 * mid, width), BF16), ((2, 2 * mid, width), BF16),
+        ((2, 2 * rows, width), BF16), ((2 * mid, width + LANES), F32), ((4 * mid, cols), BF16),
+    ]
+    leaving_shape = ((2, rows, width), BF16)
+    near_slab, far_raw, far_slab, field, after, back, far_sum, into, outer_sums = call(
+        functools.partial(outer_kernel, half),
+        [((2 * wide, width), BF16), ((2 * mid, width + LANES), BF16), *state, ((edge, cols), BF16)],
+        (
+            slices, outer_got, inner_got, across_got, corner_got, across_inner, measured, outer_meas,
+            row_near, row_half, row_half_adj, row_edge, col_taps, split_far, split_meas, waves,
+        ),
+        scratch=[
+            ((2, 2 * rows, width + LANES), BF16), ((2, rows, width + LANES), BF16), leaving_shape,
+            ((2, rows, width + LANES), BF16), ((2, 4 * half, width + LANES), BF16),
+        ],
+        flops=OWN_FLOPS,
+    )
+    outer_back = lax.ppermute(outer_sums, "rows", outer_pairs)
+    far_slab, field, after, back, far_sum, into, inner_sums, inner_far = call(
+        functools.partial(inner_kernel, half),
+        [*state, ((4 * half, cols), BF16), ((2 * half, cols), BF16)],
+        (
+            near_slab, far_raw, measured, inner_meas, far_slab, field, after, back, far_sum, into,
+            row_near, row_half, row_adj, row_near_adj, col_taps, split_far, split_meas, waves,
+        ),
+        aliases={4: 0, 5: 1, 6: 2, 7: 3, 8: 4, 9: 5},
+        scratch=[
+            ((2, 4 * half, width + LANES), BF16), ((2, rows, width + LANES), BF16), leaving_shape,
+            ((2, rows, width + LANES), BF16), ((2, 2 * rows, width + LANES), BF16),
+        ],
+        flops=INNER_FLOPS,
+    )
+    inner_back = lax.ppermute(inner_sums, "rows", inner_pairs)
+    inner_far_back = lax.ppermute(inner_far, "rows", inner_pairs)
+    near, far, near_edge, far_edge = call(
+        functools.partial(sums_kernel, half),
+        [
+            ((rows, 2, cols), F32), ((rows, 2, cols), F32), ((2 * half, 2, cols), F32), ((half, 2, cols), F32),
+        ],
+        (into, far_sum, row_near_adj, inner_back, inner_far_back), outs_outside=(0, 1),
+        scratch=[((rows, 2, cols), F32), ((rows, 2, cols), F32), pltpu.SemaphoreType.DMA((2,))],
+    )
+    near, far = call(
+        functools.partial(finish_kernel, half),
+        [((rows, 2, cols), F32)] * 2,
+        (near, far, near_edge, far_edge, outer_back), outside=(0, 1), outs_outside=(0, 1), aliases={0: 0, 1: 1},
+        scratch=[((2 * half, 2, cols), F32), ((half, 2, cols), F32), pltpu.SemaphoreType.DMA((2,))],
+    )
+    return near, far
 
 
 def with_halo(block, sides, width):
@@ -141,9 +806,24 @@
     return (near_total, far_total)
 
 
+def pick(measured, slices, kernel_taps, angle_freq, chosen):
+    rows, cols = slices.shape[1], slices.shape[3]
+    taps = kernel_taps.shape[1]
+    fits = (
+        lax.axis_size("ang") == 2
+        and lax.axis_size("rows") % 2 == 0
+        and 2 * (taps - 1) == LANES
+        and rows >= taps - 1
+        and rows % LANES == 0
+        and cols % (2 * LANES) == 0
+    )
+    run = columns_local if fits else local
+    return run(measured, slices, kernel_taps, angle_freq, chosen)
+
+
 def solution(mesh):
     return jax.shard_map(
-        local,
+        pick,
         mesh=mesh,
         in_specs=(P("ang", "rows", None, None), P(None, "rows", None, "ang"), P(), P(), P("ang")),
         out_specs=(P("rows", None, "ang"), P("rows", None, "ang")),

time: 198 us -> 41.6 us (0.21)
  the two profiles are of different devices: /device:TPU:17 before, /device:TPU:0 now
where the time goes in v3:
time: 41.6 us; the launch traced here: 41.3 us
  Pallas kernels  19.1 us (46%)
  starting transfers between devices  17.4 us (42%)
  waiting for transfers between devices  3.26 us (8%)
  between operations  1.58 us (4%)
    pallas_call x9, Pallas kernels, call(): pl.pallas_call(kernel, out_shape=[jax.ShapeDtypeStruct(shape, dtype) for...  19.1 us
    ppermute x1, starting transfers between devices, columns_local(): inner_got = lax.ppermute(inner, 'rows', inner_pairs)  4.37 us
    ppermute x1, starting transfers between devices, columns_local(): inner_back = lax.ppermute(inner_sums, 'rows', inner_pairs)  3.62 us
    ppermute x1, starting transfers between devices, columns_local(): across_inner = lax.ppermute(inner_strip, 'rows', inner_pairs)  2.96 us
    ppermute x1, starting transfers between devices, columns_local(): inner_meas = lax.ppermute(meas_inner, 'ang', side_pairs)  1.97 us
    ppermute x1, waiting for transfers between devices, columns_local(): across_got = lax.ppermute(across, 'ang', side_pairs)  1.93 us
    ppermute x1, starting transfers between devices, columns_local(): across_got = lax.ppermute(across, 'ang', side_pairs)  1.49 us
    ppermute x1, waiting for transfers between devices, columns_local(): inner_far_back = lax.ppermute(inner_far, 'rows', inner_pairs)  1.27 us
  transfers between devices with their start and end apart: 10, of which 2 were waited for; matrix products, arithmetic and copies ran while one was open for 0% of the time, Pallas kernels for 41%

profile of v3, /device:TPU:0, one launch (start us, length us, event | category | flops | bytes accessed | tf_op | source)
XLA Modules:
  0.0 41.3 jit_solution(2490344107702045113)
XLA Ops:
  0.6 0.0 copy-start.2
  1.3 1.3 %shard_map.68 = (bf16[96,2,1024]{2,1,0:T(2,128)(2,1)S(1)}, bf16[96,2,1024]{2,1,0:T(2,128)(2,1)S(1)}, bf16[528,128]{1,0:T(8,128)(2,1)S(1)}) custom-call(bf16[2,128,2,1024]{3,2,1,0:T(2,128)(2,1)} %slices.3, f32[2,128]{1,0:T(2,128)} %bitcast.1, s32[1]{0:T(128)S(6)} %copy.23.chosen), custom_call_target="tpu_custom_call" | custom-call | tf_op jit(solution)/shard_map/pallas_call | solution.py:563
  2.6 0.7 %collective-permute-start = (bf16[96,2,1024]{2,1,0:T(2,128)(2,1)S(1)}, bf16[96,2,1024]{2,1,0:T(2,128)(2,1)S(1)}, u32[]{:S(2)}, u32[]{:S(2)}) collective-permute-start(bf16[96,2,1024]{2,1,0:T(2,128)(2,1)S(1)} %get-tuple-element.38), channel_id=1, source_target_pairs={{2,4},{4,2},{6,8},{8,6},{10,12},{12,10},{14,16},{16,14},{18,20},{2... | collective-permute-start | bytes 1179656 | tf_op jit(solution)/shard_map/ppermute | solution.py:593
  3.3 4.4 %collective-permute-start.1 = (bf16[96,2,1024]{2,1,0:T(2,128)(2,1)S(1)}, bf16[96,2,1024]{2,1,0:T(2,128)(2,1)S(1)}, u32[]{:S(2)}, u32[]{:S(2)}) collective-permute-start(bf16[96,2,1024]{2,1,0:T(2,128)(2,1)S(1)} %get-tuple-element.39), channel_id=1, source_target_pairs={{0,2},{2,0},{4,6},{6,4},{8,10},{10,8},{12,14},{14,12},{16,18},{18,... | collective-permute-start | bytes 1179656 | tf_op jit(solution)/shard_map/ppermute | solution.py:595
  7.6 1.5 %collective-permute-start.2 = (bf16[528,128]{1,0:T(8,128)(2,1)S(1)}, bf16[528,128]{1,0:T(8,128)(2,1)S(1)}, u32[]{:S(2)}, u32[]{:S(2)}) collective-permute-start(bf16[528,128]{1,0:T(8,128)(2,1)S(1)} %get-tuple-element.40.sent.across), channel_id=1, source_target_pairs={{0,1},{1,0},{2,3},{3,2},{4,5},{5,4},{6,7},{7,6},{8,9},{9,8},{10,11... | collective-permute-start | bytes 405512 | tf_op jit(solution)/shard_map/ppermute | solution.py:594
  9.1 1.1 %shard_map.71 = (bf16[64,2,1152]{2,1,0:T(2,128)(2,1)S(1)}, bf16[64,2,1152]{2,1,0:T(2,128)(2,1)S(1)}) custom-call(bf16[1,128,2,2048]{3,2,1,0:T(2,128)(2,1)} %measured.5, bf16[528,128]{1,0:T(8,128)(2,1)S(1)} %get-tuple-element.40.sent.across), custom_call_target="tpu_custom_call" | custom-call | tf_op jit(solution)/shard_map/pallas_call | solution.py:563
  10.2 0.6 %collective-permute-start.5 = (bf16[64,2,1152]{2,1,0:T(2,128)(2,1)S(1)}, bf16[64,2,1152]{2,1,0:T(2,128)(2,1)S(1)}, u32[]{:S(2)}, u32[]{:S(2)}) collective-permute-start(bf16[64,2,1152]{2,1,0:T(2,128)(2,1)S(1)} %get-tuple-element.44), channel_id=1, source_target_pairs={{0,1},{1,0},{2,3},{3,2},{4,5},{5,4},{6,7},{7,6},{8,9},{9,8},{10,11... | collective-permute-start | bytes 884744 | tf_op jit(solution)/shard_map/ppermute | solution.py:600
  10.8 0.0 copy-done.2
  10.8 0.9 %shard_map.69 = (f32[192,512]{1,0:T(8,128)S(1)}, f32[192,512]{1,0:T(8,128)S(1)}, bf16[128,256]{1,0:T(8,128)(2,1)S(1)}, bf16[256,128]{1,0:T(8,128)(2,1)S(1)}, bf1...) custom-call(bf16[2,65]{1,0:T(2,128)(2,1)S(1)} %copy-done.2), custom_call_target="tpu_custom_call" | custom-call | tf_op jit(solution)/shard_map/pallas_call | solution.py:563
  11.7 1.9 %collective-permute-done.2.across.across_got = bf16[528,128]{1,0:T(8,128)(2,1)S(1)} collective-permute-done((bf16[528,128]{1,0:T(8,128)(2,1)S(1)}, bf16[528,128]{1,0:T(8,128)(2,1)S(1)}, u32[]{:S(2)}, u32[]{:S(2)}) %collective-permute-start.2) | collective-permute-done | bytes 135200 | tf_op jit(solution)/shard_map/ppermute | solution.py:594
  13.7 0.0 copy-start
  13.7 0.0 copy-start.1
  13.7 0.8 %collective-permute-start.3 = (bf16[192,128]{1,0:T(8,128)(2,1)S(1)}, bf16[192,128]{1,0:T(8,128)(2,1)S(1)}, u32[]{:S(2)}, u32[]{:S(2)}) collective-permute-start(bf16[192,128]{1,0:T(8,128)(2,1)S(1)} %get-tuple-element.42), channel_id=1, source_target_pairs={{2,4},{4,2},{6,8},{8,6},{10,12},{12,10},{14,16},{16,14},{18,20},{2... | collective-permute-start | bytes 147464 | tf_op jit(solution)/shard_map/ppermute | solution.py:615
  14.5 2.0 %collective-permute-start.6 = (bf16[64,2,1152]{2,1,0:T(2,128)(2,1)S(1)}, bf16[64,2,1152]{2,1,0:T(2,128)(2,1)S(1)}, u32[]{:S(2)}, u32[]{:S(2)}) collective-permute-start(bf16[64,2,1152]{2,1,0:T(2,128)(2,1)S(1)} %get-tuple-element.56), channel_id=1, source_target_pairs={{0,1},{1,0},{2,3},{3,2},{4,5},{5,4},{6,7},{7,6},{8,9},{9,8},{10,11... | collective-permute-start | bytes 884744 | tf_op jit(solution)/shard_map/ppermute | solution.py:601
  16.5 0.0 collective-permute-done.3.corner
  16.5 3.0 %collective-permute-start.4 = (bf16[192,128]{1,0:T(8,128)(2,1)S(1)}, bf16[192,128]{1,0:T(8,128)(2,1)S(1)}, u32[]{:S(2)}, u32[]{:S(2)}) collective-permute-start(bf16[192,128]{1,0:T(8,128)(2,1)S(1)} %get-tuple-element.43), channel_id=1, source_target_pairs={{0,2},{2,0},{4,6},{6,4},{8,10},{10,8},{12,14},{14,12},{16,18},{18,... | collective-permute-start | bytes 147464 | tf_op jit(solution)/shard_map/ppermute | solution.py:616
  19.4 0.8 %shard_map.72 = (bf16[768,512]{1,0:T(8,128)(2,1)S(1)}, bf16[512,768]{1,0:T(8,128)(2,1)S(1)}, bf16[256,128]{1,0:T(8,128)(2,1)S(1)}, f32[8,1152]{1,0:T(8,128)S(1)}) custom-call(f32[192,512]{1,0:T(8,128)S(1)} %get-tuple-element.45.row_real, f32[192,512]{1,0:T(8,128)S(1)} %get-tuple-element.46.row_imag, bf16[528,128]{1,0:T(8,128)(2,1)S(1)} %get-tuple-element.40.sent.across, ...), custom_call_target="tpu_custom_call" | custom-call | tf_op jit(solution)/shard_map/pallas_call | solution.py:563
  20.3 0.0 collective-permute-done.4.across_inner
  20.3 0.0 collective-permute-done.5.measured_got
  20.3 0.0 collective-permute-done.outer
  20.3 0.0 collective-permute-done.1.inner
  20.3 0.0 copy-done
  20.3 0.0 copy-done.1
  20.3 4.9 %shard_map.73 = (bf16[512,1152]{1,0:T(8,128)(2,1)S(1)}, bf16[384,1280]{1,0:T(8,128)(2,1)S(1)}, f32[384,1152]{1,0:T(8,128)S(1)}, bf16[2,384,1152]{2,1,0:T(8,128)(...) custom-call(bf16[2,128,2,1024]{3,2,1,0:T(2,128)(2,1)S(1)} %copy-done, ...), custom_call_target="tpu_custom_call" | custom-call | flops 1000000000 | tf_op jit(solution)/shard_map/pallas_call | solution.py:563
  25.2 0.9 %collective-permute-start.9 = (bf16[192,1024]{1,0:T(8,128)(2,1)S(1)}, bf16[192,1024]{1,0:T(8,128)(2,1)S(1)}, u32[]{:S(2)}, u32[]{:S(2)}) collective-permute-start(bf16[192,1024]{1,0:T(8,128)(2,1)S(1)} %get-tuple-element.73), channel_id=1, source_target_pairs={{2,4},{4,2},{6,8},{8,6},{10,12},{12,10},{14,16},{16,14},{18,20},{2... | collective-permute-start | bytes 1179656 | tf_op jit(solution)/shard_map/ppermute | solution.py:640
  26.1 0.0 collective-permute-done.6.measured_got
  26.1 5.3 %shard_map.74 = (f32[384,1152]{1,0:T(8,128)S(1)}, bf16[2,384,1152]{2,1,0:T(8,128)(2,1)S(1)}, bf16[2,384,1152]{2,1,0:T(8,128)(2,1)S(1)}, bf16[2,256,1152]{2,1,0:T...) custom-call(bf16[512,1152]{1,0:T(8,128)(2,1)S(1)} %get-tuple-element, ...), custom_call_target="tpu_custom_call", output_to_operand_aliasing={{0}: (4, {}), {1}: (5, {}), {2}: (6, {}), {3}: (7, {}), {4}... | custom-call | tf_op jit(solution)/shard_map/pallas_call | solution.py:563
  31.4 3.6 %collective-permute-start.7 = (bf16[128,1024]{1,0:T(8,128)(2,1)S(1)}, bf16[128,1024]{1,0:T(8,128)(2,1)S(1)}, u32[]{:S(2)}, u32[]{:S(2)}) collective-permute-start(bf16[128,1024]{1,0:T(8,128)(2,1)S(1)} %get-tuple-element.67), channel_id=1, source_target_pairs={{0,2},{2,0},{4,6},{6,4},{8,10},{10,8},{12,14},{14,12},{16,18},{18,... | collective-permute-start | bytes 786440 | tf_op jit(solution)/shard_map/ppermute | solution.py:655
  35.0 0.1 collective-permute-start.8
  35.1 1.3 %collective-permute-done.8.inner_far = bf16[64,1024]{1,0:T(8,128)(2,1)S(1)} collective-permute-done((bf16[64,1024]{1,0:T(8,128)(2,1)S(1)}, bf16[64,1024]{1,0:T(8,128)(2,1)S(1)}, u32[]{:S(2)}, u32[]{:S(2)}) %collective-permute-start.8) | collective-permute-done | bytes 131104 | tf_op jit(solution)/shard_map/ppermute | solution.py:656
  36.3 0.0 collective-permute-done.7.inner
  36.3 3.8 %shard_map.75 = (f32[128,2,1024]{2,1,0:T(2,128)}, f32[128,2,1024]{2,1,0:T(2,128)}, f32[64,2,1024]{2,1,0:T(2,128)S(1)}, f32[32,2,1024]{2,1,0:T(2,128)S(1)}) custom-call(bf16[768,1024]{1,0:T(8,128)(2,1)S(1)} %get-tuple-element.65.into, f32[384,1280]{1,0:T(8,128)S(1)} %get-tuple-element.66.far_sum, bf16[512,768]{1,0:T(8,128)(2,1)S(1)} %get-tuple-element.64.row_near_adj, ...), custom_call_target="tpu_custom_call" | custom-call | tf_op jit(solution)/shard_map/pallas_call | solution.py:563
  40.2 0.0 collective-permute-done.9.outer
  40.2 1.0 %shard_map.76 = (f32[128,2,1024]{2,1,0:T(2,128)}, f32[128,2,1024]{2,1,0:T(2,128)}) custom-call(f32[128,2,1024]{2,1,0:T(2,128)} %get-tuple-element.69.near_in, f32[128,2,1024]{2,1,0:T(2,128)} %get-tuple-element.70.far_in, f32[64,2,1024]{2,1,0:T(2,128)S(1)} %get-tuple-element.71.near_edge, ...), custom_call_target="tpu_custom_call", output_to_operand_aliasing={{0}: (0, {}), {1}: (1, {})} | custom-call | tf_op jit(solution)/shard_map/pallas_call | solution.py:563
  (1 shorter events, 0.0 us)
Async XLA Ops:
  0.6 10.2 %copy-start.2 = (bf16[2,65]{1,0:T(2,128)(2,1)S(1)}, bf16[2,65]{1,0:T(2,128)(2,1)}, u32[]{:S(2)}) copy-start(bf16[2,65]{1,0:T(2,128)(2,1)} %taps.1) | copy-start | bytes 784
  2.6 17.7 %collective-permute-start = (bf16[96,2,1024]{2,1,0:T(2,128)(2,1)S(1)}, bf16[96,2,1024]{2,1,0:T(2,128)(2,1)S(1)}, u32[]{:S(2)}, u32[]{:S(2)}) collective-permute-start(bf16[96,2,1024]{2,1,0:T(2,128)(2,1)S(1)} %get-tuple-element.38), channel_id=1, source_target_pairs={{2,4},{4,2},{6,8},{8,6},{10,12},{12,10},{14,16},{16,14},{18,20},{2... | collective-permute-start | bytes 1179656 | tf_op jit(solution)/shard_map/ppermute | solution.py:593
  3.3 17.0 %collective-permute-start.1 = (bf16[96,2,1024]{2,1,0:T(2,128)(2,1)S(1)}, bf16[96,2,1024]{2,1,0:T(2,128)(2,1)S(1)}, u32[]{:S(2)}, u32[]{:S(2)}) collective-permute-start(bf16[96,2,1024]{2,1,0:T(2,128)(2,1)S(1)} %get-tuple-element.39), channel_id=1, source_target_pairs={{0,2},{2,0},{4,6},{6,4},{8,10},{10,8},{12,14},{14,12},{16,18},{18,... | collective-permute-start | bytes 1179656 | tf_op jit(solution)/shard_map/ppermute | solution.py:595
  7.6 6.0 %collective-permute-start.2 = (bf16[528,128]{1,0:T(8,128)(2,1)S(1)}, bf16[528,128]{1,0:T(8,128)(2,1)S(1)}, u32[]{:S(2)}, u32[]{:S(2)}) collective-permute-start(bf16[528,128]{1,0:T(8,128)(2,1)S(1)} %get-tuple-element.40.sent.across), channel_id=1, source_target_pairs={{0,1},{1,0},{2,3},{3,2},{4,5},{5,4},{6,7},{7,6},{8,9},{9,8},{10,11... | collective-permute-start | bytes 405512 | tf_op jit(solution)/shard_map/ppermute | solution.py:594
  10.2 10.1 %collective-permute-start.5 = (bf16[64,2,1152]{2,1,0:T(2,128)(2,1)S(1)}, bf16[64,2,1152]{2,1,0:T(2,128)(2,1)S(1)}, u32[]{:S(2)}, u32[]{:S(2)}) collective-permute-start(bf16[64,2,1152]{2,1,0:T(2,128)(2,1)S(1)} %get-tuple-element.44), channel_id=1, source_target_pairs={{0,1},{1,0},{2,3},{3,2},{4,5},{5,4},{6,7},{7,6},{8,9},{9,8},{10,11... | collective-permute-start | bytes 884744 | tf_op jit(solution)/shard_map/ppermute | solution.py:600
  13.7 6.6 %copy-start = (bf16[1,128,2,2048]{3,2,1,0:T(2,128)(2,1)S(1)}, bf16[1,128,2,2048]{3,2,1,0:T(2,128)(2,1)}, u32[]{:S(2)}) copy-start(bf16[1,128,2,2048]{3,2,1,0:T(2,128)(2,1)} %measured.5) | copy-start | bytes 3145732
  13.7 6.7 %copy-start.1 = (bf16[2,128,2,1024]{3,2,1,0:T(2,128)(2,1)S(1)}, bf16[2,128,2,1024]{3,2,1,0:T(2,128)(2,1)}, u32[]{:S(2)}) copy-start(bf16[2,128,2,1024]{3,2,1,0:T(2,128)(2,1)} %slices.3) | copy-start | bytes 3145732
  13.7 2.8 %collective-permute-start.3 = (bf16[192,128]{1,0:T(8,128)(2,1)S(1)}, bf16[192,128]{1,0:T(8,128)(2,1)S(1)}, u32[]{:S(2)}, u32[]{:S(2)}) collective-permute-start(bf16[192,128]{1,0:T(8,128)(2,1)S(1)} %get-tuple-element.42), channel_id=1, source_target_pairs={{2,4},{4,2},{6,8},{8,6},{10,12},{12,10},{14,16},{16,14},{18,20},{2... | collective-permute-start | bytes 147464 | tf_op jit(solution)/shard_map/ppermute | solution.py:615
  14.5 11.6 %collective-permute-start.6 = (bf16[64,2,1152]{2,1,0:T(2,128)(2,1)S(1)}, bf16[64,2,1152]{2,1,0:T(2,128)(2,1)S(1)}, u32[]{:S(2)}, u32[]{:S(2)}) collective-permute-start(bf16[64,2,1152]{2,1,0:T(2,128)(2,1)S(1)} %get-tuple-element.56), channel_id=1, source_target_pairs={{0,1},{1,0},{2,3},{3,2},{4,5},{5,4},{6,7},{7,6},{8,9},{9,8},{10,11... | collective-permute-start | bytes 884744 | tf_op jit(solution)/shard_map/ppermute | solution.py:601
  16.5 3.8 %collective-permute-start.4 = (bf16[192,128]{1,0:T(8,128)(2,1)S(1)}, bf16[192,128]{1,0:T(8,128)(2,1)S(1)}, u32[]{:S(2)}, u32[]{:S(2)}) collective-permute-start(bf16[192,128]{1,0:T(8,128)(2,1)S(1)} %get-tuple-element.43), channel_id=1, source_target_pairs={{0,2},{2,0},{4,6},{6,4},{8,10},{10,8},{12,14},{14,12},{16,18},{18,... | collective-permute-start | bytes 147464 | tf_op jit(solution)/shard_map/ppermute | solution.py:616
  25.2 15.0 %collective-permute-start.9 = (bf16[192,1024]{1,0:T(8,128)(2,1)S(1)}, bf16[192,1024]{1,0:T(8,128)(2,1)S(1)}, u32[]{:S(2)}, u32[]{:S(2)}) collective-permute-start(bf16[192,1024]{1,0:T(8,128)(2,1)S(1)} %get-tuple-element.73), channel_id=1, source_target_pairs={{2,4},{4,2},{6,8},{8,6},{10,12},{12,10},{14,16},{16,14},{18,20},{2... | collective-permute-start | bytes 1179656 | tf_op jit(solution)/shard_map/ppermute | solution.py:640
  31.4 5.0 %collective-permute-start.7 = (bf16[128,1024]{1,0:T(8,128)(2,1)S(1)}, bf16[128,1024]{1,0:T(8,128)(2,1)S(1)}, u32[]{:S(2)}, u32[]{:S(2)}) collective-permute-start(bf16[128,1024]{1,0:T(8,128)(2,1)S(1)} %get-tuple-element.67), channel_id=1, source_target_pairs={{0,2},{2,0},{4,6},{6,4},{8,10},{10,8},{12,14},{14,12},{16,18},{18,... | collective-permute-start | bytes 786440 | tf_op jit(solution)/shard_map/ppermute | solution.py:655
  35.0 1.3 %collective-permute-start.8 = (bf16[64,1024]{1,0:T(8,128)(2,1)S(1)}, bf16[64,1024]{1,0:T(8,128)(2,1)S(1)}, u32[]{:S(2)}, u32[]{:S(2)}) collective-permute-start(bf16[64,1024]{1,0:T(8,128)(2,1)S(1)} %get-tuple-element.68), channel_id=1, source_target_pairs={{0,2},{2,0},{4,6},{6,4},{8,10},{10,8},{12,14},{14,12},{16,18},{18,... | collective-permute-start | bytes 393224 | tf_op jit(solution)/shard_map/ppermute | solution.py:656

commit v4 on v3

--- a/solution.py
+++ b/solution.py
@@ -10,10 +10,10 @@
 
 LANES = 128
 BF16 = jnp.bfloat16
-STRIP_FLOPS = 1 * 10**9
+STRIP_FLOPS = 17 * 10**8
 INNER_FLOPS = 0
 MATS_FLOPS = 0
-OWN_FLOPS = 1 * 10**9
+OWN_FLOPS = 5 * 10**9
 F32 = jnp.float32
 
 
@@ -29,15 +29,14 @@
     return [(at, min(step, width - at)) for at in range(0, width, step)]
 
 
-def edges_kernel(half, slices, angle_freq, chosen, outer, inner, across, strips, table, sems):
+def edges_kernel(half, slices, angle_freq, chosen, outer, across, strips, table, sems):
     rows, cols = slices.shape[1], slices.shape[3]
     parity = lax.axis_index("rows") % 2
     side = lax.axis_index("ang")
     lane = pl.multiple_of((1 - side) * (cols - LANES), LANES)
     copies = [(angle_freq, table), (slices.at[:, :, :, pl.ds(lane, LANES)], strips)]
-    for late, out in ((parity, outer), (1 - parity, inner)):
-        for slab, at, size in ((0, 0, 2 * half), (1, 2 * half, half)):
-            copies.append((slices.at[slab, pl.ds(late * (rows - size), size)], out.at[pl.ds(at, size)]))
+    for slab, at, size in ((0, 0, 2 * half), (1, 2 * half, half)):
+        copies.append((slices.at[slab, pl.ds(parity * (rows - size), size)], outer.at[pl.ds(at, size)]))
     copies = [pltpu.make_async_copy(frm, to, sems.at[i]) for i, (frm, to) in enumerate(copies)]
     for copy in copies:
         copy.start()
@@ -65,15 +64,26 @@
     return [(sent[i : i + 1] + sent[i + 1 : i + 2] + sent[i + 2 : i + 3])[:, :1] for i in (0, 3)]
 
 
-def strip_kernel(half, across, row_half, strip, inner_strip):
+def strip_kernel(half, across, row_half, strip):
     rows = (across.shape[0] - 16) // 4
     parity = lax.axis_index("rows") % 2
-    for late, out in ((parity, strip), (1 - parity, inner_strip)):
-        begin = 0
-        for slab, size in ((0, 4 * half), (1, 2 * half)):
-            frm = slab * 2 * rows + late * (2 * rows - size)
-            out[begin : begin + size] = across[pl.ds(pl.multiple_of(frm, 16), size)]
-            begin += size
+    begin = 0
+    for slab, size in ((0, 4 * half), (1, 2 * half)):
+        frm = slab * 2 * rows + parity * (2 * rows - size)
+        strip[begin : begin + size] = across[pl.ds(pl.multiple_of(frm, 16), size)]
+        begin += size
+
+
+def inner_edge_kernel(half, slices, across, strip, edge):
+    rows, cols = slices.shape[1], slices.shape[3]
+    other = 1 - lax.axis_index("rows") % 2
+    begin = 0
+    for slab, size in ((0, 2 * half), (1, half)):
+        there = slice(begin, begin + 2 * size)
+        edge[there, :cols] = slices[slab, pl.ds(other * (rows - size), size)].reshape(2 * size, cols)
+        frm = slab * 2 * rows + other * 2 * (rows - size)
+        edge[there, cols:] = across[pl.ds(pl.multiple_of(frm, 16), 2 * size)]
+        begin += 2 * size
 
 
 def measured_kernel(measured, sent, outer, inner, sems):
@@ -110,7 +120,11 @@
     return pltpu.roll(jnp.broadcast_to(base, (count, width)), 0, 1, stride=stride, stride_axis=0)
 
 
-def matrices_kernel(rows, taps, row_real, row_imag, row_half, row_half_adj, row_adj, col_taps, split_far, split_meas):
+def matrices_kernel(
+    rows, length, taps, across,
+    row_real, row_imag, row_half, row_half_adj, row_adj, col_taps, split_far, split_meas,
+    row_near, row_near_adj, row_edge, waves,
+):
     count = taps.shape[1]
     half = (count - 1) // 2
     wide = rows + 4 * half
@@ -130,6 +144,8 @@
     odd = spread(2 * wide, lambda tap: 2 * tap + 1)
     row_real[...] = skewed(even[0:1] - odd[1:2], mid, 2)
     row_imag[...] = skewed(even[1:2] + odd[0:1], mid, 2)
+
+    add_phases(half, length, 0, across, row_real, row_imag, row_near, row_near_adj, row_edge, waves)
 
     low = spread(2 * mid, lambda tap: tap)
     high = spread(2 * mid, lambda tap: mid + tap)
@@ -177,34 +193,40 @@
         out[...] = jnp.where(frm == 2 * (to % (size // 2)) + to // (size // 2), 1.0, 0.0).astype(BF16)
 
 
-def phases_kernel(half, length, row_real, row_imag, across, across_got, row_near, row_near_adj, row_edge, waves):
+def add_phases(half, length, member, sent, row_real, row_imag, row_near, row_near_adj, row_edge, waves):
     mid, wide = row_real.shape[0], row_real.shape[1] // 2
     rows, cols = mid - 2 * half, waves.shape[1] - LANES
     side = lax.axis_index("ang")
-    freqs = list(zip(sent_frequencies(across), sent_frequencies(across_got)))
+    freq_row, freq_col = sent_frequencies(sent)
     scale = 2.0 * math.pi / length
     lane = iota((1, cols + LANES), 1)
     col = jnp.where(side == 0, lane, jnp.where(lane < cols, lane + cols, lane - LANES)).astype(F32)
+    phase = scale * (freq_col * col)
+    waves[2 * member : 2 * member + 1] = jnp.cos(phase)
+    waves[2 * member + 1 : 2 * member + 2] = jnp.sin(phase)
     start = lax.axis_index("rows") * rows - 2 * half
     row = (start + iota((1, 2 * wide), 1) // 2).astype(F32)
-    for member in range(2):
-        phase = scale * (freqs[1][member] * col)
-        waves[2 * member : 2 * member + 1] = jnp.cos(phase)
-        waves[2 * member + 1 : 2 * member + 2] = jnp.sin(phase)
-        phase = scale * (freqs[0][member] * row)
-        cos, sin = jnp.cos(phase), jnp.sin(phase)
-        re = row_real[...] * cos - row_imag[...] * sin
-        im = row_imag[...] * cos + row_real[...] * sin
-        full = jnp.concatenate([re, im], axis=0)
-        at = member * 2 * mid
-        row_near[at : at + 2 * mid] = full.astype(BF16)
-        row_near_adj[:, at : at + 2 * mid] = full.T.astype(BF16)
-        for part in range(2):
-            low, high = 4 * half, 2 * wide - 4 * half
-            near = full[part * mid : part * mid + 2 * half, :low]
-            far = full[part * mid + mid - 2 * half : (part + 1) * mid, high:]
-            edge = jnp.where(lax.axis_index("rows") % 2 == 0, near, far)
-            row_edge[(2 * member + part) * 2 * half : (2 * member + part + 1) * 2 * half] = edge.astype(BF16)
+    phase = scale * (freq_row * row)
+    cos, sin = jnp.cos(phase), jnp.sin(phase)
+    re = row_real[...] * cos - row_imag[...] * sin
+    im = row_imag[...] * cos + row_real[...] * sin
+    full = jnp.concatenate([re, im], axis=0)
+    at = member * 2 * mid
+    row_near[at : at + 2 * mid] = full.astype(BF16)
+    row_near_adj[:, at : at + 2 * mid] = full.T.astype(BF16)
+    for part in range(2):
+        low, high = 4 * half, 2 * wide - 4 * half
+        near = full[part * mid : part * mid + 2 * half, :low]
+        far = full[part * mid + mid - 2 * half : (part + 1) * mid, high:]
+        edge = jnp.where(lax.axis_index("rows") % 2 == 0, near, far)
+        row_edge[(2 * member + part) * 2 * half : (2 * member + part + 1) * 2 * half] = edge.astype(BF16)
+
+
+def phases_kernel(
+    half, length, row_real, row_imag, across, near_in, near_adj_in, edge_in, waves_in,
+    row_near, row_near_adj, row_edge, waves,
+):
+    add_phases(half, length, 1, across, row_real, row_imag, row_near, row_near_adj, row_edge, waves)
 
 
 class Tiles:
@@ -270,14 +292,14 @@
 
 
 def forward_rows(
-    tiles, part, leave, near_slab, far_slab, row_near, row_half, col_taps, waves, entry, field, after, narrow, leaving,
+    tiles, part, leave, near_slab, near_lanes, far_slab, row_near, row_half, col_taps, waves, entry, field, after, narrow, leaving,
 ):
     mid, width = part.parts, tiles.width
     size = part.count
     for at, lanes in lane_chunks(width):
         here = slice(at, at + lanes)
         left = jnp.concatenate(
-            [row_near[part.at(comp, member * 2 * mid), :] for member in range(2) for comp in range(2)], axis=0
+            [row_near[part.at(comp, member * 2 * mid), near_lanes] for member in range(2) for comp in range(2)], axis=0
         )
         result = dot(left, near_slab[:, here])
         for member in range(2):
@@ -405,10 +427,9 @@
     column_step(tiles, lambda j: tiles.back(j, 7), col_taps, load, store, tiles.count - 1)
 
 
-def split_rows(tiles, part, split_far, far_raw, far_slab, half):
-    left = jnp.concatenate([split_far[part.at(0), :], split_far[part.at(1), :]], axis=0)
+def split_rows(tiles, part, split, far_raw, far_slab, half):
     for j in range(tiles.count):
-        part.write(far_slab, tile(j), dot(left, far_raw[:, pair(j)])[:, half : half + LANES])
+        part.write(far_slab, tile(j), dot(split[...], far_raw[:, pair(j)])[:, half : half + LANES])
 
 
 def far_margin(tiles, half, part, far_sum, sums):
@@ -419,10 +440,10 @@
 
 def outer_kernel(
     half,
-    slices, outer, inner, across, corner, across_inner, measured, measured_got,
+    slices, outer, across, corner, measured, measured_got,
     row_near, row_half, row_half_adj, row_edge, col_taps, split_far, split_meas, waves,
-    near_slab, far_raw, far_slab, field, after, back, far_sum, into, sums,
-    entry, narrow, leaving, residue, carry,
+    far_slab, field, after, back, far_sum, into, sums,
+    near_raw, far_raw, entry, narrow, leaving, residue, carry,
 ):
     rows, cols = slices.shape[1], slices.shape[3]
     tiles = Tiles(cols)
@@ -430,16 +451,16 @@
     mid = rows + 2 * half
     parity = lax.axis_index("rows") % 2
 
-    for slab, ref, margin in ((0, near_slab, 4 * half), (1, far_raw, 2 * half)):
-        ref[margin : margin + 2 * rows, :cols] = slices[slab].reshape(2 * rows, cols)
-        ref[margin : margin + 2 * rows, cols:width] = across[slab * 2 * rows : (slab + 1) * 2 * rows]
+    for slab, ref, margin in ((0, near_raw, 4 * half), (1, far_raw, 2 * half)):
+        own = ref.shape[0] - margin
         begin = 0 if slab == 0 else 4 * half
-        outer_at = pl.ds(pl.multiple_of(parity * (2 * rows + margin), 16), margin)
-        inner_at = pl.ds(pl.multiple_of((1 - parity) * (2 * rows + margin), 16), margin)
-        ref[outer_at, :cols] = outer[begin // 2 : (begin + margin) // 2].reshape(margin, cols)
-        ref[outer_at, cols:width] = corner[begin : begin + margin]
-        ref[inner_at, :cols] = inner[begin // 2 : (begin + margin) // 2].reshape(margin, cols)
-        ref[inner_at, cols:width] = across_inner[begin : begin + margin]
+        first = parity * (rows - own // 2)
+        at = pl.ds(pl.multiple_of((1 - parity) * margin, 16), own)
+        ref[at, :cols] = slices[slab, pl.ds(first, own // 2)].reshape(own, cols)
+        ref[at, cols:width] = across[pl.ds(pl.multiple_of(slab * 2 * rows + 2 * first, 16), own)]
+        at = pl.ds(pl.multiple_of(parity * own, 16), margin)
+        ref[at, :cols] = outer[begin // 2 : (begin + margin) // 2].reshape(margin, cols)
+        ref[at, cols:width] = corner[begin : begin + margin]
     far_raw[:, width:] = far_raw[:, :LANES]
 
     part = Rows(parity * (rows // 2), rows, mid)
@@ -448,9 +469,10 @@
     edge = Rows(parity * rows, 2 * half, mid)
     pick = Rows(parity * 2 * half, 2 * half, rows)
     split_rows(tiles, part, split_far, far_raw, far_slab, half)
+    lanes = pl.ds(pl.multiple_of(parity * 4 * half, LANES), near_raw.shape[0])
     forward_rows(
-        tiles, part, source, near_slab, far_slab, row_near, row_half, col_taps, waves, entry, field, after, narrow,
-        leaving,
+        tiles, part, source, near_raw, lanes, far_slab, row_near, row_half, col_taps, waves, entry, field, after,
+        narrow, leaving,
     )
     windows = (functools.partial(own_window, measured, parity), functools.partial(got_window, measured_got))
     residue_rows(tiles, (0, 1), windows, leave, split_meas, col_taps, leaving, residue, back)
@@ -469,10 +491,10 @@
 
 def inner_kernel(
     half,
-    near_slab, far_raw, measured, measured_got, far_slab_in, field_in, after_in, back_in, far_in, into_in,
-    row_near, row_half, row_adj, row_near_adj, col_taps, split_far, split_meas, waves,
+    slices, inner, across, measured, measured_got, far_slab_in, field_in, after_in, back_in, far_in, into_in,
+    row_near, row_half, row_adj, row_near_adj, col_taps, split_meas, waves,
     far_slab, field, after, back, far_sum, into, sums, far_sums,
-    entry, narrow, leaving, residue, carry,
+    near_raw, far_raw, entry, narrow, leaving, residue, carry,
 ):
     cols = into.shape[1]
     tiles = Tiles(cols)
@@ -482,10 +504,22 @@
     part = Rows(other * rows, 2 * half, mid)
     source = Rows(other * (rows // 2), rows // 2, mid)
     leave = Rows(other * (rows // 2), rows // 2, rows)
-    split_rows(tiles, part, split_far, far_raw, far_slab, half)
+
+    for slab, ref, margin in ((0, near_raw, 4 * half), (1, far_raw, 2 * half)):
+        own = ref.shape[0] - margin
+        begin = 0 if slab == 0 else 4 * half
+        first = other * (rows - own // 2)
+        at = pl.ds(pl.multiple_of((1 - other) * margin, 16), own)
+        ref[at, :cols] = slices[slab, pl.ds(first, own // 2)].reshape(own, cols)
+        ref[at, cols : tiles.width] = across[pl.ds(pl.multiple_of(slab * 2 * rows + 2 * first, 16), own)]
+        ref[pl.ds(pl.multiple_of(other * own, 16), margin), : tiles.width] = inner[begin : begin + margin]
+    far_raw[:, tiles.width :] = far_raw[:, :LANES]
+
+    split_rows(tiles, part, split_meas, far_raw, far_slab, half)
+    lanes = pl.ds(pl.multiple_of(other * 2 * rows, LANES), near_raw.shape[0])
     forward_rows(
-        tiles, part, source, near_slab, far_slab, row_near, row_half, col_taps, waves, entry, field, after, narrow,
-        leaving,
+        tiles, part, source, near_raw, lanes, far_slab, row_near, row_half, col_taps, waves, entry, field, after,
+        narrow, leaving,
     )
     windows = (functools.partial(own_window, measured, other), functools.partial(got_window, measured_got))
     residue_rows(tiles, (0, 1), windows, leave, split_meas, col_taps, leaving, residue, back)
@@ -503,52 +537,51 @@
     far_margin(tiles, half, Rows(other * (rows + half), half, mid), far_sum, far_sums)
 
 
-def sums_kernel(
-    half, into, far_sum, row_near_adj, inner, inner_far, near, far, near_edge, far_edge, near_total, far_total, sems
-):
+def sums_kernel(half, into, far_sum, row_near_adj, near, far):
     cols = into.shape[1]
     mid = far_sum.shape[0] // 2
     rows = mid - 2 * half
-    parity = lax.axis_index("rows") % 2
     margin = 4 * half
+    for at, size in lane_chunks(cols):
+        here = slice(at, at + size)
+        near[:, here] = dot(row_near_adj[margin : margin + 2 * rows], into[:, here])
     for j in range(cols // LANES):
         for comp in range(2):
             top = comp * mid + half
-            far_total[:, comp, tile(j)] = far_sum[top : top + rows, pair(j)][:, LANES - half : 2 * LANES - half]
-    at = pl.ds((1 - parity) * (rows - half), half)
+            far[comp, :, tile(j)] = far_sum[top : top + rows, pair(j)][:, LANES - half : 2 * LANES - half]
+
+
+def inner_sums_kernel(half, near_sum, far_sum, inner, inner_far, near, far, near_rows, far_rows, sems):
+    rows, cols = near.shape[0], near.shape[2]
+    other = 1 - lax.axis_index("rows") % 2
+    at = pl.ds(pl.multiple_of(other * (2 * rows - 4 * half), 16), 4 * half)
+    near_rows[...] = (near_sum[at] + inner[...].astype(F32)).reshape(2 * half, 2, cols)
+    near_copy = pltpu.make_async_copy(near_rows, near.at[pl.ds(other * (rows - 2 * half), 2 * half)], sems.at[0])
+    near_copy.start()
+    at = pl.ds(pl.multiple_of(other * (rows - half), 16), half)
     for comp in range(2):
-        far_total[at, comp, :] += inner_far[comp * half : (comp + 1) * half].astype(F32)
-    far_edge[...] = far_total[pl.ds(parity * (rows - half), half)]
-    rest = pl.ds((1 - parity) * half, rows - half)
-    far_copy = pltpu.make_async_copy(far_total.at[rest], far.at[rest], sems.at[0])
+        far_rows[pl.ds((1 - other) * half, rows - 2 * half), comp, :] = far_sum[comp, half : rows - half]
+        added = far_sum[comp, at] + inner_far[comp * half : (comp + 1) * half].astype(F32)
+        far_rows[pl.ds(other * (rows - 2 * half), half), comp, :] = added
+    far_copy = pltpu.make_async_copy(far_rows, far.at[pl.ds(other * half, rows - half)], sems.at[1])
     far_copy.start()
-    for at, size in lane_chunks(cols):
-        here = slice(at, at + size)
-        y = dot(row_near_adj[margin : margin + 2 * rows], into[:, here])
-        near_total[:, :, here] = y.reshape(rows, 2, size)
-    at = pl.ds((1 - parity) * (rows - 2 * half), 2 * half)
-    near_total[at] += inner[...].astype(F32).reshape(2 * half, 2, cols)
-    near_edge[...] = near_total[pl.ds(parity * (rows - 2 * half), 2 * half)]
-    rest = pl.ds((1 - parity) * 2 * half, rows - 2 * half)
-    near_copy = pltpu.make_async_copy(near_total.at[rest], near.at[rest], sems.at[1])
-    near_copy.start()
+    near_copy.wait()
     far_copy.wait()
-    near_copy.wait()
-
-
-def finish_kernel(half, near_in, far_in, near_edge, far_edge, outer, near, far, near_total, far_total, sems):
+
+
+def finish_kernel(half, near_in, far_in, near_sum, far_sum, outer, near, far, near_rows, far_rows, sems):
     rows, cols = near.shape[0], near.shape[2]
     parity = lax.axis_index("rows") % 2
     margin = 4 * half
-    near_total[...] = near_edge[...] + outer[:margin].astype(F32).reshape(2 * half, 2, cols)
-    at = pl.ds(parity * (rows - 2 * half), 2 * half)
-    near_copy = pltpu.make_async_copy(near_total, near.at[at], sems.at[0])
+    at = pl.ds(pl.multiple_of(parity * (2 * rows - margin), 16), margin)
+    near_rows[...] = (near_sum[at] + outer[:margin].astype(F32)).reshape(2 * half, 2, cols)
+    near_copy = pltpu.make_async_copy(near_rows, near.at[pl.ds(parity * (rows - 2 * half), 2 * half)], sems.at[0])
     near_copy.start()
+    at = pl.ds(pl.multiple_of(parity * (rows - half), 16), half)
     for comp in range(2):
         got = outer[margin + comp * half : margin + (comp + 1) * half].astype(F32)
-        far_total[:, comp, :] = far_edge[:, comp, :] + got
-    at = pl.ds(parity * (rows - half), half)
-    far_copy = pltpu.make_async_copy(far_total, far.at[at], sems.at[1])
+        far_rows[:, comp, :] = far_sum[comp, at] + got
+    far_copy = pltpu.make_async_copy(far_rows, far.at[pl.ds(parity * (rows - half), half)], sems.at[1])
     far_copy.start()
     near_copy.wait()
     far_copy.wait()
@@ -584,54 +617,59 @@
     inner_pairs = [(i, i + 1 - 2 * (i % 2)) for i in range(count)]
     side_pairs = [(i, 1 - i) for i in range(lax.axis_size("ang"))]
     edge = 6 * half
-    outer, inner, across = call(
+    outer, across = call(
         functools.partial(edges_kernel, half),
-        [((3 * half, 2, cols), BF16), ((3 * half, 2, cols), BF16), ((4 * rows + 16, LANES), BF16)],
-        (slices, angle_freq.T, chosen), hbm=(0, 1), scalars=(2,), outs_outside=(0, 1),
-        scratch=[((2, rows, 2, LANES), BF16), (angle_freq.shape[::-1], F32), pltpu.SemaphoreType.DMA((6,))],
+        [((3 * half, 2, cols), BF16), ((4 * rows + 16, LANES), BF16)],
+        (slices, angle_freq.T, chosen), hbm=(0, 1), scalars=(2,), outs_outside=(0,),
+        scratch=[((2, rows, 2, LANES), BF16), (angle_freq.shape[::-1], F32), pltpu.SemaphoreType.DMA((4,))],
     )
     outer_got = lax.ppermute(outer, "rows", outer_pairs)
     across_got = lax.ppermute(across, "ang", side_pairs)
-    inner_got = lax.ppermute(inner, "rows", inner_pairs)
     meas_outer, meas_inner = call(
         measured_kernel, [((rows // 2, 2, width), BF16)] * 2, (measured, across), hbm=(0,), outside=(1,),
         outs_outside=(0, 1), scratch=[pltpu.SemaphoreType.DMA((4,))],
     )
     outer_meas = lax.ppermute(meas_outer, "ang", side_pairs)
     inner_meas = lax.ppermute(meas_inner, "ang", side_pairs)
-    row_real, row_imag, row_half, row_half_adj, row_adj, col_taps, split_far, split_meas = call(
-        functools.partial(matrices_kernel, rows),
+    phased = [
+        ((4 * mid, 2 * wide), BF16), ((2 * wide, 4 * mid), BF16), ((8 * half, 4 * half), BF16), ((8, width), F32),
+    ]
+    row_real, row_imag, row_half, row_half_adj, row_adj, col_taps, split_far, split_meas, *partial = call(
+        functools.partial(matrices_kernel, rows, length),
         [
             ((mid, 2 * wide), F32), ((mid, 2 * wide), F32), ((rows, 2 * rows), BF16), ((2 * rows, rows), BF16),
-            ((2 * mid, 2 * rows), BF16), ((10, 4 * LANES, 2 * LANES), BF16), ((2 * mid, 2 * mid), BF16),
-            ((rows, rows), BF16),
+            ((2 * mid, 2 * rows), BF16), ((10, 4 * LANES, 2 * LANES), BF16), ((2 * rows, 2 * rows), BF16),
+            ((rows, rows), BF16), *phased,
         ],
-        (kernel_taps,), flops=MATS_FLOPS,
-    )
-    strip, inner_strip = call(
-        functools.partial(strip_kernel, half), [((edge, LANES), BF16)] * 2, (across_got, row_half), outside=(1,),
+        (kernel_taps, across), flops=MATS_FLOPS,
+    )
+    (strip,) = call(
+        functools.partial(strip_kernel, half), [((edge, LANES), BF16)], (across_got, row_half), outside=(1,),
         flops=STRIP_FLOPS,
     )
     corner_got = lax.ppermute(strip, "rows", outer_pairs)
-    across_inner = lax.ppermute(inner_strip, "rows", inner_pairs)
+    (inner,) = call(
+        functools.partial(inner_edge_kernel, half), [((edge, width), BF16)], (slices, across_got, strip), outside=(2,),
+    )
+    inner_got = lax.ppermute(inner, "rows", inner_pairs)
     row_near, row_near_adj, row_edge, waves = call(
-        functools.partial(phases_kernel, half, length),
-        [((4 * mid, 2 * wide), BF16), ((2 * wide, 4 * mid), BF16), ((8 * half, 4 * half), BF16), ((8, width), F32)],
-        (row_real, row_imag, across, across_got),
+        functools.partial(phases_kernel, half, length), phased, (row_real, row_imag, across_got, *partial),
+        aliases={3: 0, 4: 1, 5: 2, 6: 3},
     )
     state = [
         ((2 * mid, width), F32), ((2, 2 * mid, width), BF16), ((2, 2 * mid, width), BF16),
         ((2, 2 * rows, width), BF16), ((2 * mid, width + LANES), F32), ((4 * mid, cols), BF16),
     ]
     leaving_shape = ((2, rows, width), BF16)
-    near_slab, far_raw, far_slab, field, after, back, far_sum, into, outer_sums = call(
+    far_slab, field, after, back, far_sum, into, outer_sums = call(
         functools.partial(outer_kernel, half),
-        [((2 * wide, width), BF16), ((2 * mid, width + LANES), BF16), *state, ((edge, cols), BF16)],
+        [*state, ((edge, cols), BF16)],
         (
-            slices, outer_got, inner_got, across_got, corner_got, across_inner, measured, outer_meas,
+            slices, outer_got, across_got, corner_got, measured, outer_meas,
             row_near, row_half, row_half_adj, row_edge, col_taps, split_far, split_meas, waves,
         ),
         scratch=[
+            ((2 * rows + 4 * half, width), BF16), ((2 * rows, width + LANES), BF16),
             ((2, 2 * rows, width + LANES), BF16), ((2, rows, width + LANES), BF16), leaving_shape,
             ((2, rows, width + LANES), BF16), ((2, 4 * half, width + LANES), BF16),
         ],
@@ -642,11 +680,12 @@
         functools.partial(inner_kernel, half),
         [*state, ((4 * half, cols), BF16), ((2 * half, cols), BF16)],
         (
-            near_slab, far_raw, measured, inner_meas, far_slab, field, after, back, far_sum, into,
-            row_near, row_half, row_adj, row_near_adj, col_taps, split_far, split_meas, waves,
+            slices, inner_got, across_got, measured, inner_meas, far_slab, field, after, back, far_sum, into,
+            row_near, row_half, row_adj, row_near_adj, col_taps, split_meas, waves,
         ),
-        aliases={4: 0, 5: 1, 6: 2, 7: 3, 8: 4, 9: 5},
+        aliases={5: 0, 6: 1, 7: 2, 8: 3, 9: 4, 10: 5},
         scratch=[
+            ((rows + 4 * half, width), BF16), ((4 * half, width + LANES), BF16),
             ((2, 4 * half, width + LANES), BF16), ((2, rows, width + LANES), BF16), leaving_shape,
             ((2, rows, width + LANES), BF16), ((2, 2 * rows, width + LANES), BF16),
         ],
@@ -654,18 +693,18 @@
     )
     inner_back = lax.ppermute(inner_sums, "rows", inner_pairs)
     inner_far_back = lax.ppermute(inner_far, "rows", inner_pairs)
-    near, far, near_edge, far_edge = call(
-        functools.partial(sums_kernel, half),
-        [
-            ((rows, 2, cols), F32), ((rows, 2, cols), F32), ((2 * half, 2, cols), F32), ((half, 2, cols), F32),
-        ],
-        (into, far_sum, row_near_adj, inner_back, inner_far_back), outs_outside=(0, 1),
-        scratch=[((rows, 2, cols), F32), ((rows, 2, cols), F32), pltpu.SemaphoreType.DMA((2,))],
+    near_sum, far_own = call(
+        functools.partial(sums_kernel, half), [((2 * rows, cols), F32), ((2, rows, cols), F32)],
+        (into, far_sum, row_near_adj),
     )
     near, far = call(
-        functools.partial(finish_kernel, half),
-        [((rows, 2, cols), F32)] * 2,
-        (near, far, near_edge, far_edge, outer_back), outside=(0, 1), outs_outside=(0, 1), aliases={0: 0, 1: 1},
+        functools.partial(inner_sums_kernel, half), [((rows, 2, cols), F32)] * 2,
+        (near_sum, far_own, inner_back, inner_far_back), outs_outside=(0, 1),
+        scratch=[((2 * half, 2, cols), F32), ((rows - half, 2, cols), F32), pltpu.SemaphoreType.DMA((2,))],
+    )
+    near, far = call(
+        functools.partial(finish_kernel, half), [((rows, 2, cols), F32)] * 2,
+        (near, far, near_sum, far_own, outer_back), outside=(0, 1), outs_outside=(0, 1), aliases={0: 0, 1: 1},
         scratch=[((2 * half, 2, cols), F32), ((half, 2, cols), F32), pltpu.SemaphoreType.DMA((2,))],
     )
     return near, far

time: 41.6 us -> 37.4 us (0.90)
  the two profiles are of different devices: /device:TPU:0 before, /device:TPU:17 now
where the time goes in v4:
time: 37.4 us; the launch traced here: 37.1 us
  Pallas kernels  16.4 us (44%)
  starting transfers between devices  14.4 us (39%)
  waiting for transfers between devices  4.71 us (13%)
  between operations  1.58 us (4%)
    pallas_call x11, Pallas kernels, call(): pl.pallas_call(kernel, out_shape=[jax.ShapeDtypeStruct(shape, dtype) for...  16.4 us
    ppermute x1, starting transfers between devices, columns_local(): outer_got = lax.ppermute(outer, 'rows', outer_pairs)  3.71 us
    ppermute x1, starting transfers between devices, columns_local(): outer_back = lax.ppermute(outer_sums, 'rows', outer_pairs)  3.26 us
    ppermute x1, starting transfers between devices, columns_local(): corner_got = lax.ppermute(strip, 'rows', outer_pairs)  2.47 us
    ppermute x1, waiting for transfers between devices, columns_local(): outer_back = lax.ppermute(outer_sums, 'rows', outer_pairs)  1.98 us
    ppermute x1, waiting for transfers between devices, columns_local(): across_got = lax.ppermute(across, 'ang', side_pairs)  1.71 us
    ppermute x1, starting transfers between devices, columns_local(): inner_got = lax.ppermute(inner, 'rows', inner_pairs)  1.55 us
    ppermute x1, starting transfers between devices, columns_local(): across_got = lax.ppermute(across, 'ang', side_pairs)  1.28 us
  transfers between devices with their start and end apart: 9, of which 4 were waited for; matrix products, arithmetic and copies ran while one was open for 0% of the time, Pallas kernels for 39%

profile of v4, /device:TPU:17, one launch (start us, length us, event | category | flops | bytes accessed | tf_op | source)
XLA Modules:
  0.0 37.1 jit_solution(3972485844630237065)
XLA Ops:
  0.6 0.0 copy-start.2
  1.3 1.1 %shard_map.68 = (bf16[96,2,1024]{2,1,0:T(2,128)(2,1)S(1)}, bf16[528,128]{1,0:T(8,128)(2,1)S(1)}) custom-call(bf16[2,128,2,1024]{3,2,1,0:T(2,128)(2,1)} %slices.7, f32[2,128]{1,0:T(2,128)} %bitcast.1, s32[1]{0:T(128)S(6)} %copy.31.chosen), custom_call_target="tpu_custom_call" | custom-call | tf_op jit(solution)/shard_map/pallas_call | solution.py:596
  2.4 3.7 %collective-permute-start.3 = (bf16[96,2,1024]{2,1,0:T(2,128)(2,1)S(1)}, bf16[96,2,1024]{2,1,0:T(2,128)(2,1)S(1)}, u32[]{:S(2)}, u32[]{:S(2)}) collective-permute-start(bf16[96,2,1024]{2,1,0:T(2,128)(2,1)S(1)} %get-tuple-element.40), channel_id=1, source_target_pairs={{2,4},{4,2},{6,8},{8,6},{10,12},{12,10},{14,16},{16,14},{18,20},{2... | collective-permute-start | bytes 1179656 | tf_op jit(solution)/shard_map/ppermute | solution.py:626
  6.1 1.3 %collective-permute-start = (bf16[528,128]{1,0:T(8,128)(2,1)S(1)}, bf16[528,128]{1,0:T(8,128)(2,1)S(1)}, u32[]{:S(2)}, u32[]{:S(2)}) collective-permute-start(bf16[528,128]{1,0:T(8,128)(2,1)S(1)} %get-tuple-element.37.across.sent), channel_id=1, source_target_pairs={{0,1},{1,0},{2,3},{3,2},{4,5},{5,4},{6,7},{7,6},{8,9},{9,8},{10,11... | collective-permute-start | bytes 405512 | tf_op jit(solution)/shard_map/ppermute | solution.py:627
  7.4 1.1 %shard_map.72 = (bf16[64,2,1152]{2,1,0:T(2,128)(2,1)S(1)}, bf16[64,2,1152]{2,1,0:T(2,128)(2,1)S(1)}) custom-call(bf16[1,128,2,2048]{3,2,1,0:T(2,128)(2,1)} %measured.5, bf16[528,128]{1,0:T(8,128)(2,1)S(1)} %get-tuple-element.37.across.sent), custom_call_target="tpu_custom_call" | custom-call | tf_op jit(solution)/shard_map/pallas_call | solution.py:596
  8.5 0.3 collective-permute-start.5
  8.8 0.0 copy-done.2
  8.8 1.1 %shard_map.69 = (f32[192,512]{1,0:T(8,128)S(1)}, f32[192,512]{1,0:T(8,128)S(1)}, bf16[128,256]{1,0:T(8,128)(2,1)S(1)}, bf16[256,128]{1,0:T(8,128)(2,1)S(1)}, bf1...) custom-call(bf16[2,65]{1,0:T(2,128)(2,1)S(1)} %copy-done.2, ...), custom_call_target="tpu_custom_call" | custom-call | tf_op jit(solution)/shard_map/pallas_call | solution.py:596
  9.9 1.7 %collective-permute-done.across = bf16[528,128]{1,0:T(8,128)(2,1)S(1)} collective-permute-done((bf16[528,128]{1,0:T(8,128)(2,1)S(1)}, bf16[528,128]{1,0:T(8,128)(2,1)S(1)}, u32[]{:S(2)}, u32[]{:S(2)}) %collective-permute-start) | collective-permute-done | bytes 135200 | tf_op jit(solution)/shard_map/ppermute | solution.py:627
  11.6 0.0 copy-start
  11.6 2.5 %collective-permute-start.4 = (bf16[192,128]{1,0:T(8,128)(2,1)S(1)}, bf16[192,128]{1,0:T(8,128)(2,1)S(1)}, u32[]{:S(2)}, u32[]{:S(2)}) collective-permute-start(bf16[192,128]{1,0:T(8,128)(2,1)S(1)} %shard_map.70.strip), channel_id=1, source_target_pairs={{2,4},{4,2},{6,8},{8,6},{10,12},{12,10},{14,16},{16,14},{18,20},{2... | collective-permute-start | bytes 147464 | tf_op jit(solution)/shard_map/ppermute | solution.py:650
  14.1 0.0 copy-start.1
  14.1 1.3 %collective-permute-start.2 = (bf16[64,2,1152]{2,1,0:T(2,128)(2,1)S(1)}, bf16[64,2,1152]{2,1,0:T(2,128)(2,1)S(1)}, u32[]{:S(2)}, u32[]{:S(2)}) collective-permute-start(bf16[64,2,1152]{2,1,0:T(2,128)(2,1)S(1)} %get-tuple-element.39), channel_id=1, source_target_pairs={{0,1},{1,0},{2,3},{3,2},{4,5},{5,4},{6,7},{7,6},{8,9},{9,8},{10,11... | collective-permute-start | bytes 884744 | tf_op jit(solution)/shard_map/ppermute | solution.py:633
  15.4 0.0 copy-done
  15.4 0.1 shard_map.71
  15.5 1.5 %collective-permute-start.1 = (bf16[192,1152]{1,0:T(8,128)(2,1)S(1)}, bf16[192,1152]{1,0:T(8,128)(2,1)S(1)}, u32[]{:S(2)}, u32[]{:S(2)}) collective-permute-start(bf16[192,1152]{1,0:T(8,128)(2,1)S(1)} %shard_map.71), channel_id=1, source_target_pairs={{0,2},{2,0},{4,6},{6,4},{8,10},{10,8},{12,14},{14,12},{16,18},{18,... | collective-permute-start | bytes 1327112 | tf_op jit(solution)/shard_map/ppermute | solution.py:654
  17.0 0.5 %shard_map.73 = (bf16[768,512]{1,0:T(8,128)(2,1)S(1)}, bf16[512,768]{1,0:T(8,128)(2,1)S(1)}, bf16[256,128]{1,0:T(8,128)(2,1)S(1)}, f32[8,1152]{1,0:T(8,128)S(1)}) custom-call(f32[192,512]{1,0:T(8,128)S(1)} %get-tuple-element.42.row_real, ...), custom_call_target="tpu_custom_call", output_to_operand_aliasing={{0}: (3, {}), {1}: (4, {}), {2}: (5, {}), {3}: (6, {})} | custom-call | tf_op jit(solution)/shard_map/pallas_call | solution.py:596
  17.5 0.0 collective-permute-done.4.corner
  17.5 0.4 %collective-permute-done.5.measured_got = bf16[64,2,1152]{2,1,0:T(2,128)(2,1)S(1)} collective-permute-done((bf16[64,2,1152]{2,1,0:T(2,128)(2,1)S(1)}, bf16[64,2,1152]{2,1,0:T(2,128)(2,1)S(1)}, u32[]{:S(2)}, u32[]{:S(2)}) %collective-permute-start.5) | collective-permute-done | bytes 294944 | tf_op jit(solution)/shard_map/ppermute | solution.py:632
  17.9 0.0 collective-permute-done.3.outer
  18.0 0.0 copy-done.1
  18.0 4.7 %shard_map.74 = (f32[384,1152]{1,0:T(8,128)S(1)}, bf16[2,384,1152]{2,1,0:T(8,128)(2,1)S(1)}, bf16[2,384,1152]{2,1,0:T(8,128)(2,1)S(1)}, bf16[2,256,1152]{2,1,0:T...) custom-call(bf16[2,128,2,1024]{3,2,1,0:T(2,128)(2,1)S(1)} %copy-done, ...), custom_call_target="tpu_custom_call" | custom-call | flops 5000000000 | tf_op jit(solution)/shard_map/pallas_call | solution.py:596
  22.7 3.3 %collective-permute-start.8 = (bf16[192,1024]{1,0:T(8,128)(2,1)S(1)}, bf16[192,1024]{1,0:T(8,128)(2,1)S(1)}, u32[]{:S(2)}, u32[]{:S(2)}) collective-permute-start(bf16[192,1024]{1,0:T(8,128)(2,1)S(1)} %get-tuple-element.71), channel_id=1, source_target_pairs={{2,4},{4,2},{6,8},{8,6},{10,12},{12,10},{14,16},{16,14},{18,20},{2... | collective-permute-start | bytes 1179656 | tf_op jit(solution)/shard_map/ppermute | solution.py:678
  25.9 0.0 collective-permute-done.2.measured_got
  26.0 0.0 collective-permute-done.1.inner
  26.0 5.0 %shard_map.75 = (f32[384,1152]{1,0:T(8,128)S(1)}, bf16[2,384,1152]{2,1,0:T(8,128)(2,1)S(1)}, bf16[2,384,1152]{2,1,0:T(8,128)(2,1)S(1)}, bf16[2,256,1152]{2,1,0:T...) custom-call(bf16[2,128,2,1024]{3,2,1,0:T(2,128)(2,1)S(1)} %copy-done, ...), custom_call_target="tpu_custom_call", output_to_operand_aliasing={{0}: (5, {}), {1}: (6, {}), {2}: (7, {}), {3}: (8, {}), {4}... | custom-call | tf_op jit(solution)/shard_map/pallas_call | solution.py:596
  31.0 0.2 collective-permute-start.6
  31.3 0.3 collective-permute-start.7
  31.6 0.6 %shard_map.76 = (f32[256,1024]{1,0:T(8,128)S(1)}, f32[2,128,1024]{2,1,0:T(8,128)S(1)}) custom-call(bf16[768,1024]{1,0:T(8,128)(2,1)S(1)} %get-tuple-element.63.into, f32[384,1280]{1,0:T(8,128)S(1)} %get-tuple-element.64.far_sum, bf16[512,768]{1,0:T(8,128)(2,1)S(1)} %get-tuple-element.62.row_near_adj), custom_call_target="tpu_custom_call" | custom-call | tf_op jit(solution)/shard_map/pallas_call | solution.py:596
  32.2 0.6 %collective-permute-done.7.inner_far = bf16[64,1024]{1,0:T(8,128)(2,1)S(1)} collective-permute-done((bf16[64,1024]{1,0:T(8,128)(2,1)S(1)}, bf16[64,1024]{1,0:T(8,128)(2,1)S(1)}, u32[]{:S(2)}, u32[]{:S(2)}) %collective-permute-start.7) | collective-permute-done | bytes 131104 | tf_op jit(solution)/shard_map/ppermute | solution.py:695
  32.8 0.0 collective-permute-done.6.inner
  32.8 1.2 %shard_map.77 = (f32[128,2,1024]{2,1,0:T(2,128)}, f32[128,2,1024]{2,1,0:T(2,128)}) custom-call(f32[256,1024]{1,0:T(8,128)S(1)} %get-tuple-element.65.near_sum, f32[2,128,1024]{2,1,0:T(8,128)S(1)} %get-tuple-element.66.far_sum, bf16[128,1024]{1,0:T(8,128)(2,1)S(1)} %collective-permute-done.6.inner, bf16[64,1024]{1,0:T(8,128)(2,1)S(1)} %collective-permute-done.7.inner_far), custom_call_target="tpu_custom_call" | custom-call | tf_op jit(solution)/shard_map/pallas_call | solution.py:596
  34.0 2.0 %collective-permute-done.8.outer = bf16[192,1024]{1,0:T(8,128)(2,1)S(1)} collective-permute-done((bf16[192,1024]{1,0:T(8,128)(2,1)S(1)}, bf16[192,1024]{1,0:T(8,128)(2,1)S(1)}, u32[]{:S(2)}, u32[]{:S(2)}) %collective-permute-start.8) | collective-permute-done | bytes 393248 | tf_op jit(solution)/shard_map/ppermute | solution.py:678
  36.0 1.0 %shard_map.78 = (f32[128,2,1024]{2,1,0:T(2,128)}, f32[128,2,1024]{2,1,0:T(2,128)}) custom-call(f32[128,2,1024]{2,1,0:T(2,128)} %get-tuple-element.69.near_in, f32[128,2,1024]{2,1,0:T(2,128)} %get-tuple-element.70.far_in, f32[256,1024]{1,0:T(8,128)S(1)} %get-tuple-element.65.near_sum, ...), custom_call_target="tpu_custom_call", output_to_operand_aliasing={{0}: (0, {}), {1}: (1, {})} | custom-call | tf_op jit(solution)/shard_map/pallas_call | solution.py:596
  (1 shorter events, 0.0 us)
Async XLA Ops:
  0.6 8.2 %copy-start.2 = (bf16[2,65]{1,0:T(2,128)(2,1)S(1)}, bf16[2,65]{1,0:T(2,128)(2,1)}, u32[]{:S(2)}) copy-start(bf16[2,65]{1,0:T(2,128)(2,1)} %taps.1) | copy-start | bytes 784
  2.4 15.5 %collective-permute-start.3 = (bf16[96,2,1024]{2,1,0:T(2,128)(2,1)S(1)}, bf16[96,2,1024]{2,1,0:T(2,128)(2,1)S(1)}, u32[]{:S(2)}, u32[]{:S(2)}) collective-permute-start(bf16[96,2,1024]{2,1,0:T(2,128)(2,1)S(1)} %get-tuple-element.40), channel_id=1, source_target_pairs={{2,4},{4,2},{6,8},{8,6},{10,12},{12,10},{14,16},{16,14},{18,20},{2... | collective-permute-start | bytes 1179656 | tf_op jit(solution)/shard_map/ppermute | solution.py:626
  6.1 5.5 %collective-permute-start = (bf16[528,128]{1,0:T(8,128)(2,1)S(1)}, bf16[528,128]{1,0:T(8,128)(2,1)S(1)}, u32[]{:S(2)}, u32[]{:S(2)}) collective-permute-start(bf16[528,128]{1,0:T(8,128)(2,1)S(1)} %get-tuple-element.37.across.sent), channel_id=1, source_target_pairs={{0,1},{1,0},{2,3},{3,2},{4,5},{5,4},{6,7},{7,6},{8,9},{9,8},{10,11... | collective-permute-start | bytes 405512 | tf_op jit(solution)/shard_map/ppermute | solution.py:627
  8.5 9.4 %collective-permute-start.5 = (bf16[64,2,1152]{2,1,0:T(2,128)(2,1)S(1)}, bf16[64,2,1152]{2,1,0:T(2,128)(2,1)S(1)}, u32[]{:S(2)}, u32[]{:S(2)}) collective-permute-start(bf16[64,2,1152]{2,1,0:T(2,128)(2,1)S(1)} %get-tuple-element.41), channel_id=1, source_target_pairs={{0,1},{1,0},{2,3},{3,2},{4,5},{5,4},{6,7},{7,6},{8,9},{9,8},{10,11... | collective-permute-start | bytes 884744 | tf_op jit(solution)/shard_map/ppermute | solution.py:632
  11.6 3.8 %copy-start = (bf16[2,128,2,1024]{3,2,1,0:T(2,128)(2,1)S(1)}, bf16[2,128,2,1024]{3,2,1,0:T(2,128)(2,1)}, u32[]{:S(2)}) copy-start(bf16[2,128,2,1024]{3,2,1,0:T(2,128)(2,1)} %slices.7) | copy-start | bytes 3145732
  11.6 5.9 %collective-permute-start.4 = (bf16[192,128]{1,0:T(8,128)(2,1)S(1)}, bf16[192,128]{1,0:T(8,128)(2,1)S(1)}, u32[]{:S(2)}, u32[]{:S(2)}) collective-permute-start(bf16[192,128]{1,0:T(8,128)(2,1)S(1)} %shard_map.70.strip), channel_id=1, source_target_pairs={{2,4},{4,2},{6,8},{8,6},{10,12},{12,10},{14,16},{16,14},{18,20},{2... | collective-permute-start | bytes 147464 | tf_op jit(solution)/shard_map/ppermute | solution.py:650
  14.1 3.8 %copy-start.1 = (bf16[1,128,2,2048]{3,2,1,0:T(2,128)(2,1)S(1)}, bf16[1,128,2,2048]{3,2,1,0:T(2,128)(2,1)}, u32[]{:S(2)}) copy-start(bf16[1,128,2,2048]{3,2,1,0:T(2,128)(2,1)} %measured.5) | copy-start | bytes 3145732
  14.1 11.8 %collective-permute-start.2 = (bf16[64,2,1152]{2,1,0:T(2,128)(2,1)S(1)}, bf16[64,2,1152]{2,1,0:T(2,128)(2,1)S(1)}, u32[]{:S(2)}, u32[]{:S(2)}) collective-permute-start(bf16[64,2,1152]{2,1,0:T(2,128)(2,1)S(1)} %get-tuple-element.39), channel_id=1, source_target_pairs={{0,1},{1,0},{2,3},{3,2},{4,5},{5,4},{6,7},{7,6},{8,9},{9,8},{10,11... | collective-permute-start | bytes 884744 | tf_op jit(solution)/shard_map/ppermute | solution.py:633
  15.5 10.5 %collective-permute-start.1 = (bf16[192,1152]{1,0:T(8,128)(2,1)S(1)}, bf16[192,1152]{1,0:T(8,128)(2,1)S(1)}, u32[]{:S(2)}, u32[]{:S(2)}) collective-permute-start(bf16[192,1152]{1,0:T(8,128)(2,1)S(1)} %shard_map.71), channel_id=1, source_target_pairs={{0,2},{2,0},{4,6},{6,4},{8,10},{10,8},{12,14},{14,12},{16,18},{18,... | collective-permute-start | bytes 1327112 | tf_op jit(solution)/shard_map/ppermute | solution.py:654
  22.7 13.3 %collective-permute-start.8 = (bf16[192,1024]{1,0:T(8,128)(2,1)S(1)}, bf16[192,1024]{1,0:T(8,128)(2,1)S(1)}, u32[]{:S(2)}, u32[]{:S(2)}) collective-permute-start(bf16[192,1024]{1,0:T(8,128)(2,1)S(1)} %get-tuple-element.71), channel_id=1, source_target_pairs={{2,4},{4,2},{6,8},{8,6},{10,12},{12,10},{14,16},{16,14},{18,20},{2... | collective-permute-start | bytes 1179656 | tf_op jit(solution)/shard_map/ppermute | solution.py:678
  31.0 1.8 %collective-permute-start.6 = (bf16[128,1024]{1,0:T(8,128)(2,1)S(1)}, bf16[128,1024]{1,0:T(8,128)(2,1)S(1)}, u32[]{:S(2)}, u32[]{:S(2)}) collective-permute-start(bf16[128,1024]{1,0:T(8,128)(2,1)S(1)} %get-tuple-element.67), channel_id=1, source_target_pairs={{0,2},{2,0},{4,6},{6,4},{8,10},{10,8},{12,14},{14,12},{16,18},{18,... | collective-permute-start | bytes 786440 | tf_op jit(solution)/shard_map/ppermute | solution.py:694
  31.3 1.5 %collective-permute-start.7 = (bf16[64,1024]{1,0:T(8,128)(2,1)S(1)}, bf16[64,1024]{1,0:T(8,128)(2,1)S(1)}, u32[]{:S(2)}, u32[]{:S(2)}) collective-permute-start(bf16[64,1024]{1,0:T(8,128)(2,1)S(1)} %get-tuple-element.68), channel_id=1, source_target_pairs={{0,2},{2,0},{4,6},{6,4},{8,10},{10,8},{12,14},{14,12},{16,18},{18,... | collective-permute-start | bytes 393224 | tf_op jit(solution)/shard_map/ppermute | solution.py:695

commit v5 on v4

--- a/solution.py
+++ b/solution.py
@@ -10,10 +10,10 @@
 
 LANES = 128
 BF16 = jnp.bfloat16
-STRIP_FLOPS = 17 * 10**8
 INNER_FLOPS = 0
-MATS_FLOPS = 0
-OWN_FLOPS = 5 * 10**9
+FORWARD_FLOPS = 24 * 10**8
+BACKWARD_FLOPS = 10**9
+MEASURED_FLOPS = 4 * 10**9
 F32 = jnp.float32
 
 
@@ -29,7 +29,7 @@
     return [(at, min(step, width - at)) for at in range(0, width, step)]
 
 
-def edges_kernel(half, slices, angle_freq, chosen, outer, across, strips, table, sems):
+def edges_kernel(half, slices, angle_freq, outer, early, across, table, strips, sems):
     rows, cols = slices.shape[1], slices.shape[3]
     parity = lax.axis_index("rows") % 2
     side = lax.axis_index("ang")
@@ -42,8 +42,19 @@
         copy.start()
     for copy in copies[:2]:
         copy.wait()
-    for slab in range(2):
-        across[slab * 2 * rows : (slab + 1) * 2 * rows] = strips[slab].reshape(2 * rows, LANES)
+    begin, rest = 0, 0
+    for slab, size in ((0, 2 * half), (1, half)):
+        there = strips[slab, pl.ds(parity * (rows - size), size)]
+        early[begin : begin + 2 * size] = there.reshape(2 * size, LANES)
+        there = strips[slab, pl.ds((1 - parity) * size, rows - size)]
+        across[rest : rest + 2 * (rows - size)] = there.reshape(2 * (rows - size), LANES)
+        begin, rest = begin + 2 * size, rest + 2 * (rows - size)
+    early[begin:] = jnp.zeros((16, LANES), BF16)
+    for copy in copies[2:]:
+        copy.wait()
+
+
+def frequencies_kernel(table, chosen, early_in, early):
     row = iota((16, LANES), 0)
     block = jnp.zeros((16, LANES), F32)
     entry = jnp.where(iota(table.shape, 1) == chosen[0], table[...], 0.0)
@@ -54,9 +65,7 @@
             rounded = rest.astype(BF16).astype(F32)
             block = jnp.where(row == 3 * part + piece, rounded, block)
             rest = rest - rounded
-    across[4 * rows :] = block.astype(BF16)
-    for copy in copies[2:]:
-        copy.wait()
+    early[early.shape[0] - 16 :] = block.astype(BF16)
 
 
 def sent_frequencies(across):
@@ -64,26 +73,22 @@
     return [(sent[i : i + 1] + sent[i + 1 : i + 2] + sent[i + 2 : i + 3])[:, :1] for i in (0, 3)]
 
 
-def strip_kernel(half, across, row_half, strip):
-    rows = (across.shape[0] - 16) // 4
-    parity = lax.axis_index("rows") % 2
-    begin = 0
-    for slab, size in ((0, 4 * half), (1, 2 * half)):
-        frm = slab * 2 * rows + parity * (2 * rows - size)
-        strip[begin : begin + size] = across[pl.ds(pl.multiple_of(frm, 16), size)]
-        begin += size
-
-
-def inner_edge_kernel(half, slices, across, strip, edge):
+def inner_edge_kernel(half, slices, across, sent, edge):
     rows, cols = slices.shape[1], slices.shape[3]
     other = 1 - lax.axis_index("rows") % 2
     begin = 0
     for slab, size in ((0, 2 * half), (1, half)):
         there = slice(begin, begin + 2 * size)
         edge[there, :cols] = slices[slab, pl.ds(other * (rows - size), size)].reshape(2 * size, cols)
-        frm = slab * 2 * rows + other * 2 * (rows - size)
-        edge[there, cols:] = across[pl.ds(pl.multiple_of(frm, 16), 2 * size)]
         begin += 2 * size
+    edge[: 4 * half, cols:] = across[inner_rows(half, rows, other, 0)]
+    edge[4 * half :, cols:] = across[inner_rows(half, rows, other, 1)]
+
+
+def inner_rows(half, rows, other, slab):
+    if slab == 0:
+        return pl.ds(pl.multiple_of(other * (2 * rows - 8 * half), 16), 4 * half)
+    return pl.ds(pl.multiple_of(2 * rows - 4 * half + other * (2 * rows - 4 * half), 16), 2 * half)
 
 
 def measured_kernel(measured, sent, outer, inner, sems):
@@ -320,13 +325,11 @@
         )
 
     def store(j, y):
-        y = y.astype(BF16)
         far = part.read(far_slab, tile(j))
         sr, si = far[:size], far[size:]
         for member in range(2):
             re, im = y[member * size : (member + 1) * size, :LANES], y[member * size : (member + 1) * size, LANES:]
-            part.write(field.at[member], tile(j), jnp.concatenate([re, im], axis=0))
-            re, im = re.astype(F32), im.astype(F32)
+            part.write(field.at[member], tile(j), jnp.concatenate([re, im], axis=0).astype(BF16))
             both = jnp.concatenate([sr * re - si * im, sr * im + si * re], axis=0)
             part.write(after.at[member], tile(j), both.astype(BF16))
 
@@ -360,13 +363,13 @@
     column_step(tiles, lambda j: tiles.back(j, 2), col_taps, load2, store2, tiles.count)
 
 
-def residue_rows(tiles, members, windows, leave, split_meas, col_taps, leaving, residue, back):
+def residue_rows(tiles, members, measured, leave, col_taps, leaving, residue, back):
     size = leave.count
-    for member, window in zip(members, windows):
+    for member in members:
         for at, lanes in lane_chunks(tiles.width):
             here = slice(at, at + lanes)
-            meas = dot(split_meas[...], window(at, lanes))
-            residue[member, :, here] = (leaving[member, :, here].astype(F32) - meas).astype(BF16)
+            leaves = leaving[member, :, here].astype(F32)
+            residue[member, :, here] = (leaves - measured(member, at, lanes)).astype(BF16)
         residue[member, :, tiles.width :] = residue[member, :, :LANES]
 
     def load(j):
@@ -438,12 +441,12 @@
         sums[:, tile(j)] = y.astype(BF16)
 
 
-def outer_kernel(
+def outer_forward_kernel(
     half,
-    slices, outer, across, corner, measured, measured_got,
-    row_near, row_half, row_half_adj, row_edge, col_taps, split_far, split_meas, waves,
-    far_slab, field, after, back, far_sum, into, sums,
-    near_raw, far_raw, entry, narrow, leaving, residue, carry,
+    slices, outer, early, across, corner,
+    row_near, row_half, col_taps, split_far, waves,
+    far_slab, field, after, leaving,
+    near_raw, far_raw, entry, narrow,
 ):
     rows, cols = slices.shape[1], slices.shape[3]
     tiles = Tiles(cols)
@@ -451,36 +454,59 @@
     mid = rows + 2 * half
     parity = lax.axis_index("rows") % 2
 
+    begin, rest = 0, 0
     for slab, ref, margin in ((0, near_raw, 4 * half), (1, far_raw, 2 * half)):
         own = ref.shape[0] - margin
-        begin = 0 if slab == 0 else 4 * half
         first = parity * (rows - own // 2)
         at = pl.ds(pl.multiple_of((1 - parity) * margin, 16), own)
         ref[at, :cols] = slices[slab, pl.ds(first, own // 2)].reshape(own, cols)
-        ref[at, cols:width] = across[pl.ds(pl.multiple_of(slab * 2 * rows + 2 * first, 16), own)]
+        at = pl.ds(pl.multiple_of(margin + parity * (own - 2 * margin), 16), margin)
+        ref[at, cols:width] = early[begin : begin + margin]
+        at = pl.ds(pl.multiple_of((1 - parity) * 2 * margin, 16), own - margin)
+        frm = pl.ds(pl.multiple_of(rest + parity * (2 * rows - own), 16), own - margin)
+        ref[at, cols:width] = across[frm]
         at = pl.ds(pl.multiple_of(parity * own, 16), margin)
         ref[at, :cols] = outer[begin // 2 : (begin + margin) // 2].reshape(margin, cols)
         ref[at, cols:width] = corner[begin : begin + margin]
+        begin, rest = begin + margin, rest + 2 * rows - margin
     far_raw[:, width:] = far_raw[:, :LANES]
 
     part = Rows(parity * (rows // 2), rows, mid)
     source = Rows(parity * (rows // 2), rows // 2, mid)
-    leave = Rows(parity * (rows // 2), rows // 2, rows)
-    edge = Rows(parity * rows, 2 * half, mid)
-    pick = Rows(parity * 2 * half, 2 * half, rows)
     split_rows(tiles, part, split_far, far_raw, far_slab, half)
     lanes = pl.ds(pl.multiple_of(parity * 4 * half, LANES), near_raw.shape[0])
     forward_rows(
         tiles, part, source, near_raw, lanes, far_slab, row_near, row_half, col_taps, waves, entry, field, after,
         narrow, leaving,
     )
+
+
+def outer_backward_kernel(
+    half,
+    far_slab, field, leaving, measured, measured_got,
+    row_half_adj, row_edge, col_taps, split_meas, waves,
+    back, far_sum, into, sums,
+    residue, carry,
+):
+    cols = into.shape[1]
+    tiles = Tiles(cols)
+    mid = far_sum.shape[0] // 2
+    rows = mid - 2 * half
+    parity = lax.axis_index("rows") % 2
+    leave = Rows(parity * (rows // 2), rows // 2, rows)
+    edge = Rows(parity * rows, 2 * half, mid)
+    pick = Rows(parity * 2 * half, 2 * half, rows)
     windows = (functools.partial(own_window, measured, parity), functools.partial(got_window, measured_got))
-    residue_rows(tiles, (0, 1), windows, leave, split_meas, col_taps, leaving, residue, back)
+
+    def parts(member, at, size):
+        return dot(split_meas[...], windows[member](at, size))
+
+    residue_rows(tiles, (0, 1), parts, leave, col_taps, leaving, residue, back)
     backward_rows(
         tiles, (0, 1), edge, pick.read(row_half_adj, slice(None)), lambda one, here: leave.read(back.at[one], here),
         field, far_slab, col_taps, waves, carry, far_sum, into,
     )
-    far_sum[:, :LANES] = far_sum[:, width:]
+    far_sum[:, :LANES] = far_sum[:, tiles.width :]
     left = row_edge[...].T
     for at, size in lane_chunks(cols):
         here = slice(at, at + size)
@@ -489,9 +515,17 @@
     far_margin(tiles, half, Rows(parity * (rows + half), half, mid), far_sum, sums.at[4 * half :])
 
 
+def inner_measured_kernel(measured, measured_got, split_meas, sent, parts):
+    other = 1 - lax.axis_index("rows") % 2
+    windows = (functools.partial(own_window, measured, other), functools.partial(got_window, measured_got))
+    for member in range(2):
+        for at, size in lane_chunks(parts.shape[2]):
+            parts[member, :, at : at + size] = dot(split_meas[...], windows[member](at, size))
+
+
 def inner_kernel(
     half,
-    slices, inner, across, measured, measured_got, far_slab_in, field_in, after_in, back_in, far_in, into_in,
+    slices, inner, across, measured, far_slab_in, field_in, after_in, back_in, far_in, into_in,
     row_near, row_half, row_adj, row_near_adj, col_taps, split_meas, waves,
     far_slab, field, after, back, far_sum, into, sums, far_sums,
     near_raw, far_raw, entry, narrow, leaving, residue, carry,
@@ -511,7 +545,7 @@
         first = other * (rows - own // 2)
         at = pl.ds(pl.multiple_of((1 - other) * margin, 16), own)
         ref[at, :cols] = slices[slab, pl.ds(first, own // 2)].reshape(own, cols)
-        ref[at, cols : tiles.width] = across[pl.ds(pl.multiple_of(slab * 2 * rows + 2 * first, 16), own)]
+        ref[at, cols : tiles.width] = across[inner_rows(half, rows, other, slab)]
         ref[pl.ds(pl.multiple_of(other * own, 16), margin), : tiles.width] = inner[begin : begin + margin]
     far_raw[:, tiles.width :] = far_raw[:, :LANES]
 
@@ -521,8 +555,10 @@
         tiles, part, source, near_raw, lanes, far_slab, row_near, row_half, col_taps, waves, entry, field, after,
         narrow, leaving,
     )
-    windows = (functools.partial(own_window, measured, other), functools.partial(got_window, measured_got))
-    residue_rows(tiles, (0, 1), windows, leave, split_meas, col_taps, leaving, residue, back)
+    residue_rows(
+        tiles, (0, 1), lambda member, at, size: measured[member, :, at : at + size], leave, col_taps, leaving,
+        residue, back,
+    )
     rest = Rows(other * 2 * half, rows, mid)
     left = jnp.concatenate([row_adj[rest.at(0), :], row_adj[rest.at(1), :]], axis=0)
     backward_rows(
@@ -574,16 +610,23 @@
     parity = lax.axis_index("rows") % 2
     margin = 4 * half
     at = pl.ds(pl.multiple_of(parity * (2 * rows - margin), 16), margin)
-    near_rows[...] = (near_sum[at] + outer[:margin].astype(F32)).reshape(2 * half, 2, cols)
-    near_copy = pltpu.make_async_copy(near_rows, near.at[pl.ds(parity * (rows - 2 * half), 2 * half)], sems.at[0])
-    near_copy.start()
+    copies = []
+    for piece in range(2):
+        at = pl.ds(pl.multiple_of(parity * (2 * rows - margin) + piece * 2 * half, 16), 2 * half)
+        added = near_sum[at] + outer[piece * 2 * half : (piece + 1) * 2 * half].astype(F32)
+        here = pl.ds(piece * half, half)
+        near_rows[here] = added.reshape(half, 2, cols)
+        there = near.at[pl.ds(parity * (rows - 2 * half) + piece * half, half)]
+        copies.append(pltpu.make_async_copy(near_rows.at[here], there, sems.at[piece]))
+        copies[-1].start()
     at = pl.ds(pl.multiple_of(parity * (rows - half), 16), half)
     for comp in range(2):
         got = outer[margin + comp * half : margin + (comp + 1) * half].astype(F32)
         far_rows[:, comp, :] = far_sum[comp, at] + got
-    far_copy = pltpu.make_async_copy(far_rows, far.at[pl.ds(parity * (rows - half), half)], sems.at[1])
+    far_copy = pltpu.make_async_copy(far_rows, far.at[pl.ds(parity * (rows - half), half)], sems.at[2])
     far_copy.start()
-    near_copy.wait()
+    for copy in copies:
+        copy.wait()
     far_copy.wait()
 
 
@@ -617,14 +660,22 @@
     inner_pairs = [(i, i + 1 - 2 * (i % 2)) for i in range(count)]
     side_pairs = [(i, 1 - i) for i in range(lax.axis_size("ang"))]
     edge = 6 * half
-    outer, across = call(
+    outer, early, across, table = call(
         functools.partial(edges_kernel, half),
-        [((3 * half, 2, cols), BF16), ((4 * rows + 16, LANES), BF16)],
-        (slices, angle_freq.T, chosen), hbm=(0, 1), scalars=(2,), outs_outside=(0,),
-        scratch=[((2, rows, 2, LANES), BF16), (angle_freq.shape[::-1], F32), pltpu.SemaphoreType.DMA((4,))],
+        [
+            ((3 * half, 2, cols), BF16), ((edge + 16, LANES), BF16), ((4 * rows - edge, LANES), BF16),
+            (angle_freq.shape[::-1], F32),
+        ],
+        (slices, angle_freq.T), hbm=(0, 1), outs_outside=(0,),
+        scratch=[((2, rows, 2, LANES), BF16), pltpu.SemaphoreType.DMA((4,))],
+    )
+    (early,) = call(
+        frequencies_kernel, [((edge + 16, LANES), BF16)], (table, chosen, early), scalars=(1,), aliases={2: 0},
     )
     outer_got = lax.ppermute(outer, "rows", outer_pairs)
+    early_got = lax.ppermute(early, "ang", side_pairs)
     across_got = lax.ppermute(across, "ang", side_pairs)
+    corner_got = lax.ppermute(early_got, "rows", outer_pairs)
     meas_outer, meas_inner = call(
         measured_kernel, [((rows // 2, 2, width), BF16)] * 2, (measured, across), hbm=(0,), outside=(1,),
         outs_outside=(0, 1), scratch=[pltpu.SemaphoreType.DMA((4,))],
@@ -641,19 +692,14 @@
             ((2 * mid, 2 * rows), BF16), ((10, 4 * LANES, 2 * LANES), BF16), ((2 * rows, 2 * rows), BF16),
             ((rows, rows), BF16), *phased,
         ],
-        (kernel_taps, across), flops=MATS_FLOPS,
-    )
-    (strip,) = call(
-        functools.partial(strip_kernel, half), [((edge, LANES), BF16)], (across_got, row_half), outside=(1,),
-        flops=STRIP_FLOPS,
-    )
-    corner_got = lax.ppermute(strip, "rows", outer_pairs)
+        (kernel_taps, early),
+    )
     (inner,) = call(
-        functools.partial(inner_edge_kernel, half), [((edge, width), BF16)], (slices, across_got, strip), outside=(2,),
+        functools.partial(inner_edge_kernel, half), [((edge, width), BF16)], (slices, across_got, row_half), outside=(2,),
     )
     inner_got = lax.ppermute(inner, "rows", inner_pairs)
     row_near, row_near_adj, row_edge, waves = call(
-        functools.partial(phases_kernel, half, length), phased, (row_real, row_imag, across_got, *partial),
+        functools.partial(phases_kernel, half, length), phased, (row_real, row_imag, early_got, *partial),
         aliases={3: 0, 4: 1, 5: 2, 6: 3},
     )
     state = [
@@ -661,29 +707,39 @@
         ((2, 2 * rows, width), BF16), ((2 * mid, width + LANES), F32), ((4 * mid, cols), BF16),
     ]
     leaving_shape = ((2, rows, width), BF16)
-    far_slab, field, after, back, far_sum, into, outer_sums = call(
-        functools.partial(outer_kernel, half),
-        [*state, ((edge, cols), BF16)],
-        (
-            slices, outer_got, across_got, corner_got, measured, outer_meas,
-            row_near, row_half, row_half_adj, row_edge, col_taps, split_far, split_meas, waves,
-        ),
+    far_slab, field, after, leaving = call(
+        functools.partial(outer_forward_kernel, half),
+        [*state[:3], leaving_shape],
+        (slices, outer_got, early_got, across_got, corner_got, row_near, row_half, col_taps, split_far, waves),
         scratch=[
             ((2 * rows + 4 * half, width), BF16), ((2 * rows, width + LANES), BF16),
-            ((2, 2 * rows, width + LANES), BF16), ((2, rows, width + LANES), BF16), leaving_shape,
-            ((2, rows, width + LANES), BF16), ((2, 4 * half, width + LANES), BF16),
+            ((2, 2 * rows, width + LANES), BF16), ((2, rows, width + LANES), BF16),
         ],
-        flops=OWN_FLOPS,
+        flops=FORWARD_FLOPS,
+    )
+    back, far_sum, into, outer_sums = call(
+        functools.partial(outer_backward_kernel, half),
+        [*state[3:], ((edge, cols), BF16)],
+        (
+            far_slab, field, leaving, measured, outer_meas,
+            row_half_adj, row_edge, col_taps, split_meas, waves,
+        ),
+        scratch=[((2, rows, width + LANES), BF16), ((2, 4 * half, width + LANES), BF16)],
+        flops=BACKWARD_FLOPS,
     )
     outer_back = lax.ppermute(outer_sums, "rows", outer_pairs)
+    (inner_parts,) = call(
+        inner_measured_kernel, [((2, rows, width), F32)], (measured, inner_meas, split_meas, outer_sums), outside=(3,),
+        flops=MEASURED_FLOPS,
+    )
     far_slab, field, after, back, far_sum, into, inner_sums, inner_far = call(
         functools.partial(inner_kernel, half),
         [*state, ((4 * half, cols), BF16), ((2 * half, cols), BF16)],
         (
-            slices, inner_got, across_got, measured, inner_meas, far_slab, field, after, back, far_sum, into,
+            slices, inner_got, across_got, inner_parts, far_slab, field, after, back, far_sum, into,
             row_near, row_half, row_adj, row_near_adj, col_taps, split_meas, waves,
         ),
-        aliases={5: 0, 6: 1, 7: 2, 8: 3, 9: 4, 10: 5},
+        aliases={4: 0, 5: 1, 6: 2, 7: 3, 8: 4, 9: 5},
         scratch=[
             ((rows + 4 * half, width), BF16), ((4 * half, width + LANES), BF16),
             ((2, 4 * half, width + LANES), BF16), ((2, rows, width + LANES), BF16), leaving_shape,
@@ -705,7 +761,7 @@
     near, far = call(
         functools.partial(finish_kernel, half), [((rows, 2, cols), F32)] * 2,
         (near, far, near_sum, far_own, outer_back), outside=(0, 1), outs_outside=(0, 1), aliases={0: 0, 1: 1},
-        scratch=[((2 * half, 2, cols), F32), ((half, 2, cols), F32), pltpu.SemaphoreType.DMA((2,))],
+        scratch=[((2 * half, 2, cols), F32), ((half, 2, cols), F32), pltpu.SemaphoreType.DMA((3,))],
     )
     return near, far
 

time: 37.4 us -> 36.6 us (0.979)
  waiting for transfers between devices: 4.71 us -> 1.81 us
  starting transfers between devices: 14.4 us -> 15.6 us
  Pallas kernels: 16.4 us -> 17.3 us
    ppermute x1, waiting for transfers between devices: 1.71 us -> 0.01 us  [columns_local(): across_got = lax.ppermute(across, 'ang', side_pairs)]
    ppermute x1 -> x2, starting transfers between devices: 2.47 us -> 4 us  [the longest x1 2.75 us: columns_local(): corner_got = lax.ppermute(early_got, 'rows', outer_pairs)]
    ppermute x1, starting transfers between devices: 1.28 us -> 0.25 us  [columns_local(): across_got = lax.ppermute(across, 'ang', side_pairs)]
    ppermute x1, starting transfers between devices: 0.32 us -> 1.22 us  [columns_local(): outer_meas = lax.ppermute(meas_outer, 'ang', side_pairs)]
    pallas_call x11 -> x13, Pallas kernels: 16.4 us -> 17.3 us  [call(): pl.pallas_call(kernel, out_shape=[jax.ShapeDtypeStruct(shape, dtype) for...]
    ppermute x1, waiting for transfers between devices: 1.98 us -> 1.22 us  [columns_local(): outer_back = lax.ppermute(outer_sums, 'rows', outer_pairs)]
    ppermute x1, starting transfers between devices: 1.28 us -> 0.73 us  [columns_local(): inner_meas = lax.ppermute(meas_inner, 'ang', side_pairs)]
    ppermute x1, waiting for transfers between devices: 0.44 us -> 0.01 us  [columns_local(): outer_meas = lax.ppermute(meas_outer, 'ang', side_pairs)]
  transfers between devices with their start and end apart: 9 -> 10, of which waited for: 4 -> 2; matrix products, arithmetic and copies ran while one was open for 0% -> 0% of each run, Pallas kernels for 39% -> 42%
where the time goes in v5:
time: 36.6 us; the launch traced here: 36.4 us
  Pallas kernels  17.3 us (47%)
  starting transfers between devices  15.6 us (43%)
  waiting for transfers between devices  1.81 us (5%)
  between operations  1.61 us (4%)
    pallas_call x13, Pallas kernels, call(): pl.pallas_call(kernel, out_shape=[jax.ShapeDtypeStruct(shape, dtype) for...  17.3 us
    ppermute x1, starting transfers between devices, columns_local(): outer_got = lax.ppermute(outer, 'rows', outer_pairs)  3.71 us
    ppermute x1, starting transfers between devices, columns_local(): outer_back = lax.ppermute(outer_sums, 'rows', outer_pairs)  3.66 us
    ppermute x1, starting transfers between devices, columns_local(): corner_got = lax.ppermute(early_got, 'rows', outer_pairs)  2.75 us
    ppermute x1, starting transfers between devices, columns_local(): inner_got = lax.ppermute(inner, 'rows', inner_pairs)  1.51 us
    ppermute x1, starting transfers between devices, columns_local(): early_got = lax.ppermute(early, 'ang', side_pairs)  1.25 us
    ppermute x1, waiting for transfers between devices, columns_local(): outer_back = lax.ppermute(outer_sums, 'rows', outer_pairs)  1.22 us
    ppermute x1, starting transfers between devices, columns_local(): outer_meas = lax.ppermute(meas_outer, 'ang', side_pairs)  1.22 us
  transfers between devices with their start and end apart: 10, of which 2 were waited for; matrix products, arithmetic and copies ran while one was open for 0% of the time, Pallas kernels for 42%

profile of v5, /device:TPU:17, one launch (start us, length us, event | category | flops | bytes accessed | tf_op | source)
XLA Modules:
  0.0 36.4 jit_solution(15504276070196185389)
XLA Ops:
  0.6 0.0 copy-start.2
  0.6 1.1 %shard_map.68 = (bf16[96,2,1024]{2,1,0:T(2,128)(2,1)S(1)}, bf16[208,128]{1,0:T(8,128)(2,1)S(1)}, bf16[320,128]{1,0:T(8,128)(2,1)S(1)}, f32[2,128]{1,0:T(2,128)S(1)}) custom-call(bf16[2,128,2,1024]{3,2,1,0:T(2,128)(2,1)} %slices.7, f32[2,128]{1,0:T(2,128)} %bitcast.1), custom_call_target="tpu_custom_call" | custom-call | tf_op jit(solution)/shard_map/pallas_call | solution.py:639
  1.8 3.7 %collective-permute-start.3 = (bf16[96,2,1024]{2,1,0:T(2,128)(2,1)S(1)}, bf16[96,2,1024]{2,1,0:T(2,128)(2,1)S(1)}, u32[]{:S(2)}, u32[]{:S(2)}) collective-permute-start(bf16[96,2,1024]{2,1,0:T(2,128)(2,1)S(1)} %get-tuple-element.46), channel_id=1, source_target_pairs={{2,4},{4,2},{6,8},{8,6},{10,12},{12,10},{14,16},{16,14},{18,20},{2... | collective-permute-start | bytes 1179656 | tf_op jit(solution)/shard_map/ppermute | solution.py:675
  6.1 0.1 shard_map.69.across
  6.2 1.2 %collective-permute-start.4 = (bf16[208,128]{1,0:T(8,128)(2,1)S(1)}, bf16[208,128]{1,0:T(8,128)(2,1)S(1)}, u32[]{:S(2)}, u32[]{:S(2)}) collective-permute-start(bf16[208,128]{1,0:T(8,128)(2,1)S(1)} %shard_map.69.across), channel_id=1, source_target_pairs={{0,1},{1,0},{2,3},{3,2},{4,5},{5,4},{6,7},{7,6},{8,9},{9,8},{10,11... | collective-permute-start | bytes 159752 | tf_op jit(solution)/shard_map/ppermute | solution.py:676
  7.5 0.0 copy-start
  7.5 0.3 collective-permute-start
  7.7 1.1 %shard_map.72 = (bf16[64,2,1152]{2,1,0:T(2,128)(2,1)S(1)}, bf16[64,2,1152]{2,1,0:T(2,128)(2,1)S(1)}) custom-call(bf16[1,128,2,2048]{3,2,1,0:T(2,128)(2,1)} %measured.5, bf16[320,128]{1,0:T(8,128)(2,1)S(1)} %get-tuple-element.40.sent), custom_call_target="tpu_custom_call" | custom-call | tf_op jit(solution)/shard_map/pallas_call | solution.py:639
  8.9 1.2 %collective-permute-start.6 = (bf16[64,2,1152]{2,1,0:T(2,128)(2,1)S(1)}, bf16[64,2,1152]{2,1,0:T(2,128)(2,1)S(1)}, u32[]{:S(2)}, u32[]{:S(2)}) collective-permute-start(bf16[64,2,1152]{2,1,0:T(2,128)(2,1)S(1)} %get-tuple-element.60), channel_id=1, source_target_pairs={{0,1},{1,0},{2,3},{3,2},{4,5},{5,4},{6,7},{7,6},{8,9},{9,8},{10,11... | collective-permute-start | bytes 884744 | tf_op jit(solution)/shard_map/ppermute | solution.py:683
  10.1 0.0 collective-permute-done.4.across.early
  10.1 2.7 %collective-permute-start.5 = (bf16[208,128]{1,0:T(8,128)(2,1)S(1)}, bf16[208,128]{1,0:T(8,128)(2,1)S(1)}, u32[]{:S(2)}, u32[]{:S(2)}) collective-permute-start(bf16[208,128]{1,0:T(8,128)(2,1)S(1)} %collective-permute-done.4.across.early), channel_id=1, source_target_pairs={{2,4},{4,2},{6,8},{8,6},{10,12},{12,10},{14,16},{16,14},{18,20},{2... | collective-permute-start | bytes 159752 | tf_op jit(solution)/shard_map/ppermute | solution.py:678
  12.8 0.7 %collective-permute-start.2 = (bf16[64,2,1152]{2,1,0:T(2,128)(2,1)S(1)}, bf16[64,2,1152]{2,1,0:T(2,128)(2,1)S(1)}, u32[]{:S(2)}, u32[]{:S(2)}) collective-permute-start(bf16[64,2,1152]{2,1,0:T(2,128)(2,1)S(1)} %get-tuple-element.44), channel_id=1, source_target_pairs={{0,1},{1,0},{2,3},{3,2},{4,5},{5,4},{6,7},{7,6},{8,9},{9,8},{10,11... | collective-permute-start | bytes 884744 | tf_op jit(solution)/shard_map/ppermute | solution.py:684
  13.6 0.0 copy-done.2
  13.6 1.1 %shard_map.70 = (f32[192,512]{1,0:T(8,128)S(1)}, f32[192,512]{1,0:T(8,128)S(1)}, bf16[128,256]{1,0:T(8,128)(2,1)S(1)}, bf16[256,128]{1,0:T(8,128)(2,1)S(1)}, bf1...) custom-call(bf16[2,65]{1,0:T(2,128)(2,1)S(1)} %copy-done.2, ...), custom_call_target="tpu_custom_call" | custom-call | tf_op jit(solution)/shard_map/pallas_call | solution.py:639
  14.7 0.5 %shard_map.73 = (bf16[768,512]{1,0:T(8,128)(2,1)S(1)}, bf16[512,768]{1,0:T(8,128)(2,1)S(1)}, bf16[256,128]{1,0:T(8,128)(2,1)S(1)}, f32[8,1152]{1,0:T(8,128)S(1)}) custom-call(f32[192,512]{1,0:T(8,128)S(1)} %get-tuple-element.47.row_real, ...), custom_call_target="tpu_custom_call", output_to_operand_aliasing={{0}: (3, {}), {1}: (4, {}), {2}: (5, {}), {3}: (6, {})} | custom-call | tf_op jit(solution)/shard_map/pallas_call | solution.py:639
  15.1 0.0 collective-permute-done.across
  15.2 0.0 copy-done
  15.2 0.1 shard_map.71
  15.2 1.5 %collective-permute-start.1 = (bf16[192,1152]{1,0:T(8,128)(2,1)S(1)}, bf16[192,1152]{1,0:T(8,128)(2,1)S(1)}, u32[]{:S(2)}, u32[]{:S(2)}) collective-permute-start(bf16[192,1152]{1,0:T(8,128)(2,1)S(1)} %shard_map.71), channel_id=1, source_target_pairs={{0,2},{2,0},{4,6},{6,4},{8,10},{10,8},{12,14},{14,12},{16,18},{18,... | collective-permute-start | bytes 1327112 | tf_op jit(solution)/shard_map/ppermute | solution.py:700
  16.8 0.0 collective-permute-done.5.corner
  16.8 0.0 collective-permute-done.3.outer
  16.8 0.0 copy-start.1
  16.8 3.0 %shard_map.74 = (f32[384,1152]{1,0:T(8,128)S(1)}, bf16[2,384,1152]{2,1,0:T(8,128)(2,1)S(1)}, bf16[2,384,1152]{2,1,0:T(8,128)(2,1)S(1)}, bf16[2,128,1152]{2,1,0:T(8,128)(2,1)S(1)}) custom-call(bf16[2,128,2,1024]{3,2,1,0:T(2,128)(2,1)S(1)} %copy-done, bf16[96,2,1024]{2,1,0:T(2,128)(2,1)S(1)} %collective-permute-done.3.outer, ...), custom_call_target="tpu_custom_call" | custom-call | flops 2400000000 | tf_op jit(solution)/shard_map/pallas_call | solution.py:639
  19.8 0.0 collective-permute-done.6.measured_got
  19.8 0.0 copy-done.1
  19.8 2.1 %shard_map.75 = (bf16[2,256,1152]{2,1,0:T(8,128)(2,1)S(1)}, f32[384,1280]{1,0:T(8,128)S(1)}, bf16[768,1024]{1,0:T(8,128)(2,1)S(1)}, bf16[192,1024]{1,0:T(8,128)(2,1)S(1)}) custom-call(f32[384,1152]{1,0:T(8,128)S(1)} %get-tuple-element.57.far_slab.far_slab_in, bf16[2,384,1152]{2,1,0:T(8,128)(2,1)S(1)} %get-tuple-element.58.field.field_in, ...), custom_call_target="tpu_custom_call" | custom-call | flops 1000000000 | tf_op jit(solution)/shard_map/pallas_call | solution.py:639
  21.9 3.7 %collective-permute-start.9 = (bf16[192,1024]{1,0:T(8,128)(2,1)S(1)}, bf16[192,1024]{1,0:T(8,128)(2,1)S(1)}, u32[]{:S(2)}, u32[]{:S(2)}) collective-permute-start(bf16[192,1024]{1,0:T(8,128)(2,1)S(1)} %get-tuple-element.63.sent), channel_id=1, source_target_pairs={{2,4},{4,2},{6,8},{8,6},{10,12},{12,10},{14,16},{16,14},{18,20},{2... | collective-permute-start | bytes 1179656 | tf_op jit(solution)/shard_map/ppermute | solution.py:730
  25.6 0.0 collective-permute-done.2.measured_got
  25.6 0.4 %shard_map.76.measured = f32[2,128,1152]{2,1,0:T(8,128)S(1)} custom-call(bf16[1,128,2,2048]{3,2,1,0:T(2,128)(2,1)S(1)} %copy-done.1, bf16[64,2,1152]{2,1,0:T(2,128)(2,1)S(1)} %collective-permute-done.2.measured_got, bf16[128,128]{1,0:T(8,128)(2,1)S(1)} %get-tuple-element.45.split_meas, bf16[192,1024]{1,0:T(8,128)(2,1)S(1)} %get-tuple-element.63.sent), custom_call_target="tpu_custom_call" | custom-call | flops 4000000000 | tf_op jit(solution)/shard_map/pallas_call | solution.py:639
  26.0 0.0 collective-permute-done.1.inner
  26.0 5.0 %shard_map.77 = (f32[384,1152]{1,0:T(8,128)S(1)}, bf16[2,384,1152]{2,1,0:T(8,128)(2,1)S(1)}, bf16[2,384,1152]{2,1,0:T(8,128)(2,1)S(1)}, bf16[2,256,1152]{2,1,0:T...) custom-call(bf16[2,128,2,1024]{3,2,1,0:T(2,128)(2,1)S(1)} %copy-done, ...), custom_call_target="tpu_custom_call", output_to_operand_aliasing={{0}: (4, {}), {1}: (5, {}), {2}: (6, {}), {3}: (7, {}), {4}... | custom-call | tf_op jit(solution)/shard_map/pallas_call | solution.py:639
  31.0 0.1 collective-permute-start.7
  31.1 0.5 %collective-permute-start.8 = (bf16[64,1024]{1,0:T(8,128)(2,1)S(1)}, bf16[64,1024]{1,0:T(8,128)(2,1)S(1)}, u32[]{:S(2)}, u32[]{:S(2)}) collective-permute-start(bf16[64,1024]{1,0:T(8,128)(2,1)S(1)} %get-tuple-element.75), channel_id=1, source_target_pairs={{0,2},{2,0},{4,6},{6,4},{8,10},{10,8},{12,14},{14,12},{16,18},{18,... | collective-permute-start | bytes 393224 | tf_op jit(solution)/shard_map/ppermute | solution.py:751
  31.6 0.6 %shard_map.78 = (f32[256,1024]{1,0:T(8,128)S(1)}, f32[2,128,1024]{2,1,0:T(8,128)S(1)}) custom-call(bf16[768,1024]{1,0:T(8,128)(2,1)S(1)} %get-tuple-element.70.into, f32[384,1280]{1,0:T(8,128)S(1)} %get-tuple-element.71.far_sum, bf16[512,768]{1,0:T(8,128)(2,1)S(1)} %get-tuple-element.69.row_near_adj), custom_call_target="tpu_custom_call" | custom-call | tf_op jit(solution)/shard_map/pallas_call | solution.py:639
  32.2 0.6 %collective-permute-done.8.inner_far = bf16[64,1024]{1,0:T(8,128)(2,1)S(1)} collective-permute-done((bf16[64,1024]{1,0:T(8,128)(2,1)S(1)}, bf16[64,1024]{1,0:T(8,128)(2,1)S(1)}, u32[]{:S(2)}, u32[]{:S(2)}) %collective-permute-start.8) | collective-permute-done | bytes 131104 | tf_op jit(solution)/shard_map/ppermute | solution.py:751
  32.8 0.0 collective-permute-done.7.inner
  32.8 1.2 %shard_map.79 = (f32[128,2,1024]{2,1,0:T(2,128)}, f32[128,2,1024]{2,1,0:T(2,128)}) custom-call(f32[256,1024]{1,0:T(8,128)S(1)} %get-tuple-element.72.near_sum, f32[2,128,1024]{2,1,0:T(8,128)S(1)} %get-tuple-element.73.far_sum, bf16[128,1024]{1,0:T(8,128)(2,1)S(1)} %collective-permute-done.7.inner, bf16[64,1024]{1,0:T(8,128)(2,1)S(1)} %collective-permute-done.8.inner_far), custom_call_target="tpu_custom_call" | custom-call | tf_op jit(solution)/shard_map/pallas_call | solution.py:639
  34.0 1.2 %collective-permute-done.9.outer = bf16[192,1024]{1,0:T(8,128)(2,1)S(1)} collective-permute-done((bf16[192,1024]{1,0:T(8,128)(2,1)S(1)}, bf16[192,1024]{1,0:T(8,128)(2,1)S(1)}, u32[]{:S(2)}, u32[]{:S(2)}) %collective-permute-start.9) | collective-permute-done | bytes 393248 | tf_op jit(solution)/shard_map/ppermute | solution.py:730
  35.2 1.0 %shard_map.80 = (f32[128,2,1024]{2,1,0:T(2,128)}, f32[128,2,1024]{2,1,0:T(2,128)}) custom-call(f32[128,2,1024]{2,1,0:T(2,128)} %get-tuple-element.76.near_in, f32[128,2,1024]{2,1,0:T(2,128)} %get-tuple-element.77.far_in, f32[256,1024]{1,0:T(8,128)S(1)} %get-tuple-element.72.near_sum, ...), custom_call_target="tpu_custom_call", output_to_operand_aliasing={{0}: (0, {}), {1}: (1, {})} | custom-call | tf_op jit(solution)/shard_map/pallas_call | solution.py:639
Async XLA Ops:
  0.6 12.9 %copy-start.2 = (bf16[2,65]{1,0:T(2,128)(2,1)S(1)}, bf16[2,65]{1,0:T(2,128)(2,1)}, u32[]{:S(2)}) copy-start(bf16[2,65]{1,0:T(2,128)(2,1)} %taps.1) | copy-start | bytes 784
  1.8 15.0 %collective-permute-start.3 = (bf16[96,2,1024]{2,1,0:T(2,128)(2,1)S(1)}, bf16[96,2,1024]{2,1,0:T(2,128)(2,1)S(1)}, u32[]{:S(2)}, u32[]{:S(2)}) collective-permute-start(bf16[96,2,1024]{2,1,0:T(2,128)(2,1)S(1)} %get-tuple-element.46), channel_id=1, source_target_pairs={{2,4},{4,2},{6,8},{8,6},{10,12},{12,10},{14,16},{16,14},{18,20},{2... | collective-permute-start | bytes 1179656 | tf_op jit(solution)/shard_map/ppermute | solution.py:675
  6.2 3.9 %collective-permute-start.4 = (bf16[208,128]{1,0:T(8,128)(2,1)S(1)}, bf16[208,128]{1,0:T(8,128)(2,1)S(1)}, u32[]{:S(2)}, u32[]{:S(2)}) collective-permute-start(bf16[208,128]{1,0:T(8,128)(2,1)S(1)} %shard_map.69.across), channel_id=1, source_target_pairs={{0,1},{1,0},{2,3},{3,2},{4,5},{5,4},{6,7},{7,6},{8,9},{9,8},{10,11... | collective-permute-start | bytes 159752 | tf_op jit(solution)/shard_map/ppermute | solution.py:676
  7.5 7.7 %copy-start = (bf16[2,128,2,1024]{3,2,1,0:T(2,128)(2,1)S(1)}, bf16[2,128,2,1024]{3,2,1,0:T(2,128)(2,1)}, u32[]{:S(2)}) copy-start(bf16[2,128,2,1024]{3,2,1,0:T(2,128)(2,1)} %slices.7) | copy-start | bytes 3145732
  7.5 7.7 %collective-permute-start = (bf16[320,128]{1,0:T(8,128)(2,1)S(1)}, bf16[320,128]{1,0:T(8,128)(2,1)S(1)}, u32[]{:S(2)}, u32[]{:S(2)}) collective-permute-start(bf16[320,128]{1,0:T(8,128)(2,1)S(1)} %get-tuple-element.40.sent), channel_id=1, source_target_pairs={{0,1},{1,0},{2,3},{3,2},{4,5},{5,4},{6,7},{7,6},{8,9},{9,8},{10,11... | collective-permute-start | bytes 245768 | tf_op jit(solution)/shard_map/ppermute | solution.py:677
  8.9 11.0 %collective-permute-start.6 = (bf16[64,2,1152]{2,1,0:T(2,128)(2,1)S(1)}, bf16[64,2,1152]{2,1,0:T(2,128)(2,1)S(1)}, u32[]{:S(2)}, u32[]{:S(2)}) collective-permute-start(bf16[64,2,1152]{2,1,0:T(2,128)(2,1)S(1)} %get-tuple-element.60), channel_id=1, source_target_pairs={{0,1},{1,0},{2,3},{3,2},{4,5},{5,4},{6,7},{7,6},{8,9},{9,8},{10,11... | collective-permute-start | bytes 884744 | tf_op jit(solution)/shard_map/ppermute | solution.py:683
  10.1 6.7 %collective-permute-start.5 = (bf16[208,128]{1,0:T(8,128)(2,1)S(1)}, bf16[208,128]{1,0:T(8,128)(2,1)S(1)}, u32[]{:S(2)}, u32[]{:S(2)}) collective-permute-start(bf16[208,128]{1,0:T(8,128)(2,1)S(1)} %collective-permute-done.4.across.early), channel_id=1, source_target_pairs={{2,4},{4,2},{6,8},{8,6},{10,12},{12,10},{14,16},{16,14},{18,20},{2... | collective-permute-start | bytes 159752 | tf_op jit(solution)/shard_map/ppermute | solution.py:678
  12.8 12.7 %collective-permute-start.2 = (bf16[64,2,1152]{2,1,0:T(2,128)(2,1)S(1)}, bf16[64,2,1152]{2,1,0:T(2,128)(2,1)S(1)}, u32[]{:S(2)}, u32[]{:S(2)}) collective-permute-start(bf16[64,2,1152]{2,1,0:T(2,128)(2,1)S(1)} %get-tuple-element.44), channel_id=1, source_target_pairs={{0,1},{1,0},{2,3},{3,2},{4,5},{5,4},{6,7},{7,6},{8,9},{9,8},{10,11... | collective-permute-start | bytes 884744 | tf_op jit(solution)/shard_map/ppermute | solution.py:684
  15.2 10.8 %collective-permute-start.1 = (bf16[192,1152]{1,0:T(8,128)(2,1)S(1)}, bf16[192,1152]{1,0:T(8,128)(2,1)S(1)}, u32[]{:S(2)}, u32[]{:S(2)}) collective-permute-start(bf16[192,1152]{1,0:T(8,128)(2,1)S(1)} %shard_map.71), channel_id=1, source_target_pairs={{0,2},{2,0},{4,6},{6,4},{8,10},{10,8},{12,14},{14,12},{16,18},{18,... | collective-permute-start | bytes 1327112 | tf_op jit(solution)/shard_map/ppermute | solution.py:700
  16.8 3.1 %copy-start.1 = (bf16[1,128,2,2048]{3,2,1,0:T(2,128)(2,1)S(1)}, bf16[1,128,2,2048]{3,2,1,0:T(2,128)(2,1)}, u32[]{:S(2)}) copy-start(bf16[1,128,2,2048]{3,2,1,0:T(2,128)(2,1)} %measured.5) | copy-start | bytes 3145732
  21.9 13.3 %collective-permute-start.9 = (bf16[192,1024]{1,0:T(8,128)(2,1)S(1)}, bf16[192,1024]{1,0:T(8,128)(2,1)S(1)}, u32[]{:S(2)}, u32[]{:S(2)}) collective-permute-start(bf16[192,1024]{1,0:T(8,128)(2,1)S(1)} %get-tuple-element.63.sent), channel_id=1, source_target_pairs={{2,4},{4,2},{6,8},{8,6},{10,12},{12,10},{14,16},{16,14},{18,20},{2... | collective-permute-start | bytes 1179656 | tf_op jit(solution)/shard_map/ppermute | solution.py:730
  31.0 1.8 %collective-permute-start.7 = (bf16[128,1024]{1,0:T(8,128)(2,1)S(1)}, bf16[128,1024]{1,0:T(8,128)(2,1)S(1)}, u32[]{:S(2)}, u32[]{:S(2)}) collective-permute-start(bf16[128,1024]{1,0:T(8,128)(2,1)S(1)} %get-tuple-element.74), channel_id=1, source_target_pairs={{0,2},{2,0},{4,6},{6,4},{8,10},{10,8},{12,14},{14,12},{16,18},{18,... | collective-permute-start | bytes 786440 | tf_op jit(solution)/shard_map/ppermute | solution.py:750
  31.1 1.7 %collective-permute-start.8 = (bf16[64,1024]{1,0:T(8,128)(2,1)S(1)}, bf16[64,1024]{1,0:T(8,128)(2,1)S(1)}, u32[]{:S(2)}, u32[]{:S(2)}) collective-permute-start(bf16[64,1024]{1,0:T(8,128)(2,1)S(1)} %get-tuple-element.75), channel_id=1, source_target_pairs={{0,2},{2,0},{4,6},{6,4},{8,10},{10,8},{12,14},{14,12},{16,18},{18,... | collective-permute-start | bytes 393224 | tf_op jit(solution)/shard_map/ppermute | solution.py:751

commit v6 on v5

--- a/solution.py
+++ b/solution.py
@@ -277,7 +277,7 @@
         ref[self.at(1, top), lanes] = both[self.count :]
 
 
-def column_step(tiles, index, col_taps, load, store, count, limit=512):
+def column_step(tiles, index, col_taps, load, store, count, limit=256):
     groups, room = [], 0
     for j in range(count):
         which = index(j)
@@ -297,22 +297,26 @@
 
 
 def forward_rows(
-    tiles, part, leave, near_slab, near_lanes, far_slab, row_near, row_half, col_taps, waves, entry, field, after, narrow, leaving,
+    tiles, part, leave, near_slab, near_first, far_slab, row_near, row_half, col_taps, waves, entry, field, after, narrow, leaving,
 ):
     mid, width = part.parts, tiles.width
     size = part.count
-    for at, lanes in lane_chunks(width):
-        here = slice(at, at + lanes)
+    block = near_slab.shape[0] // 2 - size
+    for top in range(0, size, block):
+        rows = Rows(part.first + top, block, mid)
+        lefts = pl.ds(pl.multiple_of(near_first + 2 * top, LANES), 4 * block)
         left = jnp.concatenate(
-            [row_near[part.at(comp, member * 2 * mid), near_lanes] for member in range(2) for comp in range(2)], axis=0
+            [row_near[rows.at(comp, member * 2 * mid), lefts] for member in range(2) for comp in range(2)], axis=0
         )
-        result = dot(left, near_slab[:, here])
-        for member in range(2):
-            re = result[2 * member * size : (2 * member + 1) * size]
-            im = result[(2 * member + 1) * size : (2 * member + 2) * size]
-            vr, vi = waves[2 * member : 2 * member + 1, here], waves[2 * member + 1 : 2 * member + 2, here]
-            entry[member, :size, here] = (re * vr - im * vi).astype(BF16)
-            entry[member, size:, here] = (re * vi + im * vr).astype(BF16)
+        for at, lanes in lane_chunks(width):
+            here = slice(at, at + lanes)
+            result = dot(left, near_slab[2 * top : 2 * top + 4 * block, here])
+            for member in range(2):
+                re = result[2 * member * block : (2 * member + 1) * block]
+                im = result[(2 * member + 1) * block : (2 * member + 2) * block]
+                vr, vi = waves[2 * member : 2 * member + 1, here], waves[2 * member + 1 : 2 * member + 2, here]
+                entry[member, top : top + block, here] = (re * vr - im * vi).astype(BF16)
+                entry[member, size + top : size + top + block, here] = (re * vi + im * vr).astype(BF16)
     entry[:, :, width:] = entry[:, :, :LANES]
 
     def load(j):
@@ -431,8 +435,9 @@
 
 
 def split_rows(tiles, part, split, far_raw, far_slab, half):
-    for j in range(tiles.count):
-        part.write(far_slab, tile(j), dot(split[...], far_raw[:, pair(j)])[:, half : half + LANES])
+    for at, lanes in lane_chunks(tiles.width):
+        window = far_raw[:, at : at + lanes + LANES]
+        part.write(far_slab, slice(at, at + lanes), dot(split[...], window[:, half : half + lanes]))
 
 
 def far_margin(tiles, half, part, far_sum, sums):
@@ -474,9 +479,8 @@
     part = Rows(parity * (rows // 2), rows, mid)
     source = Rows(parity * (rows // 2), rows // 2, mid)
     split_rows(tiles, part, split_far, far_raw, far_slab, half)
-    lanes = pl.ds(pl.multiple_of(parity * 4 * half, LANES), near_raw.shape[0])
     forward_rows(
-        tiles, part, source, near_raw, lanes, far_slab, row_near, row_half, col_taps, waves, entry, field, after,
+        tiles, part, source, near_raw, parity * 4 * half, far_slab, row_near, row_half, col_taps, waves, entry, field, after,
         narrow, leaving,
     )
 
@@ -550,9 +554,8 @@
     far_raw[:, tiles.width :] = far_raw[:, :LANES]
 
     split_rows(tiles, part, split_meas, far_raw, far_slab, half)
-    lanes = pl.ds(pl.multiple_of(other * 2 * rows, LANES), near_raw.shape[0])
     forward_rows(
-        tiles, part, source, near_raw, lanes, far_slab, row_near, row_half, col_taps, waves, entry, field, after,
+        tiles, part, source, near_raw, other * 2 * rows, far_slab, row_near, row_half, col_taps, waves, entry, field, after,
         narrow, leaving,
     )
     residue_rows(

time: 36.6 us -> 36.1 us (0.986)
  Pallas kernels: 17.3 us -> 16.7 us
    pallas_call x13, Pallas kernels: 17.3 us -> 16.7 us  [call(): pl.pallas_call(kernel, out_shape=[jax.ShapeDtypeStruct(shape, dtype) for...]
  transfers between devices with their start and end apart: 10 -> 10, of which waited for: 2 -> 2; matrix products, arithmetic and copies ran while one was open for 0% -> 0% of each run, Pallas kernels for 42% -> 41%
where the time goes in v6:
time: 36.1 us; the launch traced here: 35.9 us
  Pallas kernels  16.7 us (46%)
  starting transfers between devices  15.7 us (43%)
  waiting for transfers between devices  1.86 us (5%)
  between operations  1.61 us (4%)
    pallas_call x13, Pallas kernels, call(): pl.pallas_call(kernel, out_shape=[jax.ShapeDtypeStruct(shape, dtype) for...  16.7 us
    ppermute x1, starting transfers between devices, columns_local(): outer_got = lax.ppermute(outer, 'rows', outer_pairs)  3.71 us
    ppermute x1, starting transfers between devices, columns_local(): outer_back = lax.ppermute(outer_sums, 'rows', outer_pairs)  3.68 us
    ppermute x1, starting transfers between devices, columns_local(): corner_got = lax.ppermute(early_got, 'rows', outer_pairs)  2.75 us
    ppermute x1, starting transfers between devices, columns_local(): inner_got = lax.ppermute(inner, 'rows', inner_pairs)  1.51 us
    ppermute x1, waiting for transfers between devices, columns_local(): outer_back = lax.ppermute(outer_sums, 'rows', outer_pairs)  1.27 us
    ppermute x1, starting transfers between devices, columns_local(): early_got = lax.ppermute(early, 'ang', side_pairs)  1.25 us
    ppermute x1, starting transfers between devices, columns_local(): outer_meas = lax.ppermute(meas_outer, 'ang', side_pairs)  1.22 us
  transfers between devices with their start and end apart: 10, of which 2 were waited for; matrix products, arithmetic and copies ran while one was open for 0% of the time, Pallas kernels for 41%

profile of v6, /device:TPU:17, one launch (start us, length us, event | category | flops | bytes accessed | tf_op | source)
XLA Modules:
  0.0 35.9 jit_solution(13028896942316088441)
XLA Ops:
  0.6 0.0 copy-start.2
  0.6 1.1 %shard_map.68 = (bf16[96,2,1024]{2,1,0:T(2,128)(2,1)S(1)}, bf16[208,128]{1,0:T(8,128)(2,1)S(1)}, bf16[320,128]{1,0:T(8,128)(2,1)S(1)}, f32[2,128]{1,0:T(2,128)S(1)}) custom-call(bf16[2,128,2,1024]{3,2,1,0:T(2,128)(2,1)} %slices.7, f32[2,128]{1,0:T(2,128)} %bitcast.1), custom_call_target="tpu_custom_call" | custom-call | tf_op jit(solution)/shard_map/pallas_call | solution.py:642
  1.8 3.7 %collective-permute-start.3 = (bf16[96,2,1024]{2,1,0:T(2,128)(2,1)S(1)}, bf16[96,2,1024]{2,1,0:T(2,128)(2,1)S(1)}, u32[]{:S(2)}, u32[]{:S(2)}) collective-permute-start(bf16[96,2,1024]{2,1,0:T(2,128)(2,1)S(1)} %get-tuple-element.46), channel_id=1, source_target_pairs={{2,4},{4,2},{6,8},{8,6},{10,12},{12,10},{14,16},{16,14},{18,20},{2... | collective-permute-start | bytes 1179656 | tf_op jit(solution)/shard_map/ppermute | solution.py:678
  6.1 0.1 shard_map.69.across
  6.2 1.2 %collective-permute-start.4 = (bf16[208,128]{1,0:T(8,128)(2,1)S(1)}, bf16[208,128]{1,0:T(8,128)(2,1)S(1)}, u32[]{:S(2)}, u32[]{:S(2)}) collective-permute-start(bf16[208,128]{1,0:T(8,128)(2,1)S(1)} %shard_map.69.across), channel_id=1, source_target_pairs={{0,1},{1,0},{2,3},{3,2},{4,5},{5,4},{6,7},{7,6},{8,9},{9,8},{10,11... | collective-permute-start | bytes 159752 | tf_op jit(solution)/shard_map/ppermute | solution.py:679
  7.5 0.0 copy-start
  7.5 0.3 collective-permute-start
  7.7 1.1 %shard_map.72 = (bf16[64,2,1152]{2,1,0:T(2,128)(2,1)S(1)}, bf16[64,2,1152]{2,1,0:T(2,128)(2,1)S(1)}) custom-call(bf16[1,128,2,2048]{3,2,1,0:T(2,128)(2,1)} %measured.5, bf16[320,128]{1,0:T(8,128)(2,1)S(1)} %get-tuple-element.40.sent), custom_call_target="tpu_custom_call" | custom-call | tf_op jit(solution)/shard_map/pallas_call | solution.py:642
  8.9 1.2 %collective-permute-start.6 = (bf16[64,2,1152]{2,1,0:T(2,128)(2,1)S(1)}, bf16[64,2,1152]{2,1,0:T(2,128)(2,1)S(1)}, u32[]{:S(2)}, u32[]{:S(2)}) collective-permute-start(bf16[64,2,1152]{2,1,0:T(2,128)(2,1)S(1)} %get-tuple-element.60), channel_id=1, source_target_pairs={{0,1},{1,0},{2,3},{3,2},{4,5},{5,4},{6,7},{7,6},{8,9},{9,8},{10,11... | collective-permute-start | bytes 884744 | tf_op jit(solution)/shard_map/ppermute | solution.py:686
  10.1 0.0 collective-permute-done.4.across.early
  10.1 2.7 %collective-permute-start.5 = (bf16[208,128]{1,0:T(8,128)(2,1)S(1)}, bf16[208,128]{1,0:T(8,128)(2,1)S(1)}, u32[]{:S(2)}, u32[]{:S(2)}) collective-permute-start(bf16[208,128]{1,0:T(8,128)(2,1)S(1)} %collective-permute-done.4.across.early), channel_id=1, source_target_pairs={{2,4},{4,2},{6,8},{8,6},{10,12},{12,10},{14,16},{16,14},{18,20},{2... | collective-permute-start | bytes 159752 | tf_op jit(solution)/shard_map/ppermute | solution.py:681
  12.8 0.7 %collective-permute-start.2 = (bf16[64,2,1152]{2,1,0:T(2,128)(2,1)S(1)}, bf16[64,2,1152]{2,1,0:T(2,128)(2,1)S(1)}, u32[]{:S(2)}, u32[]{:S(2)}) collective-permute-start(bf16[64,2,1152]{2,1,0:T(2,128)(2,1)S(1)} %get-tuple-element.44), channel_id=1, source_target_pairs={{0,1},{1,0},{2,3},{3,2},{4,5},{5,4},{6,7},{7,6},{8,9},{9,8},{10,11... | collective-permute-start | bytes 884744 | tf_op jit(solution)/shard_map/ppermute | solution.py:687
  13.6 0.0 copy-done.2
  13.6 1.1 %shard_map.70 = (f32[192,512]{1,0:T(8,128)S(1)}, f32[192,512]{1,0:T(8,128)S(1)}, bf16[128,256]{1,0:T(8,128)(2,1)S(1)}, bf16[256,128]{1,0:T(8,128)(2,1)S(1)}, bf1...) custom-call(bf16[2,65]{1,0:T(2,128)(2,1)S(1)} %copy-done.2, ...), custom_call_target="tpu_custom_call" | custom-call | tf_op jit(solution)/shard_map/pallas_call | solution.py:642
  14.7 0.5 %shard_map.73 = (bf16[768,512]{1,0:T(8,128)(2,1)S(1)}, bf16[512,768]{1,0:T(8,128)(2,1)S(1)}, bf16[256,128]{1,0:T(8,128)(2,1)S(1)}, f32[8,1152]{1,0:T(8,128)S(1)}) custom-call(f32[192,512]{1,0:T(8,128)S(1)} %get-tuple-element.47.row_real, ...), custom_call_target="tpu_custom_call", output_to_operand_aliasing={{0}: (3, {}), {1}: (4, {}), {2}: (5, {}), {3}: (6, {})} | custom-call | tf_op jit(solution)/shard_map/pallas_call | solution.py:642
  15.1 0.0 collective-permute-done.across
  15.2 0.0 copy-done
  15.2 0.1 shard_map.71
  15.2 1.5 %collective-permute-start.1 = (bf16[192,1152]{1,0:T(8,128)(2,1)S(1)}, bf16[192,1152]{1,0:T(8,128)(2,1)S(1)}, u32[]{:S(2)}, u32[]{:S(2)}) collective-permute-start(bf16[192,1152]{1,0:T(8,128)(2,1)S(1)} %shard_map.71), channel_id=1, source_target_pairs={{0,2},{2,0},{4,6},{6,4},{8,10},{10,8},{12,14},{14,12},{16,18},{18,... | collective-permute-start | bytes 1327112 | tf_op jit(solution)/shard_map/ppermute | solution.py:703
  16.8 0.0 collective-permute-done.5.corner
  16.8 0.0 collective-permute-done.3.outer
  16.8 0.0 copy-start.1
  16.8 2.6 %shard_map.74 = (f32[384,1152]{1,0:T(8,128)S(1)}, bf16[2,384,1152]{2,1,0:T(8,128)(2,1)S(1)}, bf16[2,384,1152]{2,1,0:T(8,128)(2,1)S(1)}, bf16[2,128,1152]{2,1,0:T(8,128)(2,1)S(1)}) custom-call(bf16[2,128,2,1024]{3,2,1,0:T(2,128)(2,1)S(1)} %copy-done, bf16[96,2,1024]{2,1,0:T(2,128)(2,1)S(1)} %collective-permute-done.3.outer, ...), custom_call_target="tpu_custom_call" | custom-call | flops 2400000000 | tf_op jit(solution)/shard_map/pallas_call | solution.py:642
  19.4 0.0 collective-permute-done.6.measured_got
  19.4 0.0 copy-done.1
  19.4 2.0 %shard_map.75 = (bf16[2,256,1152]{2,1,0:T(8,128)(2,1)S(1)}, f32[384,1280]{1,0:T(8,128)S(1)}, bf16[768,1024]{1,0:T(8,128)(2,1)S(1)}, bf16[192,1024]{1,0:T(8,128)(2,1)S(1)}) custom-call(f32[384,1152]{1,0:T(8,128)S(1)} %get-tuple-element.57.far_slab.far_slab_in, bf16[2,384,1152]{2,1,0:T(8,128)(2,1)S(1)} %get-tuple-element.58.field.field_in, ...), custom_call_target="tpu_custom_call" | custom-call | flops 1000000000 | tf_op jit(solution)/shard_map/pallas_call | solution.py:642
  21.5 3.7 %collective-permute-start.9 = (bf16[192,1024]{1,0:T(8,128)(2,1)S(1)}, bf16[192,1024]{1,0:T(8,128)(2,1)S(1)}, u32[]{:S(2)}, u32[]{:S(2)}) collective-permute-start(bf16[192,1024]{1,0:T(8,128)(2,1)S(1)} %get-tuple-element.63.sent), channel_id=1, source_target_pairs={{2,4},{4,2},{6,8},{8,6},{10,12},{12,10},{14,16},{16,14},{18,20},{2... | collective-permute-start | bytes 1179656 | tf_op jit(solution)/shard_map/ppermute | solution.py:733
  25.1 0.0 collective-permute-done.2.measured_got
  25.2 0.4 %shard_map.76.measured = f32[2,128,1152]{2,1,0:T(8,128)S(1)} custom-call(bf16[1,128,2,2048]{3,2,1,0:T(2,128)(2,1)S(1)} %copy-done.1, bf16[64,2,1152]{2,1,0:T(2,128)(2,1)S(1)} %collective-permute-done.2.measured_got, bf16[128,128]{1,0:T(8,128)(2,1)S(1)} %get-tuple-element.45.split_meas, bf16[192,1024]{1,0:T(8,128)(2,1)S(1)} %get-tuple-element.63.sent), custom_call_target="tpu_custom_call" | custom-call | flops 4000000000 | tf_op jit(solution)/shard_map/pallas_call | solution.py:642
  25.6 0.0 collective-permute-done.1.inner
  25.6 4.9 %shard_map.77 = (f32[384,1152]{1,0:T(8,128)S(1)}, bf16[2,384,1152]{2,1,0:T(8,128)(2,1)S(1)}, bf16[2,384,1152]{2,1,0:T(8,128)(2,1)S(1)}, bf16[2,256,1152]{2,1,0:T...) custom-call(bf16[2,128,2,1024]{3,2,1,0:T(2,128)(2,1)S(1)} %copy-done, ...), custom_call_target="tpu_custom_call", output_to_operand_aliasing={{0}: (4, {}), {1}: (5, {}), {2}: (6, {}), {3}: (7, {}), {4}... | custom-call | tf_op jit(solution)/shard_map/pallas_call | solution.py:642
  30.5 0.1 collective-permute-start.7
  30.6 0.5 %collective-permute-start.8 = (bf16[64,1024]{1,0:T(8,128)(2,1)S(1)}, bf16[64,1024]{1,0:T(8,128)(2,1)S(1)}, u32[]{:S(2)}, u32[]{:S(2)}) collective-permute-start(bf16[64,1024]{1,0:T(8,128)(2,1)S(1)} %get-tuple-element.75), channel_id=1, source_target_pairs={{0,2},{2,0},{4,6},{6,4},{8,10},{10,8},{12,14},{14,12},{16,18},{18,... | collective-permute-start | bytes 393224 | tf_op jit(solution)/shard_map/ppermute | solution.py:754
  31.1 0.6 %shard_map.78 = (f32[256,1024]{1,0:T(8,128)S(1)}, f32[2,128,1024]{2,1,0:T(8,128)S(1)}) custom-call(bf16[768,1024]{1,0:T(8,128)(2,1)S(1)} %get-tuple-element.70.into, f32[384,1280]{1,0:T(8,128)S(1)} %get-tuple-element.71.far_sum, bf16[512,768]{1,0:T(8,128)(2,1)S(1)} %get-tuple-element.69.row_near_adj), custom_call_target="tpu_custom_call" | custom-call | tf_op jit(solution)/shard_map/pallas_call | solution.py:642
  31.7 0.6 %collective-permute-done.8.inner_far = bf16[64,1024]{1,0:T(8,128)(2,1)S(1)} collective-permute-done((bf16[64,1024]{1,0:T(8,128)(2,1)S(1)}, bf16[64,1024]{1,0:T(8,128)(2,1)S(1)}, u32[]{:S(2)}, u32[]{:S(2)}) %collective-permute-start.8) | collective-permute-done | bytes 131104 | tf_op jit(solution)/shard_map/ppermute | solution.py:754
  32.3 0.0 collective-permute-done.7.inner
  32.3 1.2 %shard_map.79 = (f32[128,2,1024]{2,1,0:T(2,128)}, f32[128,2,1024]{2,1,0:T(2,128)}) custom-call(f32[256,1024]{1,0:T(8,128)S(1)} %get-tuple-element.72.near_sum, f32[2,128,1024]{2,1,0:T(8,128)S(1)} %get-tuple-element.73.far_sum, bf16[128,1024]{1,0:T(8,128)(2,1)S(1)} %collective-permute-done.7.inner, bf16[64,1024]{1,0:T(8,128)(2,1)S(1)} %collective-permute-done.8.inner_far), custom_call_target="tpu_custom_call" | custom-call | tf_op jit(solution)/shard_map/pallas_call | solution.py:642
  33.5 1.3 %collective-permute-done.9.outer = bf16[192,1024]{1,0:T(8,128)(2,1)S(1)} collective-permute-done((bf16[192,1024]{1,0:T(8,128)(2,1)S(1)}, bf16[192,1024]{1,0:T(8,128)(2,1)S(1)}, u32[]{:S(2)}, u32[]{:S(2)}) %collective-permute-start.9) | collective-permute-done | bytes 393248 | tf_op jit(solution)/shard_map/ppermute | solution.py:733
  34.8 1.0 %shard_map.80 = (f32[128,2,1024]{2,1,0:T(2,128)}, f32[128,2,1024]{2,1,0:T(2,128)}) custom-call(f32[128,2,1024]{2,1,0:T(2,128)} %get-tuple-element.76.near_in, f32[128,2,1024]{2,1,0:T(2,128)} %get-tuple-element.77.far_in, f32[256,1024]{1,0:T(8,128)S(1)} %get-tuple-element.72.near_sum, ...), custom_call_target="tpu_custom_call", output_to_operand_aliasing={{0}: (0, {}), {1}: (1, {})} | custom-call | tf_op jit(solution)/shard_map/pallas_call | solution.py:642
Async XLA Ops:
  0.6 12.9 %copy-start.2 = (bf16[2,65]{1,0:T(2,128)(2,1)S(1)}, bf16[2,65]{1,0:T(2,128)(2,1)}, u32[]{:S(2)}) copy-start(bf16[2,65]{1,0:T(2,128)(2,1)} %taps.1) | copy-start | bytes 784
  1.8 15.0 %collective-permute-start.3 = (bf16[96,2,1024]{2,1,0:T(2,128)(2,1)S(1)}, bf16[96,2,1024]{2,1,0:T(2,128)(2,1)S(1)}, u32[]{:S(2)}, u32[]{:S(2)}) collective-permute-start(bf16[96,2,1024]{2,1,0:T(2,128)(2,1)S(1)} %get-tuple-element.46), channel_id=1, source_target_pairs={{2,4},{4,2},{6,8},{8,6},{10,12},{12,10},{14,16},{16,14},{18,20},{2... | collective-permute-start | bytes 1179656 | tf_op jit(solution)/shard_map/ppermute | solution.py:678
  6.2 3.9 %collective-permute-start.4 = (bf16[208,128]{1,0:T(8,128)(2,1)S(1)}, bf16[208,128]{1,0:T(8,128)(2,1)S(1)}, u32[]{:S(2)}, u32[]{:S(2)}) collective-permute-start(bf16[208,128]{1,0:T(8,128)(2,1)S(1)} %shard_map.69.across), channel_id=1, source_target_pairs={{0,1},{1,0},{2,3},{3,2},{4,5},{5,4},{6,7},{7,6},{8,9},{9,8},{10,11... | collective-permute-start | bytes 159752 | tf_op jit(solution)/shard_map/ppermute | solution.py:679
  7.5 7.7 %copy-start = (bf16[2,128,2,1024]{3,2,1,0:T(2,128)(2,1)S(1)}, bf16[2,128,2,1024]{3,2,1,0:T(2,128)(2,1)}, u32[]{:S(2)}) copy-start(bf16[2,128,2,1024]{3,2,1,0:T(2,128)(2,1)} %slices.7) | copy-start | bytes 3145732
  7.5 7.7 %collective-permute-start = (bf16[320,128]{1,0:T(8,128)(2,1)S(1)}, bf16[320,128]{1,0:T(8,128)(2,1)S(1)}, u32[]{:S(2)}, u32[]{:S(2)}) collective-permute-start(bf16[320,128]{1,0:T(8,128)(2,1)S(1)} %get-tuple-element.40.sent), channel_id=1, source_target_pairs={{0,1},{1,0},{2,3},{3,2},{4,5},{5,4},{6,7},{7,6},{8,9},{9,8},{10,11... | collective-permute-start | bytes 245768 | tf_op jit(solution)/shard_map/ppermute | solution.py:680
  8.9 10.5 %collective-permute-start.6 = (bf16[64,2,1152]{2,1,0:T(2,128)(2,1)S(1)}, bf16[64,2,1152]{2,1,0:T(2,128)(2,1)S(1)}, u32[]{:S(2)}, u32[]{:S(2)}) collective-permute-start(bf16[64,2,1152]{2,1,0:T(2,128)(2,1)S(1)} %get-tuple-element.60), channel_id=1, source_target_pairs={{0,1},{1,0},{2,3},{3,2},{4,5},{5,4},{6,7},{7,6},{8,9},{9,8},{10,11... | collective-permute-start | bytes 884744 | tf_op jit(solution)/shard_map/ppermute | solution.py:686
  10.1 6.7 %collective-permute-start.5 = (bf16[208,128]{1,0:T(8,128)(2,1)S(1)}, bf16[208,128]{1,0:T(8,128)(2,1)S(1)}, u32[]{:S(2)}, u32[]{:S(2)}) collective-permute-start(bf16[208,128]{1,0:T(8,128)(2,1)S(1)} %collective-permute-done.4.across.early), channel_id=1, source_target_pairs={{2,4},{4,2},{6,8},{8,6},{10,12},{12,10},{14,16},{16,14},{18,20},{2... | collective-permute-start | bytes 159752 | tf_op jit(solution)/shard_map/ppermute | solution.py:681
  12.8 12.3 %collective-permute-start.2 = (bf16[64,2,1152]{2,1,0:T(2,128)(2,1)S(1)}, bf16[64,2,1152]{2,1,0:T(2,128)(2,1)S(1)}, u32[]{:S(2)}, u32[]{:S(2)}) collective-permute-start(bf16[64,2,1152]{2,1,0:T(2,128)(2,1)S(1)} %get-tuple-element.44), channel_id=1, source_target_pairs={{0,1},{1,0},{2,3},{3,2},{4,5},{5,4},{6,7},{7,6},{8,9},{9,8},{10,11... | collective-permute-start | bytes 884744 | tf_op jit(solution)/shard_map/ppermute | solution.py:687
  15.2 10.3 %collective-permute-start.1 = (bf16[192,1152]{1,0:T(8,128)(2,1)S(1)}, bf16[192,1152]{1,0:T(8,128)(2,1)S(1)}, u32[]{:S(2)}, u32[]{:S(2)}) collective-permute-start(bf16[192,1152]{1,0:T(8,128)(2,1)S(1)} %shard_map.71), channel_id=1, source_target_pairs={{0,2},{2,0},{4,6},{6,4},{8,10},{10,8},{12,14},{14,12},{16,18},{18,... | collective-permute-start | bytes 1327112 | tf_op jit(solution)/shard_map/ppermute | solution.py:703
  16.8 2.6 %copy-start.1 = (bf16[1,128,2,2048]{3,2,1,0:T(2,128)(2,1)S(1)}, bf16[1,128,2,2048]{3,2,1,0:T(2,128)(2,1)}, u32[]{:S(2)}) copy-start(bf16[1,128,2,2048]{3,2,1,0:T(2,128)(2,1)} %measured.5) | copy-start | bytes 3145732
  21.5 13.3 %collective-permute-start.9 = (bf16[192,1024]{1,0:T(8,128)(2,1)S(1)}, bf16[192,1024]{1,0:T(8,128)(2,1)S(1)}, u32[]{:S(2)}, u32[]{:S(2)}) collective-permute-start(bf16[192,1024]{1,0:T(8,128)(2,1)S(1)} %get-tuple-element.63.sent), channel_id=1, source_target_pairs={{2,4},{4,2},{6,8},{8,6},{10,12},{12,10},{14,16},{16,14},{18,20},{2... | collective-permute-start | bytes 1179656 | tf_op jit(solution)/shard_map/ppermute | solution.py:733
  30.5 1.8 %collective-permute-start.7 = (bf16[128,1024]{1,0:T(8,128)(2,1)S(1)}, bf16[128,1024]{1,0:T(8,128)(2,1)S(1)}, u32[]{:S(2)}, u32[]{:S(2)}) collective-permute-start(bf16[128,1024]{1,0:T(8,128)(2,1)S(1)} %get-tuple-element.74), channel_id=1, source_target_pairs={{0,2},{2,0},{4,6},{6,4},{8,10},{10,8},{12,14},{14,12},{16,18},{18,... | collective-permute-start | bytes 786440 | tf_op jit(solution)/shard_map/ppermute | solution.py:753
  30.6 1.7 %collective-permute-start.8 = (bf16[64,1024]{1,0:T(8,128)(2,1)S(1)}, bf16[64,1024]{1,0:T(8,128)(2,1)S(1)}, u32[]{:S(2)}, u32[]{:S(2)}) collective-permute-start(bf16[64,1024]{1,0:T(8,128)(2,1)S(1)} %get-tuple-element.75), channel_id=1, source_target_pairs={{0,2},{2,0},{4,6},{6,4},{8,10},{10,8},{12,14},{14,12},{16,18},{18,... | collective-permute-start | bytes 393224 | tf_op jit(solution)/shard_map/ppermute | solution.py:754

commit v7 on v6

--- a/solution.py
+++ b/solution.py
@@ -54,7 +54,7 @@
         copy.wait()
 
 
-def frequencies_kernel(table, chosen, early_in, early):
+def frequencies_kernel(table, chosen, early_in, measured, early):
     row = iota((16, LANES), 0)
     block = jnp.zeros((16, LANES), F32)
     entry = jnp.where(iota(table.shape, 1) == chosen[0], table[...], 0.0)
@@ -91,20 +91,17 @@
     return pl.ds(pl.multiple_of(2 * rows - 4 * half + other * (2 * rows - 4 * half), 16), 2 * half)
 
 
-def measured_kernel(measured, sent, outer, inner, sems):
-    size, cols = outer.shape[0], measured.shape[3] // 2
+def measured_kernel(measured, sent, outer, inner):
+    size, cols = outer.shape[0] // 2, measured.shape[3] // 2
     parity = lax.axis_index("rows") % 2
     side = lax.axis_index("ang")
-    copies = []
     for late, out in ((parity, outer), (1 - parity, inner)):
-        for frm, at, lanes in (((1 - side) * cols, 0, cols), (cols - (1 - side) * LANES, cols, LANES)):
-            here = pl.ds(pl.multiple_of(frm, LANES), lanes)
-            there = measured.at[0, pl.ds(late * size, size), :, here]
-            copies.append(pltpu.make_async_copy(there, out.at[:, :, at : at + lanes], sems.at[len(copies)]))
-    for copy in copies:
-        copy.start()
-    for copy in copies:
-        copy.wait()
+        rows = pl.ds(late * size, size)
+        for at, first, second in ((0, cols, 0), (cols, cols - LANES, cols)):
+            lanes = cols if at == 0 else LANES
+            left = measured[0, rows, :, first : first + lanes].reshape(2 * size, lanes)
+            right = measured[0, rows, :, second : second + lanes].reshape(2 * size, lanes)
+            out[:, at : at + lanes] = jnp.where(side == 0, left, right)
 
 
 def own_window(measured, late, at, size):
@@ -117,7 +114,7 @@
 
 
 def got_window(window, at, size):
-    return window[:, :, at : at + size].reshape(2 * window.shape[0], size)
+    return window[:, at : at + size]
 
 
 def skewed(base, count, stride):
@@ -673,15 +670,14 @@
         scratch=[((2, rows, 2, LANES), BF16), pltpu.SemaphoreType.DMA((4,))],
     )
     (early,) = call(
-        frequencies_kernel, [((edge + 16, LANES), BF16)], (table, chosen, early), scalars=(1,), aliases={2: 0},
+        frequencies_kernel, [((edge + 16, LANES), BF16)], (table, chosen, early, measured), scalars=(1,), aliases={2: 0},
     )
     outer_got = lax.ppermute(outer, "rows", outer_pairs)
     early_got = lax.ppermute(early, "ang", side_pairs)
     across_got = lax.ppermute(across, "ang", side_pairs)
     corner_got = lax.ppermute(early_got, "rows", outer_pairs)
     meas_outer, meas_inner = call(
-        measured_kernel, [((rows // 2, 2, width), BF16)] * 2, (measured, across), hbm=(0,), outside=(1,),
-        outs_outside=(0, 1), scratch=[pltpu.SemaphoreType.DMA((4,))],
+        measured_kernel, [((rows, width), BF16)] * 2, (measured, across), outside=(1,),
     )
     outer_meas = lax.ppermute(meas_outer, "ang", side_pairs)
     inner_meas = lax.ppermute(meas_inner, "ang", side_pairs)
@@ -911,8 +907,7 @@
         lax.axis_size("ang") == 2
         and lax.axis_size("rows") % 2 == 0
         and 2 * (taps - 1) == LANES
-        and rows >= taps - 1
-        and rows % LANES == 0
+        and rows == 2 * (taps - 1)
         and cols % (2 * LANES) == 0
     )
     run = columns_local if fits else local

time: 36.1 us -> 36.1 us (level)
  Pallas kernels: 16.7 us -> 15.8 us
  waiting for transfers between devices: 1.86 us -> 2.65 us
    pallas_call x13, Pallas kernels: 16.7 us -> 15.8 us  [call(): pl.pallas_call(kernel, out_shape=[jax.ShapeDtypeStruct(shape, dtype) for...]
    ppermute x1, waiting for transfers between devices: 0.01 us -> 0.78 us  [columns_local(): early_got = lax.ppermute(early, 'ang', side_pairs)]
    ppermute x1, starting transfers between devices: 0.73 us -> 1.28 us  [columns_local(): inner_meas = lax.ppermute(meas_inner, 'ang', side_pairs)]
    ppermute x1, starting transfers between devices: 2.75 us -> 2.37 us  [columns_local(): corner_got = lax.ppermute(early_got, 'rows', outer_pairs)]
  transfers between devices with their start and end apart: 10 -> 10, of which waited for: 2 -> 3; matrix products, arithmetic and copies ran while one was open for 0% -> 0% of each run, Pallas kernels for 41% -> 38%
where the time goes in v7:
time: 36.1 us; the launch traced here: 36 us
  starting transfers between devices  15.9 us (44%)
  Pallas kernels  15.8 us (44%)
  waiting for transfers between devices  2.65 us (7%)
  between operations  1.61 us (4%)
    pallas_call x13, Pallas kernels, call(): pl.pallas_call(kernel, out_shape=[jax.ShapeDtypeStruct(shape, dtype) for...  15.8 us
    ppermute x1, starting transfers between devices, columns_local(): outer_got = lax.ppermute(outer, 'rows', outer_pairs)  3.71 us
    ppermute x1, starting transfers between devices, columns_local(): outer_back = lax.ppermute(outer_sums, 'rows', outer_pairs)  3.67 us
    ppermute x1, starting transfers between devices, columns_local(): corner_got = lax.ppermute(early_got, 'rows', outer_pairs)  2.37 us
    ppermute x1, starting transfers between devices, columns_local(): inner_got = lax.ppermute(inner, 'rows', inner_pairs)  1.51 us
    ppermute x1, waiting for transfers between devices, columns_local(): outer_back = lax.ppermute(outer_sums, 'rows', outer_pairs)  1.28 us
    ppermute x1, starting transfers between devices, columns_local(): inner_meas = lax.ppermute(meas_inner, 'ang', side_pairs)  1.28 us
    ppermute x1, starting transfers between devices, columns_local(): outer_meas = lax.ppermute(meas_outer, 'ang', side_pairs)  1.28 us
  transfers between devices with their start and end apart: 10, of which 3 were waited for; matrix products, arithmetic and copies ran while one was open for 0% of the time, Pallas kernels for 38%

profile of v7, /device:TPU:17, one launch (start us, length us, event | category | flops | bytes accessed | tf_op | source)
XLA Modules:
  0.0 36.0 jit_solution(15674989389244230350)
XLA Ops:
  0.6 0.0 copy-start
  0.6 0.0 copy-start.2
  0.6 1.2 %shard_map.68 = (bf16[96,2,1024]{2,1,0:T(2,128)(2,1)S(1)}, bf16[208,128]{1,0:T(8,128)(2,1)S(1)}, bf16[320,128]{1,0:T(8,128)(2,1)S(1)}, f32[2,128]{1,0:T(2,128)S(1)}) custom-call(bf16[2,128,2,1024]{3,2,1,0:T(2,128)(2,1)} %slices.7, f32[2,128]{1,0:T(2,128)} %bitcast.1), custom_call_target="tpu_custom_call" | custom-call | tf_op jit(solution)/shard_map/pallas_call | solution.py:639
  1.8 3.7 %collective-permute-start.3 = (bf16[96,2,1024]{2,1,0:T(2,128)(2,1)S(1)}, bf16[96,2,1024]{2,1,0:T(2,128)(2,1)S(1)}, u32[]{:S(2)}, u32[]{:S(2)}) collective-permute-start(bf16[96,2,1024]{2,1,0:T(2,128)(2,1)S(1)} %get-tuple-element.46), channel_id=1, source_target_pairs={{2,4},{4,2},{6,8},{8,6},{10,12},{12,10},{14,16},{16,14},{18,20},{2... | collective-permute-start | bytes 1179656 | tf_op jit(solution)/shard_map/ppermute | solution.py:675
  6.2 0.0 copy-done
  6.2 0.1 shard_map.69.across
  6.3 1.2 %collective-permute-start.4 = (bf16[208,128]{1,0:T(8,128)(2,1)S(1)}, bf16[208,128]{1,0:T(8,128)(2,1)S(1)}, u32[]{:S(2)}, u32[]{:S(2)}) collective-permute-start(bf16[208,128]{1,0:T(8,128)(2,1)S(1)} %shard_map.69.across), channel_id=1, source_target_pairs={{0,1},{1,0},{2,3},{3,2},{4,5},{5,4},{6,7},{7,6},{8,9},{9,8},{10,11... | collective-permute-start | bytes 159752 | tf_op jit(solution)/shard_map/ppermute | solution.py:676
  7.6 0.0 copy-start.1
  7.6 0.3 collective-permute-start
  7.8 0.1 shard_map.72
  8.0 1.3 %collective-permute-start.6 = (bf16[128,1152]{1,0:T(8,128)(2,1)S(1)}, bf16[128,1152]{1,0:T(8,128)(2,1)S(1)}, u32[]{:S(2)}, u32[]{:S(2)}) collective-permute-start(bf16[128,1152]{1,0:T(8,128)(2,1)S(1)} %get-tuple-element.60), channel_id=1, source_target_pairs={{0,1},{1,0},{2,3},{3,2},{4,5},{5,4},{6,7},{7,6},{8,9},{9,8},{10,11... | collective-permute-start | bytes 884744 | tf_op jit(solution)/shard_map/ppermute | solution.py:682
  9.2 0.8 %collective-permute-done.4.across.early = bf16[208,128]{1,0:T(8,128)(2,1)S(1)} collective-permute-done((bf16[208,128]{1,0:T(8,128)(2,1)S(1)}, bf16[208,128]{1,0:T(8,128)(2,1)S(1)}, u32[]{:S(2)}, u32[]{:S(2)}) %collective-permute-start.4) | collective-permute-done | bytes 53280 | tf_op jit(solution)/shard_map/ppermute | solution.py:676
  10.0 2.4 %collective-permute-start.5 = (bf16[208,128]{1,0:T(8,128)(2,1)S(1)}, bf16[208,128]{1,0:T(8,128)(2,1)S(1)}, u32[]{:S(2)}, u32[]{:S(2)}) collective-permute-start(bf16[208,128]{1,0:T(8,128)(2,1)S(1)} %collective-permute-done.4.across.early), channel_id=1, source_target_pairs={{2,4},{4,2},{6,8},{8,6},{10,12},{12,10},{14,16},{16,14},{18,20},{2... | collective-permute-start | bytes 159752 | tf_op jit(solution)/shard_map/ppermute | solution.py:678
  12.4 1.3 %collective-permute-start.2 = (bf16[128,1152]{1,0:T(8,128)(2,1)S(1)}, bf16[128,1152]{1,0:T(8,128)(2,1)S(1)}, u32[]{:S(2)}, u32[]{:S(2)}) collective-permute-start(bf16[128,1152]{1,0:T(8,128)(2,1)S(1)} %get-tuple-element.44), channel_id=1, source_target_pairs={{0,1},{1,0},{2,3},{3,2},{4,5},{5,4},{6,7},{7,6},{8,9},{9,8},{10,11... | collective-permute-start | bytes 884744 | tf_op jit(solution)/shard_map/ppermute | solution.py:683
  13.7 0.0 copy-done.2
  13.7 1.1 %shard_map.70 = (f32[192,512]{1,0:T(8,128)S(1)}, f32[192,512]{1,0:T(8,128)S(1)}, bf16[128,256]{1,0:T(8,128)(2,1)S(1)}, bf16[256,128]{1,0:T(8,128)(2,1)S(1)}, bf1...) custom-call(bf16[2,65]{1,0:T(2,128)(2,1)S(1)} %copy-done.2, ...), custom_call_target="tpu_custom_call" | custom-call | tf_op jit(solution)/shard_map/pallas_call | solution.py:639
  14.8 0.5 %shard_map.73 = (bf16[768,512]{1,0:T(8,128)(2,1)S(1)}, bf16[512,768]{1,0:T(8,128)(2,1)S(1)}, bf16[256,128]{1,0:T(8,128)(2,1)S(1)}, f32[8,1152]{1,0:T(8,128)S(1)}) custom-call(f32[192,512]{1,0:T(8,128)S(1)} %get-tuple-element.47.row_real, ...), custom_call_target="tpu_custom_call", output_to_operand_aliasing={{0}: (3, {}), {1}: (4, {}), {2}: (5, {}), {3}: (6, {})} | custom-call | tf_op jit(solution)/shard_map/pallas_call | solution.py:639
  15.2 0.0 collective-permute-done.across
  15.3 0.0 copy-done.1
  15.3 0.1 shard_map.71
  15.3 1.5 %collective-permute-start.1 = (bf16[192,1152]{1,0:T(8,128)(2,1)S(1)}, bf16[192,1152]{1,0:T(8,128)(2,1)S(1)}, u32[]{:S(2)}, u32[]{:S(2)}) collective-permute-start(bf16[192,1152]{1,0:T(8,128)(2,1)S(1)} %shard_map.71), channel_id=1, source_target_pairs={{0,2},{2,0},{4,6},{6,4},{8,10},{10,8},{12,14},{14,12},{16,18},{18,... | collective-permute-start | bytes 1327112 | tf_op jit(solution)/shard_map/ppermute | solution.py:699
  16.9 0.0 collective-permute-done.5.corner
  16.9 0.0 collective-permute-done.3.outer
  16.9 2.6 %shard_map.74 = (f32[384,1152]{1,0:T(8,128)S(1)}, bf16[2,384,1152]{2,1,0:T(8,128)(2,1)S(1)}, bf16[2,384,1152]{2,1,0:T(8,128)(2,1)S(1)}, bf16[2,128,1152]{2,1,0:T(8,128)(2,1)S(1)}) custom-call(bf16[2,128,2,1024]{3,2,1,0:T(2,128)(2,1)S(1)} %copy-done.1, bf16[96,2,1024]{2,1,0:T(2,128)(2,1)S(1)} %collective-permute-done.3.outer, ...), custom_call_target="tpu_custom_call" | custom-call | flops 2400000000 | tf_op jit(solution)/shard_map/pallas_call | solution.py:639
  19.5 0.0 collective-permute-done.6.measured_got
  19.5 2.0 %shard_map.75 = (bf16[2,256,1152]{2,1,0:T(8,128)(2,1)S(1)}, f32[384,1280]{1,0:T(8,128)S(1)}, bf16[768,1024]{1,0:T(8,128)(2,1)S(1)}, bf16[192,1024]{1,0:T(8,128)(2,1)S(1)}) custom-call(f32[384,1152]{1,0:T(8,128)S(1)} %get-tuple-element.57.far_slab.far_slab_in, bf16[2,384,1152]{2,1,0:T(8,128)(2,1)S(1)} %get-tuple-element.58.field.field_in, ...), custom_call_target="tpu_custom_call" | custom-call | flops 1000000000 | tf_op jit(solution)/shard_map/pallas_call | solution.py:639
  21.5 3.7 %collective-permute-start.9 = (bf16[192,1024]{1,0:T(8,128)(2,1)S(1)}, bf16[192,1024]{1,0:T(8,128)(2,1)S(1)}, u32[]{:S(2)}, u32[]{:S(2)}) collective-permute-start(bf16[192,1024]{1,0:T(8,128)(2,1)S(1)} %get-tuple-element.63.sent), channel_id=1, source_target_pairs={{2,4},{4,2},{6,8},{8,6},{10,12},{12,10},{14,16},{16,14},{18,20},{2... | collective-permute-start | bytes 1179656 | tf_op jit(solution)/shard_map/ppermute | solution.py:729
  25.2 0.0 collective-permute-done.2.measured_got
  25.2 0.4 %shard_map.76.measured = f32[2,128,1152]{2,1,0:T(8,128)S(1)} custom-call(bf16[1,128,2,2048]{3,2,1,0:T(2,128)(2,1)S(1)} %copy-done, bf16[128,1152]{1,0:T(8,128)(2,1)S(1)} %collective-permute-done.2.measured_got, bf16[128,128]{1,0:T(8,128)(2,1)S(1)} %get-tuple-element.45.split_meas, bf16[192,1024]{1,0:T(8,128)(2,1)S(1)} %get-tuple-element.63.sent), custom_call_target="tpu_custom_call" | custom-call | flops 4000000000 | tf_op jit(solution)/shard_map/pallas_call | solution.py:639
  25.6 0.0 collective-permute-done.1.inner
  25.6 4.9 %shard_map.77 = (f32[384,1152]{1,0:T(8,128)S(1)}, bf16[2,384,1152]{2,1,0:T(8,128)(2,1)S(1)}, bf16[2,384,1152]{2,1,0:T(8,128)(2,1)S(1)}, bf16[2,256,1152]{2,1,0:T...) custom-call(bf16[2,128,2,1024]{3,2,1,0:T(2,128)(2,1)S(1)} %copy-done, ...), custom_call_target="tpu_custom_call", output_to_operand_aliasing={{0}: (4, {}), {1}: (5, {}), {2}: (6, {}), {3}: (7, {}), {4}... | custom-call | tf_op jit(solution)/shard_map/pallas_call | solution.py:639
  30.5 0.1 collective-permute-start.7
  30.6 0.5 %collective-permute-start.8 = (bf16[64,1024]{1,0:T(8,128)(2,1)S(1)}, bf16[64,1024]{1,0:T(8,128)(2,1)S(1)}, u32[]{:S(2)}, u32[]{:S(2)}) collective-permute-start(bf16[64,1024]{1,0:T(8,128)(2,1)S(1)} %get-tuple-element.75), channel_id=1, source_target_pairs={{0,2},{2,0},{4,6},{6,4},{8,10},{10,8},{12,14},{14,12},{16,18},{18,... | collective-permute-start | bytes 393224 | tf_op jit(solution)/shard_map/ppermute | solution.py:750
  31.1 0.6 %shard_map.78 = (f32[256,1024]{1,0:T(8,128)S(1)}, f32[2,128,1024]{2,1,0:T(8,128)S(1)}) custom-call(bf16[768,1024]{1,0:T(8,128)(2,1)S(1)} %get-tuple-element.70.into, f32[384,1280]{1,0:T(8,128)S(1)} %get-tuple-element.71.far_sum, bf16[512,768]{1,0:T(8,128)(2,1)S(1)} %get-tuple-element.69.row_near_adj), custom_call_target="tpu_custom_call" | custom-call | tf_op jit(solution)/shard_map/pallas_call | solution.py:639
  31.8 0.6 %collective-permute-done.8.inner_far = bf16[64,1024]{1,0:T(8,128)(2,1)S(1)} collective-permute-done((bf16[64,1024]{1,0:T(8,128)(2,1)S(1)}, bf16[64,1024]{1,0:T(8,128)(2,1)S(1)}, u32[]{:S(2)}, u32[]{:S(2)}) %collective-permute-start.8) | collective-permute-done | bytes 131104 | tf_op jit(solution)/shard_map/ppermute | solution.py:750
  32.3 0.0 collective-permute-done.7.inner
  32.3 1.2 %shard_map.79 = (f32[128,2,1024]{2,1,0:T(2,128)}, f32[128,2,1024]{2,1,0:T(2,128)}) custom-call(f32[256,1024]{1,0:T(8,128)S(1)} %get-tuple-element.72.near_sum, f32[2,128,1024]{2,1,0:T(8,128)S(1)} %get-tuple-element.73.far_sum, bf16[128,1024]{1,0:T(8,128)(2,1)S(1)} %collective-permute-done.7.inner, bf16[64,1024]{1,0:T(8,128)(2,1)S(1)} %collective-permute-done.8.inner_far), custom_call_target="tpu_custom_call" | custom-call | tf_op jit(solution)/shard_map/pallas_call | solution.py:639
  33.5 1.3 %collective-permute-done.9.outer = bf16[192,1024]{1,0:T(8,128)(2,1)S(1)} collective-permute-done((bf16[192,1024]{1,0:T(8,128)(2,1)S(1)}, bf16[192,1024]{1,0:T(8,128)(2,1)S(1)}, u32[]{:S(2)}, u32[]{:S(2)}) %collective-permute-start.9) | collective-permute-done | bytes 393248 | tf_op jit(solution)/shard_map/ppermute | solution.py:729
  34.8 1.0 %shard_map.80 = (f32[128,2,1024]{2,1,0:T(2,128)}, f32[128,2,1024]{2,1,0:T(2,128)}) custom-call(f32[128,2,1024]{2,1,0:T(2,128)} %get-tuple-element.76.near_in, f32[128,2,1024]{2,1,0:T(2,128)} %get-tuple-element.77.far_in, f32[256,1024]{1,0:T(8,128)S(1)} %get-tuple-element.72.near_sum, ...), custom_call_target="tpu_custom_call", output_to_operand_aliasing={{0}: (0, {}), {1}: (1, {})} | custom-call | tf_op jit(solution)/shard_map/pallas_call | solution.py:639
Async XLA Ops:
  0.6 5.6 %copy-start = (bf16[1,128,2,2048]{3,2,1,0:T(2,128)(2,1)S(1)}, bf16[1,128,2,2048]{3,2,1,0:T(2,128)(2,1)}, u32[]{:S(2)}) copy-start(bf16[1,128,2,2048]{3,2,1,0:T(2,128)(2,1)} %measured.7) | copy-start | bytes 3145732
  0.6 13.0 %copy-start.2 = (bf16[2,65]{1,0:T(2,128)(2,1)S(1)}, bf16[2,65]{1,0:T(2,128)(2,1)}, u32[]{:S(2)}) copy-start(bf16[2,65]{1,0:T(2,128)(2,1)} %taps.1) | copy-start | bytes 784
  1.8 15.0 %collective-permute-start.3 = (bf16[96,2,1024]{2,1,0:T(2,128)(2,1)S(1)}, bf16[96,2,1024]{2,1,0:T(2,128)(2,1)S(1)}, u32[]{:S(2)}, u32[]{:S(2)}) collective-permute-start(bf16[96,2,1024]{2,1,0:T(2,128)(2,1)S(1)} %get-tuple-element.46), channel_id=1, source_target_pairs={{2,4},{4,2},{6,8},{8,6},{10,12},{12,10},{14,16},{16,14},{18,20},{2... | collective-permute-start | bytes 1179656 | tf_op jit(solution)/shard_map/ppermute | solution.py:675
  6.3 3.7 %collective-permute-start.4 = (bf16[208,128]{1,0:T(8,128)(2,1)S(1)}, bf16[208,128]{1,0:T(8,128)(2,1)S(1)}, u32[]{:S(2)}, u32[]{:S(2)}) collective-permute-start(bf16[208,128]{1,0:T(8,128)(2,1)S(1)} %shard_map.69.across), channel_id=1, source_target_pairs={{0,1},{1,0},{2,3},{3,2},{4,5},{5,4},{6,7},{7,6},{8,9},{9,8},{10,11... | collective-permute-start | bytes 159752 | tf_op jit(solution)/shard_map/ppermute | solution.py:676
  7.6 7.7 %copy-start.1 = (bf16[2,128,2,1024]{3,2,1,0:T(2,128)(2,1)S(1)}, bf16[2,128,2,1024]{3,2,1,0:T(2,128)(2,1)}, u32[]{:S(2)}) copy-start(bf16[2,128,2,1024]{3,2,1,0:T(2,128)(2,1)} %slices.7) | copy-start | bytes 3145732
  7.6 7.7 %collective-permute-start = (bf16[320,128]{1,0:T(8,128)(2,1)S(1)}, bf16[320,128]{1,0:T(8,128)(2,1)S(1)}, u32[]{:S(2)}, u32[]{:S(2)}) collective-permute-start(bf16[320,128]{1,0:T(8,128)(2,1)S(1)} %get-tuple-element.40.sent), channel_id=1, source_target_pairs={{0,1},{1,0},{2,3},{3,2},{4,5},{5,4},{6,7},{7,6},{8,9},{9,8},{10,11... | collective-permute-start | bytes 245768 | tf_op jit(solution)/shard_map/ppermute | solution.py:677
  8.0 11.5 %collective-permute-start.6 = (bf16[128,1152]{1,0:T(8,128)(2,1)S(1)}, bf16[128,1152]{1,0:T(8,128)(2,1)S(1)}, u32[]{:S(2)}, u32[]{:S(2)}) collective-permute-start(bf16[128,1152]{1,0:T(8,128)(2,1)S(1)} %get-tuple-element.60), channel_id=1, source_target_pairs={{0,1},{1,0},{2,3},{3,2},{4,5},{5,4},{6,7},{7,6},{8,9},{9,8},{10,11... | collective-permute-start | bytes 884744 | tf_op jit(solution)/shard_map/ppermute | solution.py:682
  10.0 6.8 %collective-permute-start.5 = (bf16[208,128]{1,0:T(8,128)(2,1)S(1)}, bf16[208,128]{1,0:T(8,128)(2,1)S(1)}, u32[]{:S(2)}, u32[]{:S(2)}) collective-permute-start(bf16[208,128]{1,0:T(8,128)(2,1)S(1)} %collective-permute-done.4.across.early), channel_id=1, source_target_pairs={{2,4},{4,2},{6,8},{8,6},{10,12},{12,10},{14,16},{16,14},{18,20},{2... | collective-permute-start | bytes 159752 | tf_op jit(solution)/shard_map/ppermute | solution.py:678
  12.4 12.8 %collective-permute-start.2 = (bf16[128,1152]{1,0:T(8,128)(2,1)S(1)}, bf16[128,1152]{1,0:T(8,128)(2,1)S(1)}, u32[]{:S(2)}, u32[]{:S(2)}) collective-permute-start(bf16[128,1152]{1,0:T(8,128)(2,1)S(1)} %get-tuple-element.44), channel_id=1, source_target_pairs={{0,1},{1,0},{2,3},{3,2},{4,5},{5,4},{6,7},{7,6},{8,9},{9,8},{10,11... | collective-permute-start | bytes 884744 | tf_op jit(solution)/shard_map/ppermute | solution.py:683
  15.3 10.3 %collective-permute-start.1 = (bf16[192,1152]{1,0:T(8,128)(2,1)S(1)}, bf16[192,1152]{1,0:T(8,128)(2,1)S(1)}, u32[]{:S(2)}, u32[]{:S(2)}) collective-permute-start(bf16[192,1152]{1,0:T(8,128)(2,1)S(1)} %shard_map.71), channel_id=1, source_target_pairs={{0,2},{2,0},{4,6},{6,4},{8,10},{10,8},{12,14},{14,12},{16,18},{18,... | collective-permute-start | bytes 1327112 | tf_op jit(solution)/shard_map/ppermute | solution.py:699
  21.5 13.3 %collective-permute-start.9 = (bf16[192,1024]{1,0:T(8,128)(2,1)S(1)}, bf16[192,1024]{1,0:T(8,128)(2,1)S(1)}, u32[]{:S(2)}, u32[]{:S(2)}) collective-permute-start(bf16[192,1024]{1,0:T(8,128)(2,1)S(1)} %get-tuple-element.63.sent), channel_id=1, source_target_pairs={{2,4},{4,2},{6,8},{8,6},{10,12},{12,10},{14,16},{16,14},{18,20},{2... | collective-permute-start | bytes 1179656 | tf_op jit(solution)/shard_map/ppermute | solution.py:729
  30.5 1.8 %collective-permute-start.7 = (bf16[128,1024]{1,0:T(8,128)(2,1)S(1)}, bf16[128,1024]{1,0:T(8,128)(2,1)S(1)}, u32[]{:S(2)}, u32[]{:S(2)}) collective-permute-start(bf16[128,1024]{1,0:T(8,128)(2,1)S(1)} %get-tuple-element.74), channel_id=1, source_target_pairs={{0,2},{2,0},{4,6},{6,4},{8,10},{10,8},{12,14},{14,12},{16,18},{18,... | collective-permute-start | bytes 786440 | tf_op jit(solution)/shard_map/ppermute | solution.py:749
  30.6 1.7 %collective-permute-start.8 = (bf16[64,1024]{1,0:T(8,128)(2,1)S(1)}, bf16[64,1024]{1,0:T(8,128)(2,1)S(1)}, u32[]{:S(2)}, u32[]{:S(2)}) collective-permute-start(bf16[64,1024]{1,0:T(8,128)(2,1)S(1)} %get-tuple-element.75), channel_id=1, source_target_pairs={{0,2},{2,0},{4,6},{6,4},{8,10},{10,8},{12,14},{14,12},{16,18},{18,... | collective-permute-start | bytes 393224 | tf_op jit(solution)/shard_map/ppermute | solution.py:750

commit v8 on v7

--- a/solution.py
+++ b/solution.py
@@ -91,7 +91,7 @@
     return pl.ds(pl.multiple_of(2 * rows - 4 * half + other * (2 * rows - 4 * half), 16), 2 * half)
 
 
-def measured_kernel(measured, sent, outer, inner):
+def measured_kernel(measured, sent, ready, outer, inner):
     size, cols = outer.shape[0] // 2, measured.shape[3] // 2
     parity = lax.axis_index("rows") % 2
     side = lax.axis_index("ang")
@@ -676,11 +676,6 @@
     early_got = lax.ppermute(early, "ang", side_pairs)
     across_got = lax.ppermute(across, "ang", side_pairs)
     corner_got = lax.ppermute(early_got, "rows", outer_pairs)
-    meas_outer, meas_inner = call(
-        measured_kernel, [((rows, width), BF16)] * 2, (measured, across), outside=(1,),
-    )
-    outer_meas = lax.ppermute(meas_outer, "ang", side_pairs)
-    inner_meas = lax.ppermute(meas_inner, "ang", side_pairs)
     phased = [
         ((4 * mid, 2 * wide), BF16), ((2 * wide, 4 * mid), BF16), ((8 * half, 4 * half), BF16), ((8, width), F32),
     ]
@@ -693,6 +688,11 @@
         ],
         (kernel_taps, early),
     )
+    meas_outer, meas_inner = call(
+        measured_kernel, [((rows, width), BF16)] * 2, (measured, across, row_half), outside=(1, 2),
+    )
+    outer_meas = lax.ppermute(meas_outer, "ang", side_pairs)
+    inner_meas = lax.ppermute(meas_inner, "ang", side_pairs)
     (inner,) = call(
         functools.partial(inner_edge_kernel, half), [((edge, width), BF16)], (slices, across_got, row_half), outside=(2,),
     )

time: 36.1 us -> 35.4 us (0.981)
  waiting for transfers between devices: 2.65 us -> 2.02 us
    ppermute x1, waiting for transfers between devices: 0.78 us -> 0.01 us  [columns_local(): early_got = lax.ppermute(early, 'ang', side_pairs)]
    ppermute x1, starting transfers between devices: 0.07 us -> 0.82 us  [columns_local(): inner_back = lax.ppermute(inner_sums, 'rows', inner_pairs)]
    ppermute x1, starting transfers between devices: 1.28 us -> 0.57 us  [columns_local(): inner_meas = lax.ppermute(meas_inner, 'ang', side_pairs)]
    ppermute x1, starting transfers between devices: 0.5 us -> 0.08 us  [columns_local(): inner_far_back = lax.ppermute(inner_far, 'rows', inner_pairs)]
    ppermute x1, starting transfers between devices: 2.37 us -> 2.75 us  [columns_local(): corner_got = lax.ppermute(early_got, 'rows', outer_pairs)]
  transfers between devices with their start and end apart: 10 -> 10, of which waited for: 3 -> 3; matrix products, arithmetic and copies ran while one was open for 0% -> 0% of each run, Pallas kernels for 38% -> 39%
where the time goes in v8:
time: 35.4 us; the launch traced here: 35.2 us
  Pallas kernels  15.8 us (45%)
  starting transfers between devices  15.7 us (44%)
  waiting for transfers between devices  2.02 us (6%)
  between operations  1.61 us (5%)
    pallas_call x13, Pallas kernels, call(): pl.pallas_call(kernel, out_shape=[jax.ShapeDtypeStruct(shape, dtype) for...  15.8 us
    ppermute x1, starting transfers between devices, columns_local(): outer_got = lax.ppermute(outer, 'rows', outer_pairs)  3.71 us
    ppermute x1, starting transfers between devices, columns_local(): outer_back = lax.ppermute(outer_sums, 'rows', outer_pairs)  3.53 us
    ppermute x1, starting transfers between devices, columns_local(): corner_got = lax.ppermute(early_got, 'rows', outer_pairs)  2.75 us
    ppermute x1, starting transfers between devices, columns_local(): inner_got = lax.ppermute(inner, 'rows', inner_pairs)  1.51 us
    ppermute x1, starting transfers between devices, columns_local(): outer_meas = lax.ppermute(meas_outer, 'ang', side_pairs)  1.28 us
    ppermute x1, starting transfers between devices, columns_local(): early_got = lax.ppermute(early, 'ang', side_pairs)  1.25 us
    ppermute x1, waiting for transfers between devices, columns_local(): outer_back = lax.ppermute(outer_sums, 'rows', outer_pairs)  1.06 us
  transfers between devices with their start and end apart: 10, of which 3 were waited for; matrix products, arithmetic and copies ran while one was open for 0% of the time, Pallas kernels for 39%

profile of v8, /device:TPU:17, one launch (start us, length us, event | category | flops | bytes accessed | tf_op | source)
XLA Modules:
  0.0 35.2 jit_solution(2095897500780051034)
XLA Ops:
  0.6 0.0 copy-start
  0.6 0.0 copy-start.2
  0.6 1.2 %shard_map.68 = (bf16[96,2,1024]{2,1,0:T(2,128)(2,1)S(1)}, bf16[208,128]{1,0:T(8,128)(2,1)S(1)}, bf16[320,128]{1,0:T(8,128)(2,1)S(1)}, f32[2,128]{1,0:T(2,128)S(1)}) custom-call(bf16[2,128,2,1024]{3,2,1,0:T(2,128)(2,1)} %slices.7, f32[2,128]{1,0:T(2,128)} %bitcast.1), custom_call_target="tpu_custom_call" | custom-call | tf_op jit(solution)/shard_map/pallas_call | solution.py:639
  1.8 3.7 %collective-permute-start.3 = (bf16[96,2,1024]{2,1,0:T(2,128)(2,1)S(1)}, bf16[96,2,1024]{2,1,0:T(2,128)(2,1)S(1)}, u32[]{:S(2)}, u32[]{:S(2)}) collective-permute-start(bf16[96,2,1024]{2,1,0:T(2,128)(2,1)S(1)} %get-tuple-element.46), channel_id=1, source_target_pairs={{2,4},{4,2},{6,8},{8,6},{10,12},{12,10},{14,16},{16,14},{18,20},{2... | collective-permute-start | bytes 1179656 | tf_op jit(solution)/shard_map/ppermute | solution.py:675
  6.2 0.0 copy-done
  6.2 0.1 shard_map.69.across
  6.3 1.2 %collective-permute-start.4 = (bf16[208,128]{1,0:T(8,128)(2,1)S(1)}, bf16[208,128]{1,0:T(8,128)(2,1)S(1)}, u32[]{:S(2)}, u32[]{:S(2)}) collective-permute-start(bf16[208,128]{1,0:T(8,128)(2,1)S(1)} %shard_map.69.across), channel_id=1, source_target_pairs={{0,1},{1,0},{2,3},{3,2},{4,5},{5,4},{6,7},{7,6},{8,9},{9,8},{10,11... | collective-permute-start | bytes 159752 | tf_op jit(solution)/shard_map/ppermute | solution.py:676
  7.6 0.3 collective-permute-start
  7.8 0.0 copy-done.2
  7.8 1.1 %shard_map.70 = (f32[192,512]{1,0:T(8,128)S(1)}, f32[192,512]{1,0:T(8,128)S(1)}, bf16[128,256]{1,0:T(8,128)(2,1)S(1)}, bf16[256,128]{1,0:T(8,128)(2,1)S(1)}, bf1...) custom-call(bf16[2,65]{1,0:T(2,128)(2,1)S(1)} %copy-done.2, ...), custom_call_target="tpu_custom_call" | custom-call | tf_op jit(solution)/shard_map/pallas_call | solution.py:639
  8.9 0.0 copy-start.1
  8.9 0.1 shard_map.72
  9.1 1.3 %collective-permute-start.6 = (bf16[128,1152]{1,0:T(8,128)(2,1)S(1)}, bf16[128,1152]{1,0:T(8,128)(2,1)S(1)}, u32[]{:S(2)}, u32[]{:S(2)}) collective-permute-start(bf16[128,1152]{1,0:T(8,128)(2,1)S(1)} %get-tuple-element.60), channel_id=1, source_target_pairs={{0,1},{1,0},{2,3},{3,2},{4,5},{5,4},{6,7},{7,6},{8,9},{9,8},{10,11... | collective-permute-start | bytes 884744 | tf_op jit(solution)/shard_map/ppermute | solution.py:694
  10.3 0.0 collective-permute-done.4.across.early
  10.4 2.7 %collective-permute-start.5 = (bf16[208,128]{1,0:T(8,128)(2,1)S(1)}, bf16[208,128]{1,0:T(8,128)(2,1)S(1)}, u32[]{:S(2)}, u32[]{:S(2)}) collective-permute-start(bf16[208,128]{1,0:T(8,128)(2,1)S(1)} %collective-permute-done.4.across.early), channel_id=1, source_target_pairs={{2,4},{4,2},{6,8},{8,6},{10,12},{12,10},{14,16},{16,14},{18,20},{2... | collective-permute-start | bytes 159752 | tf_op jit(solution)/shard_map/ppermute | solution.py:678
  13.1 0.6 %collective-permute-start.2 = (bf16[128,1152]{1,0:T(8,128)(2,1)S(1)}, bf16[128,1152]{1,0:T(8,128)(2,1)S(1)}, u32[]{:S(2)}, u32[]{:S(2)}) collective-permute-start(bf16[128,1152]{1,0:T(8,128)(2,1)S(1)} %get-tuple-element.44), channel_id=1, source_target_pairs={{0,1},{1,0},{2,3},{3,2},{4,5},{5,4},{6,7},{7,6},{8,9},{9,8},{10,11... | collective-permute-start | bytes 884744 | tf_op jit(solution)/shard_map/ppermute | solution.py:695
  13.7 0.5 %shard_map.73 = (bf16[768,512]{1,0:T(8,128)(2,1)S(1)}, bf16[512,768]{1,0:T(8,128)(2,1)S(1)}, bf16[256,128]{1,0:T(8,128)(2,1)S(1)}, f32[8,1152]{1,0:T(8,128)S(1)}) custom-call(f32[192,512]{1,0:T(8,128)S(1)} %get-tuple-element.47.row_real, ...), custom_call_target="tpu_custom_call", output_to_operand_aliasing={{0}: (3, {}), {1}: (4, {}), {2}: (5, {}), {3}: (6, {})} | custom-call | tf_op jit(solution)/shard_map/pallas_call | solution.py:639
  14.2 0.0 collective-permute-done.across
  14.2 0.0 copy-done.1
  14.2 0.1 shard_map.71
  14.3 1.5 %collective-permute-start.1 = (bf16[192,1152]{1,0:T(8,128)(2,1)S(1)}, bf16[192,1152]{1,0:T(8,128)(2,1)S(1)}, u32[]{:S(2)}, u32[]{:S(2)}) collective-permute-start(bf16[192,1152]{1,0:T(8,128)(2,1)S(1)} %shard_map.71), channel_id=1, source_target_pairs={{0,2},{2,0},{4,6},{6,4},{8,10},{10,8},{12,14},{14,12},{16,18},{18,... | collective-permute-start | bytes 1327112 | tf_op jit(solution)/shard_map/ppermute | solution.py:699
  15.8 0.3 collective-permute-done.5.corner
  16.1 0.0 collective-permute-done.3.outer
  16.1 2.6 %shard_map.74 = (f32[384,1152]{1,0:T(8,128)S(1)}, bf16[2,384,1152]{2,1,0:T(8,128)(2,1)S(1)}, bf16[2,384,1152]{2,1,0:T(8,128)(2,1)S(1)}, bf16[2,128,1152]{2,1,0:T(8,128)(2,1)S(1)}) custom-call(bf16[2,128,2,1024]{3,2,1,0:T(2,128)(2,1)S(1)} %copy-done.1, bf16[96,2,1024]{2,1,0:T(2,128)(2,1)S(1)} %collective-permute-done.3.outer, ...), custom_call_target="tpu_custom_call" | custom-call | flops 2400000000 | tf_op jit(solution)/shard_map/pallas_call | solution.py:639
  18.7 0.0 collective-permute-done.6.measured_got
  18.7 2.0 %shard_map.75 = (bf16[2,256,1152]{2,1,0:T(8,128)(2,1)S(1)}, f32[384,1280]{1,0:T(8,128)S(1)}, bf16[768,1024]{1,0:T(8,128)(2,1)S(1)}, bf16[192,1024]{1,0:T(8,128)(2,1)S(1)}) custom-call(f32[384,1152]{1,0:T(8,128)S(1)} %get-tuple-element.57.far_slab.far_slab_in, bf16[2,384,1152]{2,1,0:T(8,128)(2,1)S(1)} %get-tuple-element.58.field.field_in, ...), custom_call_target="tpu_custom_call" | custom-call | flops 1000000000 | tf_op jit(solution)/shard_map/pallas_call | solution.py:639
  20.7 3.5 %collective-permute-start.9 = (bf16[192,1024]{1,0:T(8,128)(2,1)S(1)}, bf16[192,1024]{1,0:T(8,128)(2,1)S(1)}, u32[]{:S(2)}, u32[]{:S(2)}) collective-permute-start(bf16[192,1024]{1,0:T(8,128)(2,1)S(1)} %get-tuple-element.63.sent), channel_id=1, source_target_pairs={{2,4},{4,2},{6,8},{8,6},{10,12},{12,10},{14,16},{16,14},{18,20},{2... | collective-permute-start | bytes 1179656 | tf_op jit(solution)/shard_map/ppermute | solution.py:729
  24.3 0.0 collective-permute-done.2.measured_got
  24.3 0.4 %shard_map.76.measured = f32[2,128,1152]{2,1,0:T(8,128)S(1)} custom-call(bf16[1,128,2,2048]{3,2,1,0:T(2,128)(2,1)S(1)} %copy-done, bf16[128,1152]{1,0:T(8,128)(2,1)S(1)} %collective-permute-done.2.measured_got, bf16[128,128]{1,0:T(8,128)(2,1)S(1)} %get-tuple-element.45.split_meas, bf16[192,1024]{1,0:T(8,128)(2,1)S(1)} %get-tuple-element.63.sent), custom_call_target="tpu_custom_call" | custom-call | flops 4000000000 | tf_op jit(solution)/shard_map/pallas_call | solution.py:639
  24.7 0.0 collective-permute-done.1.inner
  24.7 4.9 %shard_map.77 = (f32[384,1152]{1,0:T(8,128)S(1)}, bf16[2,384,1152]{2,1,0:T(8,128)(2,1)S(1)}, bf16[2,384,1152]{2,1,0:T(8,128)(2,1)S(1)}, bf16[2,256,1152]{2,1,0:T...) custom-call(bf16[2,128,2,1024]{3,2,1,0:T(2,128)(2,1)S(1)} %copy-done, ...), custom_call_target="tpu_custom_call", output_to_operand_aliasing={{0}: (4, {}), {1}: (5, {}), {2}: (6, {}), {3}: (7, {}), {4}... | custom-call | tf_op jit(solution)/shard_map/pallas_call | solution.py:639
  29.6 0.8 %collective-permute-start.7 = (bf16[128,1024]{1,0:T(8,128)(2,1)S(1)}, bf16[128,1024]{1,0:T(8,128)(2,1)S(1)}, u32[]{:S(2)}, u32[]{:S(2)}) collective-permute-start(bf16[128,1024]{1,0:T(8,128)(2,1)S(1)} %get-tuple-element.74), channel_id=1, source_target_pairs={{0,2},{2,0},{4,6},{6,4},{8,10},{10,8},{12,14},{14,12},{16,18},{18,... | collective-permute-start | bytes 786440 | tf_op jit(solution)/shard_map/ppermute | solution.py:749
  30.4 0.1 collective-permute-start.8
  30.5 0.6 %shard_map.78 = (f32[256,1024]{1,0:T(8,128)S(1)}, f32[2,128,1024]{2,1,0:T(8,128)S(1)}) custom-call(bf16[768,1024]{1,0:T(8,128)(2,1)S(1)} %get-tuple-element.70.into, f32[384,1280]{1,0:T(8,128)S(1)} %get-tuple-element.71.far_sum, bf16[512,768]{1,0:T(8,128)(2,1)S(1)} %get-tuple-element.69.row_near_adj), custom_call_target="tpu_custom_call" | custom-call | tf_op jit(solution)/shard_map/pallas_call | solution.py:639
  31.2 0.6 %collective-permute-done.8.inner_far = bf16[64,1024]{1,0:T(8,128)(2,1)S(1)} collective-permute-done((bf16[64,1024]{1,0:T(8,128)(2,1)S(1)}, bf16[64,1024]{1,0:T(8,128)(2,1)S(1)}, u32[]{:S(2)}, u32[]{:S(2)}) %collective-permute-start.8) | collective-permute-done | bytes 131104 | tf_op jit(solution)/shard_map/ppermute | solution.py:750
  31.8 0.0 collective-permute-done.7.inner
  31.8 1.2 %shard_map.79 = (f32[128,2,1024]{2,1,0:T(2,128)}, f32[128,2,1024]{2,1,0:T(2,128)}) custom-call(f32[256,1024]{1,0:T(8,128)S(1)} %get-tuple-element.72.near_sum, f32[2,128,1024]{2,1,0:T(8,128)S(1)} %get-tuple-element.73.far_sum, bf16[128,1024]{1,0:T(8,128)(2,1)S(1)} %collective-permute-done.7.inner, bf16[64,1024]{1,0:T(8,128)(2,1)S(1)} %collective-permute-done.8.inner_far), custom_call_target="tpu_custom_call" | custom-call | tf_op jit(solution)/shard_map/pallas_call | solution.py:639
  33.0 1.1 %collective-permute-done.9.outer = bf16[192,1024]{1,0:T(8,128)(2,1)S(1)} collective-permute-done((bf16[192,1024]{1,0:T(8,128)(2,1)S(1)}, bf16[192,1024]{1,0:T(8,128)(2,1)S(1)}, u32[]{:S(2)}, u32[]{:S(2)}) %collective-permute-start.9) | collective-permute-done | bytes 393248 | tf_op jit(solution)/shard_map/ppermute | solution.py:729
  34.1 1.0 %shard_map.80 = (f32[128,2,1024]{2,1,0:T(2,128)}, f32[128,2,1024]{2,1,0:T(2,128)}) custom-call(f32[128,2,1024]{2,1,0:T(2,128)} %get-tuple-element.76.near_in, f32[128,2,1024]{2,1,0:T(2,128)} %get-tuple-element.77.far_in, f32[256,1024]{1,0:T(8,128)S(1)} %get-tuple-element.72.near_sum, ...), custom_call_target="tpu_custom_call", output_to_operand_aliasing={{0}: (0, {}), {1}: (1, {})} | custom-call | tf_op jit(solution)/shard_map/pallas_call | solution.py:639
Async XLA Ops:
  0.6 5.6 %copy-start = (bf16[1,128,2,2048]{3,2,1,0:T(2,128)(2,1)S(1)}, bf16[1,128,2,2048]{3,2,1,0:T(2,128)(2,1)}, u32[]{:S(2)}) copy-start(bf16[1,128,2,2048]{3,2,1,0:T(2,128)(2,1)} %measured.7) | copy-start | bytes 3145732
  0.6 7.2 %copy-start.2 = (bf16[2,65]{1,0:T(2,128)(2,1)S(1)}, bf16[2,65]{1,0:T(2,128)(2,1)}, u32[]{:S(2)}) copy-start(bf16[2,65]{1,0:T(2,128)(2,1)} %taps.1) | copy-start | bytes 784
  1.8 14.2 %collective-permute-start.3 = (bf16[96,2,1024]{2,1,0:T(2,128)(2,1)S(1)}, bf16[96,2,1024]{2,1,0:T(2,128)(2,1)S(1)}, u32[]{:S(2)}, u32[]{:S(2)}) collective-permute-start(bf16[96,2,1024]{2,1,0:T(2,128)(2,1)S(1)} %get-tuple-element.46), channel_id=1, source_target_pairs={{2,4},{4,2},{6,8},{8,6},{10,12},{12,10},{14,16},{16,14},{18,20},{2... | collective-permute-start | bytes 1179656 | tf_op jit(solution)/shard_map/ppermute | solution.py:675
  6.3 4.0 %collective-permute-start.4 = (bf16[208,128]{1,0:T(8,128)(2,1)S(1)}, bf16[208,128]{1,0:T(8,128)(2,1)S(1)}, u32[]{:S(2)}, u32[]{:S(2)}) collective-permute-start(bf16[208,128]{1,0:T(8,128)(2,1)S(1)} %shard_map.69.across), channel_id=1, source_target_pairs={{0,1},{1,0},{2,3},{3,2},{4,5},{5,4},{6,7},{7,6},{8,9},{9,8},{10,11... | collective-permute-start | bytes 159752 | tf_op jit(solution)/shard_map/ppermute | solution.py:676
  7.6 6.6 %collective-permute-start = (bf16[320,128]{1,0:T(8,128)(2,1)S(1)}, bf16[320,128]{1,0:T(8,128)(2,1)S(1)}, u32[]{:S(2)}, u32[]{:S(2)}) collective-permute-start(bf16[320,128]{1,0:T(8,128)(2,1)S(1)} %get-tuple-element.40.sent), channel_id=1, source_target_pairs={{0,1},{1,0},{2,3},{3,2},{4,5},{5,4},{6,7},{7,6},{8,9},{9,8},{10,11... | collective-permute-start | bytes 245768 | tf_op jit(solution)/shard_map/ppermute | solution.py:677
  8.9 5.3 %copy-start.1 = (bf16[2,128,2,1024]{3,2,1,0:T(2,128)(2,1)S(1)}, bf16[2,128,2,1024]{3,2,1,0:T(2,128)(2,1)}, u32[]{:S(2)}) copy-start(bf16[2,128,2,1024]{3,2,1,0:T(2,128)(2,1)} %slices.7) | copy-start | bytes 3145732
  9.1 9.6 %collective-permute-start.6 = (bf16[128,1152]{1,0:T(8,128)(2,1)S(1)}, bf16[128,1152]{1,0:T(8,128)(2,1)S(1)}, u32[]{:S(2)}, u32[]{:S(2)}) collective-permute-start(bf16[128,1152]{1,0:T(8,128)(2,1)S(1)} %get-tuple-element.60), channel_id=1, source_target_pairs={{0,1},{1,0},{2,3},{3,2},{4,5},{5,4},{6,7},{7,6},{8,9},{9,8},{10,11... | collective-permute-start | bytes 884744 | tf_op jit(solution)/shard_map/ppermute | solution.py:694
  10.4 5.7 %collective-permute-start.5 = (bf16[208,128]{1,0:T(8,128)(2,1)S(1)}, bf16[208,128]{1,0:T(8,128)(2,1)S(1)}, u32[]{:S(2)}, u32[]{:S(2)}) collective-permute-start(bf16[208,128]{1,0:T(8,128)(2,1)S(1)} %collective-permute-done.4.across.early), channel_id=1, source_target_pairs={{2,4},{4,2},{6,8},{8,6},{10,12},{12,10},{14,16},{16,14},{18,20},{2... | collective-permute-start | bytes 159752 | tf_op jit(solution)/shard_map/ppermute | solution.py:678
  13.1 11.2 %collective-permute-start.2 = (bf16[128,1152]{1,0:T(8,128)(2,1)S(1)}, bf16[128,1152]{1,0:T(8,128)(2,1)S(1)}, u32[]{:S(2)}, u32[]{:S(2)}) collective-permute-start(bf16[128,1152]{1,0:T(8,128)(2,1)S(1)} %get-tuple-element.44), channel_id=1, source_target_pairs={{0,1},{1,0},{2,3},{3,2},{4,5},{5,4},{6,7},{7,6},{8,9},{9,8},{10,11... | collective-permute-start | bytes 884744 | tf_op jit(solution)/shard_map/ppermute | solution.py:695
  14.3 10.4 %collective-permute-start.1 = (bf16[192,1152]{1,0:T(8,128)(2,1)S(1)}, bf16[192,1152]{1,0:T(8,128)(2,1)S(1)}, u32[]{:S(2)}, u32[]{:S(2)}) collective-permute-start(bf16[192,1152]{1,0:T(8,128)(2,1)S(1)} %shard_map.71), channel_id=1, source_target_pairs={{0,2},{2,0},{4,6},{6,4},{8,10},{10,8},{12,14},{14,12},{16,18},{18,... | collective-permute-start | bytes 1327112 | tf_op jit(solution)/shard_map/ppermute | solution.py:699
  20.7 13.3 %collective-permute-start.9 = (bf16[192,1024]{1,0:T(8,128)(2,1)S(1)}, bf16[192,1024]{1,0:T(8,128)(2,1)S(1)}, u32[]{:S(2)}, u32[]{:S(2)}) collective-permute-start(bf16[192,1024]{1,0:T(8,128)(2,1)S(1)} %get-tuple-element.63.sent), channel_id=1, source_target_pairs={{2,4},{4,2},{6,8},{8,6},{10,12},{12,10},{14,16},{16,14},{18,20},{2... | collective-permute-start | bytes 1179656 | tf_op jit(solution)/shard_map/ppermute | solution.py:729
  29.6 2.2 %collective-permute-start.7 = (bf16[128,1024]{1,0:T(8,128)(2,1)S(1)}, bf16[128,1024]{1,0:T(8,128)(2,1)S(1)}, u32[]{:S(2)}, u32[]{:S(2)}) collective-permute-start(bf16[128,1024]{1,0:T(8,128)(2,1)S(1)} %get-tuple-element.74), channel_id=1, source_target_pairs={{0,2},{2,0},{4,6},{6,4},{8,10},{10,8},{12,14},{14,12},{16,18},{18,... | collective-permute-start | bytes 786440 | tf_op jit(solution)/shard_map/ppermute | solution.py:749
  30.4 1.3 %collective-permute-start.8 = (bf16[64,1024]{1,0:T(8,128)(2,1)S(1)}, bf16[64,1024]{1,0:T(8,128)(2,1)S(1)}, u32[]{:S(2)}, u32[]{:S(2)}) collective-permute-start(bf16[64,1024]{1,0:T(8,128)(2,1)S(1)} %get-tuple-element.75), channel_id=1, source_target_pairs={{0,2},{2,0},{4,6},{6,4},{8,10},{10,8},{12,14},{14,12},{16,18},{18,... | collective-permute-start | bytes 393224 | tf_op jit(solution)/shard_map/ppermute | solution.py:750

commit v9 on v8

--- a/solution.py
+++ b/solution.py
@@ -124,8 +124,8 @@
 
 def matrices_kernel(
     rows, length, taps, across,
-    row_real, row_imag, row_half, row_half_adj, row_adj, col_taps, split_far, split_meas,
-    row_near, row_near_adj, row_edge, waves,
+    row_real, row_imag, row_half, row_half_adj, row_fwd, col_taps, split_far, split_meas,
+    row_near, row_edge, waves,
 ):
     count = taps.shape[1]
     half = (count - 1) // 2
@@ -147,14 +147,14 @@
     row_real[...] = skewed(even[0:1] - odd[1:2], mid, 2)
     row_imag[...] = skewed(even[1:2] + odd[0:1], mid, 2)
 
-    add_phases(half, length, 0, across, row_real, row_imag, row_near, row_near_adj, row_edge, waves)
+    add_phases(half, length, 0, across, row_real, row_imag, row_near, row_edge, waves)
 
     low = spread(2 * mid, lambda tap: tap)
     high = spread(2 * mid, lambda tap: mid + tap)
     full = jnp.concatenate(
         [skewed(low[0:1] - high[1:2], rows, 1), skewed(low[1:2] + high[0:1], rows, 1)], axis=0
     )
-    row_adj[...] = full.T.astype(BF16)
+    row_fwd[...] = full.astype(BF16)
     low = spread(2 * rows, lambda tap: tap)
     high = spread(2 * rows, lambda tap: rows + tap)
     full = jnp.concatenate(
@@ -195,7 +195,7 @@
         out[...] = jnp.where(frm == 2 * (to % (size // 2)) + to // (size // 2), 1.0, 0.0).astype(BF16)
 
 
-def add_phases(half, length, member, sent, row_real, row_imag, row_near, row_near_adj, row_edge, waves):
+def add_phases(half, length, member, sent, row_real, row_imag, row_near, row_edge, waves):
     mid, wide = row_real.shape[0], row_real.shape[1] // 2
     rows, cols = mid - 2 * half, waves.shape[1] - LANES
     side = lax.axis_index("ang")
@@ -215,7 +215,6 @@
     full = jnp.concatenate([re, im], axis=0)
     at = member * 2 * mid
     row_near[at : at + 2 * mid] = full.astype(BF16)
-    row_near_adj[:, at : at + 2 * mid] = full.T.astype(BF16)
     for part in range(2):
         low, high = 4 * half, 2 * wide - 4 * half
         near = full[part * mid : part * mid + 2 * half, :low]
@@ -225,10 +224,10 @@
 
 
 def phases_kernel(
-    half, length, row_real, row_imag, across, near_in, near_adj_in, edge_in, waves_in,
-    row_near, row_near_adj, row_edge, waves,
+    half, length, row_real, row_imag, across, near_in, edge_in, waves_in,
+    row_near, row_edge, waves,
 ):
-    add_phases(half, length, 1, across, row_real, row_imag, row_near, row_near_adj, row_edge, waves)
+    add_phases(half, length, 1, across, row_real, row_imag, row_near, row_edge, waves)
 
 
 class Tiles:
@@ -516,7 +515,9 @@
     far_margin(tiles, half, Rows(parity * (rows + half), half, mid), far_sum, sums.at[4 * half :])
 
 
-def inner_measured_kernel(measured, measured_got, split_meas, sent, parts):
+def inner_measured_kernel(measured, measured_got, split_meas, row_near, row_fwd, sent, parts, row_near_adj, row_adj):
+    row_near_adj[...] = row_near[...].astype(F32).T.astype(BF16)
+    row_adj[...] = row_fwd[...].astype(F32).T.astype(BF16)
     other = 1 - lax.axis_index("rows") % 2
     windows = (functools.partial(own_window, measured, other), functools.partial(got_window, measured_got))
     for member in range(2):
@@ -677,13 +678,13 @@
     across_got = lax.ppermute(across, "ang", side_pairs)
     corner_got = lax.ppermute(early_got, "rows", outer_pairs)
     phased = [
-        ((4 * mid, 2 * wide), BF16), ((2 * wide, 4 * mid), BF16), ((8 * half, 4 * half), BF16), ((8, width), F32),
+        ((4 * mid, 2 * wide), BF16), ((8 * half, 4 * half), BF16), ((8, width), F32),
     ]
-    row_real, row_imag, row_half, row_half_adj, row_adj, col_taps, split_far, split_meas, *partial = call(
+    row_real, row_imag, row_half, row_half_adj, row_fwd, col_taps, split_far, split_meas, *partial = call(
         functools.partial(matrices_kernel, rows, length),
         [
             ((mid, 2 * wide), F32), ((mid, 2 * wide), F32), ((rows, 2 * rows), BF16), ((2 * rows, rows), BF16),
-            ((2 * mid, 2 * rows), BF16), ((10, 4 * LANES, 2 * LANES), BF16), ((2 * rows, 2 * rows), BF16),
+            ((2 * rows, 2 * mid), BF16), ((10, 4 * LANES, 2 * LANES), BF16), ((2 * rows, 2 * rows), BF16),
             ((rows, rows), BF16), *phased,
         ],
         (kernel_taps, early),
@@ -697,9 +698,9 @@
         functools.partial(inner_edge_kernel, half), [((edge, width), BF16)], (slices, across_got, row_half), outside=(2,),
     )
     inner_got = lax.ppermute(inner, "rows", inner_pairs)
-    row_near, row_near_adj, row_edge, waves = call(
+    row_near, row_edge, waves = call(
         functools.partial(phases_kernel, half, length), phased, (row_real, row_imag, early_got, *partial),
-        aliases={3: 0, 4: 1, 5: 2, 6: 3},
+        aliases={3: 0, 4: 1, 5: 2},
     )
     state = [
         ((2 * mid, width), F32), ((2, 2 * mid, width), BF16), ((2, 2 * mid, width), BF16),
@@ -727,8 +728,10 @@
         flops=BACKWARD_FLOPS,
     )
     outer_back = lax.ppermute(outer_sums, "rows", outer_pairs)
-    (inner_parts,) = call(
-        inner_measured_kernel, [((2, rows, width), F32)], (measured, inner_meas, split_meas, outer_sums), outside=(3,),
+    inner_parts, row_near_adj, row_adj = call(
+        inner_measured_kernel,
+        [((2, rows, width), F32), ((2 * wide, 4 * mid), BF16), ((2 * mid, 2 * rows), BF16)],
+        (measured, inner_meas, split_meas, row_near, row_fwd, outer_sums), outside=(5,),
         flops=MEASURED_FLOPS,
     )
     far_slab, field, after, back, far_sum, into, inner_sums, inner_far = call(

time: 35.4 us -> 35.4 us (level)
  no operation moved by 1% of the time
where the time goes in v9:
time: 35.4 us; the launch traced here: 35.2 us
  starting transfers between devices  15.9 us (45%)
  Pallas kernels  15.8 us (45%)
  waiting for transfers between devices  1.84 us (5%)
  between operations  1.6 us (5%)
    pallas_call x13, Pallas kernels, call(): pl.pallas_call(kernel, out_shape=[jax.ShapeDtypeStruct(shape, dtype) for...  15.8 us
    ppermute x1, starting transfers between devices, columns_local(): outer_got = lax.ppermute(outer, 'rows', outer_pairs)  3.71 us
    ppermute x1, starting transfers between devices, columns_local(): outer_back = lax.ppermute(outer_sums, 'rows', outer_pairs)  3.53 us
    ppermute x1, starting transfers between devices, columns_local(): corner_got = lax.ppermute(early_got, 'rows', outer_pairs)  2.75 us
    ppermute x1, starting transfers between devices, columns_local(): inner_got = lax.ppermute(inner, 'rows', inner_pairs)  1.51 us
    ppermute x1, starting transfers between devices, columns_local(): early_got = lax.ppermute(early, 'ang', side_pairs)  1.28 us
    ppermute x1, starting transfers between devices, columns_local(): outer_meas = lax.ppermute(meas_outer, 'ang', side_pairs)  1.28 us
    ppermute x1, waiting for transfers between devices, columns_local(): outer_back = lax.ppermute(outer_sums, 'rows', outer_pairs)  0.91 us
  transfers between devices with their start and end apart: 10, of which 3 were waited for; matrix products, arithmetic and copies ran while one was open for 0% of the time, Pallas kernels for 39%

profile of v9, /device:TPU:17, one launch (start us, length us, event | category | flops | bytes accessed | tf_op | source)
XLA Modules:
  0.0 35.2 jit_solution(9154663433216685164)
XLA Ops:
  0.6 0.0 copy-start
  0.6 0.0 copy-start.2
  0.6 1.2 %shard_map.68 = (bf16[96,2,1024]{2,1,0:T(2,128)(2,1)S(1)}, bf16[208,128]{1,0:T(8,128)(2,1)S(1)}, bf16[320,128]{1,0:T(8,128)(2,1)S(1)}, f32[2,128]{1,0:T(2,128)S(1)}) custom-call(bf16[2,128,2,1024]{3,2,1,0:T(2,128)(2,1)} %slices.7, f32[2,128]{1,0:T(2,128)} %bitcast.1), custom_call_target="tpu_custom_call" | custom-call | tf_op jit(solution)/shard_map/pallas_call | solution.py:640
  1.8 3.7 %collective-permute-start.4 = (bf16[96,2,1024]{2,1,0:T(2,128)(2,1)S(1)}, bf16[96,2,1024]{2,1,0:T(2,128)(2,1)S(1)}, u32[]{:S(2)}, u32[]{:S(2)}) collective-permute-start(bf16[96,2,1024]{2,1,0:T(2,128)(2,1)S(1)} %get-tuple-element.54), channel_id=1, source_target_pairs={{2,4},{4,2},{6,8},{8,6},{10,12},{12,10},{14,16},{16,14},{18,20},{2... | collective-permute-start | bytes 1179656 | tf_op jit(solution)/shard_map/ppermute | solution.py:676
  6.2 0.0 copy-done
  6.2 0.1 shard_map.69.across
  6.3 0.0 copy-start.1
  6.3 1.3 %collective-permute-start.3 = (bf16[208,128]{1,0:T(8,128)(2,1)S(1)}, bf16[208,128]{1,0:T(8,128)(2,1)S(1)}, u32[]{:S(2)}, u32[]{:S(2)}) collective-permute-start(bf16[208,128]{1,0:T(8,128)(2,1)S(1)} %shard_map.69.across), channel_id=1, source_target_pairs={{0,1},{1,0},{2,3},{3,2},{4,5},{5,4},{6,7},{7,6},{8,9},{9,8},{10,11... | collective-permute-start | bytes 159752 | tf_op jit(solution)/shard_map/ppermute | solution.py:677
  7.6 0.3 collective-permute-start
  7.8 0.0 copy-done.2
  7.8 0.9 %shard_map.70 = (f32[192,512]{1,0:T(8,128)S(1)}, f32[192,512]{1,0:T(8,128)S(1)}, bf16[128,256]{1,0:T(8,128)(2,1)S(1)}, bf16[256,128]{1,0:T(8,128)(2,1)S(1)}, bf1...) custom-call(bf16[2,65]{1,0:T(2,128)(2,1)S(1)} %copy-done.2, ...), custom_call_target="tpu_custom_call" | custom-call | tf_op jit(solution)/shard_map/pallas_call | solution.py:640
  8.8 0.1 shard_map.72
  8.9 1.3 %collective-permute-start.6 = (bf16[128,1152]{1,0:T(8,128)(2,1)S(1)}, bf16[128,1152]{1,0:T(8,128)(2,1)S(1)}, u32[]{:S(2)}, u32[]{:S(2)}) collective-permute-start(bf16[128,1152]{1,0:T(8,128)(2,1)S(1)} %get-tuple-element.61), channel_id=1, source_target_pairs={{0,1},{1,0},{2,3},{3,2},{4,5},{5,4},{6,7},{7,6},{8,9},{9,8},{10,11... | collective-permute-start | bytes 884744 | tf_op jit(solution)/shard_map/ppermute | solution.py:695
  10.2 0.0 collective-permute-done.3.across.early
  10.2 2.7 %collective-permute-start.5 = (bf16[208,128]{1,0:T(8,128)(2,1)S(1)}, bf16[208,128]{1,0:T(8,128)(2,1)S(1)}, u32[]{:S(2)}, u32[]{:S(2)}) collective-permute-start(bf16[208,128]{1,0:T(8,128)(2,1)S(1)} %collective-permute-done.3.across.early), channel_id=1, source_target_pairs={{2,4},{4,2},{6,8},{8,6},{10,12},{12,10},{14,16},{16,14},{18,20},{2... | collective-permute-start | bytes 159752 | tf_op jit(solution)/shard_map/ppermute | solution.py:679
  13.0 0.7 %collective-permute-start.2 = (bf16[128,1152]{1,0:T(8,128)(2,1)S(1)}, bf16[128,1152]{1,0:T(8,128)(2,1)S(1)}, u32[]{:S(2)}, u32[]{:S(2)}) collective-permute-start(bf16[128,1152]{1,0:T(8,128)(2,1)S(1)} %get-tuple-element.45), channel_id=1, source_target_pairs={{0,1},{1,0},{2,3},{3,2},{4,5},{5,4},{6,7},{7,6},{8,9},{9,8},{10,11... | collective-permute-start | bytes 884744 | tf_op jit(solution)/shard_map/ppermute | solution.py:696
  13.7 0.5 %shard_map.73 = (bf16[768,512]{1,0:T(8,128)(2,1)S(1)}, bf16[256,128]{1,0:T(8,128)(2,1)S(1)}, f32[8,1152]{1,0:T(8,128)S(1)}) custom-call(f32[192,512]{1,0:T(8,128)S(1)} %get-tuple-element.47.row_real, f32[192,512]{1,0:T(8,128)S(1)} %get-tuple-element.48.row_imag, ...), custom_call_target="tpu_custom_call", output_to_operand_aliasing={{0}: (3, {}), {1}: (4, {}), {2}: (5, {})} | custom-call | tf_op jit(solution)/shard_map/pallas_call | solution.py:640
  14.2 0.0 collective-permute-done.across
  14.2 0.0 copy-done.1
  14.2 0.1 shard_map.71
  14.3 1.5 %collective-permute-start.1 = (bf16[192,1152]{1,0:T(8,128)(2,1)S(1)}, bf16[192,1152]{1,0:T(8,128)(2,1)S(1)}, u32[]{:S(2)}, u32[]{:S(2)}) collective-permute-start(bf16[192,1152]{1,0:T(8,128)(2,1)S(1)} %shard_map.71), channel_id=1, source_target_pairs={{0,2},{2,0},{4,6},{6,4},{8,10},{10,8},{12,14},{14,12},{16,18},{18,... | collective-permute-start | bytes 1327112 | tf_op jit(solution)/shard_map/ppermute | solution.py:700
  15.8 0.3 collective-permute-done.5.corner
  16.1 0.0 collective-permute-done.4.outer
  16.1 2.6 %shard_map.74 = (f32[384,1152]{1,0:T(8,128)S(1)}, bf16[2,384,1152]{2,1,0:T(8,128)(2,1)S(1)}, bf16[2,384,1152]{2,1,0:T(8,128)(2,1)S(1)}, bf16[2,128,1152]{2,1,0:T(8,128)(2,1)S(1)}) custom-call(bf16[2,128,2,1024]{3,2,1,0:T(2,128)(2,1)S(1)} %copy-done.1, bf16[96,2,1024]{2,1,0:T(2,128)(2,1)S(1)} %collective-permute-done.4.outer, ...), custom_call_target="tpu_custom_call" | custom-call | flops 2400000000 | tf_op jit(solution)/shard_map/pallas_call | solution.py:640
  18.7 0.0 collective-permute-done.6.measured_got
  18.7 2.0 %shard_map.75 = (bf16[2,256,1152]{2,1,0:T(8,128)(2,1)S(1)}, f32[384,1280]{1,0:T(8,128)S(1)}, bf16[768,1024]{1,0:T(8,128)(2,1)S(1)}, bf16[192,1024]{1,0:T(8,128)(2,1)S(1)}) custom-call(f32[384,1152]{1,0:T(8,128)S(1)} %get-tuple-element.58.far_slab.far_slab_in, bf16[2,384,1152]{2,1,0:T(8,128)(2,1)S(1)} %get-tuple-element.59.field.field_in, ...), custom_call_target="tpu_custom_call" | custom-call | flops 1000000000 | tf_op jit(solution)/shard_map/pallas_call | solution.py:640
  20.7 3.5 %collective-permute-start.9 = (bf16[192,1024]{1,0:T(8,128)(2,1)S(1)}, bf16[192,1024]{1,0:T(8,128)(2,1)S(1)}, u32[]{:S(2)}, u32[]{:S(2)}) collective-permute-start(bf16[192,1024]{1,0:T(8,128)(2,1)S(1)} %get-tuple-element.64.sent), channel_id=1, source_target_pairs={{2,4},{4,2},{6,8},{8,6},{10,12},{12,10},{14,16},{16,14},{18,20},{2... | collective-permute-start | bytes 1179656 | tf_op jit(solution)/shard_map/ppermute | solution.py:730
  24.3 0.0 collective-permute-done.2.measured_got
  24.3 0.5 %shard_map.76 = (f32[2,128,1152]{2,1,0:T(8,128)S(1)}, bf16[512,768]{1,0:T(8,128)(2,1)S(1)}, bf16[384,256]{1,0:T(8,128)(2,1)S(1)}) custom-call(bf16[1,128,2,2048]{3,2,1,0:T(2,128)(2,1)S(1)} %copy-done, bf16[128,1152]{1,0:T(8,128)(2,1)S(1)} %collective-permute-done.2.measured_got, bf16[128,128]{1,0:T(8,128)(2,1)S(1)} %get-tuple-element.46.split_meas, ...), custom_call_target="tpu_custom_call" | custom-call | flops 4000000000 | tf_op jit(solution)/shard_map/pallas_call | solution.py:640
  24.8 0.0 collective-permute-done.1.inner
  24.8 4.9 %shard_map.77 = (f32[384,1152]{1,0:T(8,128)S(1)}, bf16[2,384,1152]{2,1,0:T(8,128)(2,1)S(1)}, bf16[2,384,1152]{2,1,0:T(8,128)(2,1)S(1)}, bf16[2,256,1152]{2,1,0:T...) custom-call(bf16[2,128,2,1024]{3,2,1,0:T(2,128)(2,1)S(1)} %copy-done, ...), custom_call_target="tpu_custom_call", output_to_operand_aliasing={{0}: (4, {}), {1}: (5, {}), {2}: (6, {}), {3}: (7, {}), {4}... | custom-call | tf_op jit(solution)/shard_map/pallas_call | solution.py:640
  29.7 0.8 %collective-permute-start.7 = (bf16[128,1024]{1,0:T(8,128)(2,1)S(1)}, bf16[128,1024]{1,0:T(8,128)(2,1)S(1)}, u32[]{:S(2)}, u32[]{:S(2)}) collective-permute-start(bf16[128,1024]{1,0:T(8,128)(2,1)S(1)} %get-tuple-element.76), channel_id=1, source_target_pairs={{0,2},{2,0},{4,6},{6,4},{8,10},{10,8},{12,14},{14,12},{16,18},{18,... | collective-permute-start | bytes 786440 | tf_op jit(solution)/shard_map/ppermute | solution.py:752
  30.6 0.1 collective-permute-start.8
  30.6 0.7 %shard_map.78 = (f32[256,1024]{1,0:T(8,128)S(1)}, f32[2,128,1024]{2,1,0:T(8,128)S(1)}) custom-call(bf16[768,1024]{1,0:T(8,128)(2,1)S(1)} %get-tuple-element.72.into, f32[384,1280]{1,0:T(8,128)S(1)} %get-tuple-element.73.far_sum, bf16[512,768]{1,0:T(8,128)(2,1)S(1)} %get-tuple-element.71.row_near_adj), custom_call_target="tpu_custom_call" | custom-call | tf_op jit(solution)/shard_map/pallas_call | solution.py:640
  31.3 0.6 %collective-permute-done.8.inner_far = bf16[64,1024]{1,0:T(8,128)(2,1)S(1)} collective-permute-done((bf16[64,1024]{1,0:T(8,128)(2,1)S(1)}, bf16[64,1024]{1,0:T(8,128)(2,1)S(1)}, u32[]{:S(2)}, u32[]{:S(2)}) %collective-permute-start.8) | collective-permute-done | bytes 131104 | tf_op jit(solution)/shard_map/ppermute | solution.py:753
  31.9 0.0 collective-permute-done.7.inner
  31.9 1.2 %shard_map.79 = (f32[128,2,1024]{2,1,0:T(2,128)}, f32[128,2,1024]{2,1,0:T(2,128)}) custom-call(f32[256,1024]{1,0:T(8,128)S(1)} %get-tuple-element.74.near_sum, f32[2,128,1024]{2,1,0:T(8,128)S(1)} %get-tuple-element.75.far_sum, bf16[128,1024]{1,0:T(8,128)(2,1)S(1)} %collective-permute-done.7.inner, bf16[64,1024]{1,0:T(8,128)(2,1)S(1)} %collective-permute-done.8.inner_far), custom_call_target="tpu_custom_call" | custom-call | tf_op jit(solution)/shard_map/pallas_call | solution.py:640
  33.1 0.9 %collective-permute-done.9.outer = bf16[192,1024]{1,0:T(8,128)(2,1)S(1)} collective-permute-done((bf16[192,1024]{1,0:T(8,128)(2,1)S(1)}, bf16[192,1024]{1,0:T(8,128)(2,1)S(1)}, u32[]{:S(2)}, u32[]{:S(2)}) %collective-permute-start.9) | collective-permute-done | bytes 393248 | tf_op jit(solution)/shard_map/ppermute | solution.py:730
  34.0 1.0 %shard_map.80 = (f32[128,2,1024]{2,1,0:T(2,128)}, f32[128,2,1024]{2,1,0:T(2,128)}) custom-call(f32[128,2,1024]{2,1,0:T(2,128)} %get-tuple-element.78.near_in, f32[128,2,1024]{2,1,0:T(2,128)} %get-tuple-element.79.far_in, f32[256,1024]{1,0:T(8,128)S(1)} %get-tuple-element.74.near_sum, ...), custom_call_target="tpu_custom_call", output_to_operand_aliasing={{0}: (0, {}), {1}: (1, {})} | custom-call | tf_op jit(solution)/shard_map/pallas_call | solution.py:640
Async XLA Ops:
  0.6 5.6 %copy-start = (bf16[1,128,2,2048]{3,2,1,0:T(2,128)(2,1)S(1)}, bf16[1,128,2,2048]{3,2,1,0:T(2,128)(2,1)}, u32[]{:S(2)}) copy-start(bf16[1,128,2,2048]{3,2,1,0:T(2,128)(2,1)} %measured.7) | copy-start | bytes 3145732
  0.6 7.2 %copy-start.2 = (bf16[2,65]{1,0:T(2,128)(2,1)S(1)}, bf16[2,65]{1,0:T(2,128)(2,1)}, u32[]{:S(2)}) copy-start(bf16[2,65]{1,0:T(2,128)(2,1)} %taps.1) | copy-start | bytes 784
  1.8 14.2 %collective-permute-start.4 = (bf16[96,2,1024]{2,1,0:T(2,128)(2,1)S(1)}, bf16[96,2,1024]{2,1,0:T(2,128)(2,1)S(1)}, u32[]{:S(2)}, u32[]{:S(2)}) collective-permute-start(bf16[96,2,1024]{2,1,0:T(2,128)(2,1)S(1)} %get-tuple-element.54), channel_id=1, source_target_pairs={{2,4},{4,2},{6,8},{8,6},{10,12},{12,10},{14,16},{16,14},{18,20},{2... | collective-permute-start | bytes 1179656 | tf_op jit(solution)/shard_map/ppermute | solution.py:676
  6.3 7.9 %copy-start.1 = (bf16[2,128,2,1024]{3,2,1,0:T(2,128)(2,1)S(1)}, bf16[2,128,2,1024]{3,2,1,0:T(2,128)(2,1)}, u32[]{:S(2)}) copy-start(bf16[2,128,2,1024]{3,2,1,0:T(2,128)(2,1)} %slices.7) | copy-start | bytes 3145732
  6.3 3.9 %collective-permute-start.3 = (bf16[208,128]{1,0:T(8,128)(2,1)S(1)}, bf16[208,128]{1,0:T(8,128)(2,1)S(1)}, u32[]{:S(2)}, u32[]{:S(2)}) collective-permute-start(bf16[208,128]{1,0:T(8,128)(2,1)S(1)} %shard_map.69.across), channel_id=1, source_target_pairs={{0,1},{1,0},{2,3},{3,2},{4,5},{5,4},{6,7},{7,6},{8,9},{9,8},{10,11... | collective-permute-start | bytes 159752 | tf_op jit(solution)/shard_map/ppermute | solution.py:677
  7.6 6.6 %collective-permute-start = (bf16[320,128]{1,0:T(8,128)(2,1)S(1)}, bf16[320,128]{1,0:T(8,128)(2,1)S(1)}, u32[]{:S(2)}, u32[]{:S(2)}) collective-permute-start(bf16[320,128]{1,0:T(8,128)(2,1)S(1)} %get-tuple-element.41.sent), channel_id=1, source_target_pairs={{0,1},{1,0},{2,3},{3,2},{4,5},{5,4},{6,7},{7,6},{8,9},{9,8},{10,11... | collective-permute-start | bytes 245768 | tf_op jit(solution)/shard_map/ppermute | solution.py:678
  8.9 9.7 %collective-permute-start.6 = (bf16[128,1152]{1,0:T(8,128)(2,1)S(1)}, bf16[128,1152]{1,0:T(8,128)(2,1)S(1)}, u32[]{:S(2)}, u32[]{:S(2)}) collective-permute-start(bf16[128,1152]{1,0:T(8,128)(2,1)S(1)} %get-tuple-element.61), channel_id=1, source_target_pairs={{0,1},{1,0},{2,3},{3,2},{4,5},{5,4},{6,7},{7,6},{8,9},{9,8},{10,11... | collective-permute-start | bytes 884744 | tf_op jit(solution)/shard_map/ppermute | solution.py:695
  10.2 5.9 %collective-permute-start.5 = (bf16[208,128]{1,0:T(8,128)(2,1)S(1)}, bf16[208,128]{1,0:T(8,128)(2,1)S(1)}, u32[]{:S(2)}, u32[]{:S(2)}) collective-permute-start(bf16[208,128]{1,0:T(8,128)(2,1)S(1)} %collective-permute-done.3.across.early), channel_id=1, source_target_pairs={{2,4},{4,2},{6,8},{8,6},{10,12},{12,10},{14,16},{16,14},{18,20},{2... | collective-permute-start | bytes 159752 | tf_op jit(solution)/shard_map/ppermute | solution.py:679
  13.0 11.3 %collective-permute-start.2 = (bf16[128,1152]{1,0:T(8,128)(2,1)S(1)}, bf16[128,1152]{1,0:T(8,128)(2,1)S(1)}, u32[]{:S(2)}, u32[]{:S(2)}) collective-permute-start(bf16[128,1152]{1,0:T(8,128)(2,1)S(1)} %get-tuple-element.45), channel_id=1, source_target_pairs={{0,1},{1,0},{2,3},{3,2},{4,5},{5,4},{6,7},{7,6},{8,9},{9,8},{10,11... | collective-permute-start | bytes 884744 | tf_op jit(solution)/shard_map/ppermute | solution.py:696
  14.3 10.5 %collective-permute-start.1 = (bf16[192,1152]{1,0:T(8,128)(2,1)S(1)}, bf16[192,1152]{1,0:T(8,128)(2,1)S(1)}, u32[]{:S(2)}, u32[]{:S(2)}) collective-permute-start(bf16[192,1152]{1,0:T(8,128)(2,1)S(1)} %shard_map.71), channel_id=1, source_target_pairs={{0,2},{2,0},{4,6},{6,4},{8,10},{10,8},{12,14},{14,12},{16,18},{18,... | collective-permute-start | bytes 1327112 | tf_op jit(solution)/shard_map/ppermute | solution.py:700
  20.7 13.3 %collective-permute-start.9 = (bf16[192,1024]{1,0:T(8,128)(2,1)S(1)}, bf16[192,1024]{1,0:T(8,128)(2,1)S(1)}, u32[]{:S(2)}, u32[]{:S(2)}) collective-permute-start(bf16[192,1024]{1,0:T(8,128)(2,1)S(1)} %get-tuple-element.64.sent), channel_id=1, source_target_pairs={{2,4},{4,2},{6,8},{8,6},{10,12},{12,10},{14,16},{16,14},{18,20},{2... | collective-permute-start | bytes 1179656 | tf_op jit(solution)/shard_map/ppermute | solution.py:730
  29.7 2.2 %collective-permute-start.7 = (bf16[128,1024]{1,0:T(8,128)(2,1)S(1)}, bf16[128,1024]{1,0:T(8,128)(2,1)S(1)}, u32[]{:S(2)}, u32[]{:S(2)}) collective-permute-start(bf16[128,1024]{1,0:T(8,128)(2,1)S(1)} %get-tuple-element.76), channel_id=1, source_target_pairs={{0,2},{2,0},{4,6},{6,4},{8,10},{10,8},{12,14},{14,12},{16,18},{18,... | collective-permute-start | bytes 786440 | tf_op jit(solution)/shard_map/ppermute | solution.py:752
  30.6 1.3 %collective-permute-start.8 = (bf16[64,1024]{1,0:T(8,128)(2,1)S(1)}, bf16[64,1024]{1,0:T(8,128)(2,1)S(1)}, u32[]{:S(2)}, u32[]{:S(2)}) collective-permute-start(bf16[64,1024]{1,0:T(8,128)(2,1)S(1)} %get-tuple-element.77), channel_id=1, source_target_pairs={{0,2},{2,0},{4,6},{6,4},{8,10},{10,8},{12,14},{14,12},{16,18},{18,... | collective-permute-start | bytes 393224 | tf_op jit(solution)/shard_map/ppermute | solution.py:753
